TPU v7x, 256 devices: a whole 4x4x8 slice. The times are simulated.
256 devices in a mesh: gx: 16 (over z_hi, x), gz: 8 (over y, core), ga: 2 (over z_lo).
Axes of the slice: x: 4, y: 4, z: 8 (z_hi: 4, z_lo: 2; z = z_hi * 2 + z_lo), core: 2. Of those that a mesh axis runs over, the one named last changes fastest.
Arguments:
- fields: float32 [5, 512, 32, 2048], P(None, 'gx', 'ga', 'gz'), may hold values from -6 to 6
- diffusivity: float32 [5], replicated, may hold values from 0.05 to 0.5
- subsample_offsets: int32 [3], replicated, may hold values from 0 to 3
- column_id: int32 [1], replicated, may hold values from 0 to 15
- pod_basis: float32 [64, 3, 128, 8, 512], P(None, None, ('gx', 'gz'), 'ga'), may hold values from -12 to 12
- held_block: float32 [16, 3, 128, 8, 512], P(None, None, ('gx', 'gz'), 'ga'), may hold values from -24 to 24
Outputs:
- fields_out: float32 [5, 512, 32, 2048], P(None, 'gx', 'ga', 'gz')
- coefficients: float32 [64, 16], replicated
- r_factor: float32 [16, 16], replicated
- new_columns: float32 [16, 3, 128, 8, 512], P(None, None, ('gx', 'gz'), 'ga')
All inputs are finite; a program needn't handle non-finite values.
Results may differ from a plain program's by a relative error of at most 0.000087.
Values sent between devices are 32-bit elements; how exact they have to be, the bound alone decides.
No kernel may reach another device: no remote copies, remote signals or barrier semaphores. Data moves between devices by JAX's collectives and lax.ppermute only.
A program may use at most 192 MiB of HBM per device.

v0:
```python
import jax
import jax.numpy as jnp
from jax import lax
from jax.sharding import PartitionSpec as P

STRIDE = 4


time_step = 0.1
smagorinsky = 0.02


def extended_2(block, sides, width):
    for axis, dim in sides:
        count = lax.axis_size(axis)
        forward = [(i, i + 1) for i in range(count - 1)]
        forward.append((count - 1, 0))
        backward = [(target, source) for source, target in forward]
        low = lax.ppermute(
            lax.slice_in_dim(block, block.shape[dim] - width, None, axis=dim), axis, forward
        )
        high = lax.ppermute(lax.slice_in_dim(block, 0, width, axis=dim), axis, backward)
        block = jnp.concatenate([low, block, high], axis=dim)
    return block


def tendency(padded, diffusivity):
    centre = padded[:, 1:-1, 1:-1, 1:-1]
    x_plus = padded[:, 2:, 1:-1, 1:-1]
    x_minus = padded[:, :-2, 1:-1, 1:-1]
    y_plus = padded[:, 1:-1, 2:, 1:-1]
    y_minus = padded[:, 1:-1, :-2, 1:-1]
    z_plus = padded[:, 1:-1, 1:-1, 2:]
    z_minus = padded[:, 1:-1, 1:-1, :-2]
    slope_x = 0.5 * (x_plus - x_minus)
    slope_y = 0.5 * (y_plus - y_minus)
    slope_z = 0.5 * (z_plus - z_minus)
    strain = jnp.sum(
        slope_x[:3] * slope_x[:3] + slope_y[:3] * slope_y[:3] + slope_z[:3] * slope_z[:3], axis=0
    )
    eddy = smagorinsky * jnp.sqrt(strain)
    advect = centre[0] * slope_x + centre[1] * slope_y + centre[2] * slope_z
    laplace = x_plus + x_minus + y_plus + y_minus + z_plus + z_minus - 6.0 * centre
    return (diffusivity[:, None, None, None] + eddy) * laplace - advect


def with_walls(extended, width):
    extent = extended.shape[2]
    wall_rank = lax.axis_index("ga")
    final_rank = lax.axis_size("ga") - 1
    positions = jnp.arange(extent, dtype=jnp.int32)
    keep = ((positions >= width) | (wall_rank > 0)) & (
        (positions < extent - width) | (wall_rank < final_rank)
    )
    return extended * keep.astype(jnp.float32)[None, None, :, None]


def inner(left, right):
    return jnp.dot(
        left, right.T, precision=lax.Precision.HIGHEST, preferred_element_type=jnp.float32
    )


def on_device(fields, diffusivity, subsample_offsets, column_id, pod_basis, held_block):

    def section_rate(current):
        extended = extended_2(current, (("gx", 1), ("gz", 3), ("ga", 2)), 1)
        return tendency(with_walls(extended, 1), diffusivity)

    first = fields + time_step * section_rate(fields)
    fields_out = 0.5 * (fields + first + time_step * section_rate(first))
    cells_x, cells_y, cells_z = (fields.shape[1], fields.shape[2], fields.shape[3])
    velocity = fields_out[:3].reshape(
        3, cells_x // STRIDE, STRIDE, cells_y // STRIDE, STRIDE, cells_z // STRIDE, STRIDE
    )
    picked = lax.dynamic_index_in_dim(velocity, subsample_offsets[0], 6, keepdims=False)
    picked = lax.dynamic_index_in_dim(picked, subsample_offsets[1], 4, keepdims=False)
    snapshot = lax.dynamic_index_in_dim(picked, subsample_offsets[2], 2, keepdims=False)
    relayed = lax.all_to_all(snapshot, "gz", split_axis=1, concat_axis=3, tiled=True)
    columns_count = held_block.shape[0]
    chosen = (jnp.arange(columns_count, dtype=jnp.int32) == column_id[0]).reshape(
        columns_count, 1, 1, 1, 1
    )
    block = jnp.where(chosen, relayed[None], held_block)
    matrix_b = block.reshape(columns_count, -1)
    matrix_q = pod_basis.reshape(pod_basis.shape[0], -1)
    row_total = matrix_b.shape[1] * lax.axis_size("gx") * lax.axis_size("gz") * lax.axis_size("ga")
    first_coef = lax.psum(inner(matrix_q, matrix_b), ("gx", "gz", "ga")) / row_total
    residual_one = matrix_b - inner(first_coef.T, matrix_q.T)
    second_coef = lax.psum(inner(matrix_q, residual_one), ("gx", "gz", "ga")) / row_total
    residual_two = residual_one - inner(second_coef.T, matrix_q.T)
    coefficients = first_coef + second_coef
    gram = lax.psum(inner(residual_two, residual_two), ("gx", "gz", "ga")) / row_total
    lower = jnp.linalg.cholesky(gram)
    columns = jax.scipy.linalg.solve_triangular(lower, residual_two, lower=True)
    return (fields_out, coefficients, lower.T, columns.reshape(held_block.shape))


def solution(mesh):
    placed = (
        P(None, "gx", "ga", "gz"),
        P(),
        P(),
        P(),
        P(None, None, ("gx", "gz"), "ga", None),
        P(None, None, ("gx", "gz"), "ga", None),
    )
    return jax.shard_map(
        on_device,
        mesh=mesh,
        in_specs=placed,
        out_specs=(P(None, "gx", "ga", "gz"), P(), P(), P(None, None, ("gx", "gz"), "ga", None)),
        check_vma=False,
    )
```

profile of v0, /device:TPU:1, one launch (start us, length us, event | category | flops | bytes accessed | tf_op | source)
XLA Modules:
  0.0 456.6 jit_solution(1686121662985195871)
XLA Ops:
  1.6 2.1 collective-permute-start
  3.7 7.1 %collective-permute-start.1 = (f32[5,1,16,256]{3,2,1,0:T(8,128)S(1)}, f32[5,1,16,256]{3,2,1,0:T(8,128)S(1)}, u32[]{:S(2)}, u32[]{:S(2)}) collective-permute-start(f32[5,1,16,256]{3,2,1,0:T(8,128)S(1)} %get-tuple-element.50), channel_id=1, source_target_pairs={{16,0},{32,16},{48,32},{64,48},{80,64},{96,80},{112,96},{128,112},... | collective-permute-start | bytes 245768 | tf_op jit(solution)/shard_map/ppermute | solution.py:22
  10.8 2.1 collective-permute-done
  17.2 3.0 collective-permute-start.2
  20.9 3.4 copy.111
  24.4 2.2 copy.110
  28.4 2.1 pad_maximum_fusion.8
  32.9 5.6 %collective-permute-done.4 = f32[5,34,1,258]{3,1,2,0:T(8,128)} collective-permute-done((f32[5,34,1,258]{3,1,2,0:T(8,128)}, f32[5,34,1,258]{3,1,2,0:T(8,128)}, u32[]{:S(2)}, u32[]{:S(2)}) %collective-permute-start.4) | collective-permute-done | bytes 175472 | tf_op jit(solution)/shard_map/ppermute | solution.py:19
  38.6 6.6 %collective-permute-done.5 = f32[5,34,1,258]{3,1,2,0:T(8,128)} collective-permute-done((f32[5,34,1,258]{3,1,2,0:T(8,128)}, f32[5,34,1,258]{3,1,2,0:T(8,128)}, u32[]{:S(2)}, u32[]{:S(2)}) %collective-permute-start.5) | collective-permute-done | bytes 175472 | tf_op jit(solution)/shard_map/ppermute | solution.py:22
  45.2 4.7 %maximum_multiply_fusion = f32[5,34,18,258]{3,1,2,0:T(8,128)S(1)} fusion(f32[5,34,1,258]{3,1,2,0:T(8,128)} %collective-permute-done.5, f32[5,34,16,1]{3,1,2,0:T(8,128)} %copy.112, f32[5,34,16,256]{3,1,2,0:T(8,128)} %copy-done.1, f32[5,34,16,1]{3,1,2,0:T(8,128)} %copy.110, f32[5,34,1,258]{3,1,2,0:T(8,128)} %collective-permute-done.4, f32[18]{0:T(128)S(1)} %and_convert_fusion), kind=kLoop, calls=%fused_computation.2 | loop fusion | flops 3947400 | bytes 6315912 | tf_op jit(solution)/shard_map/mul | solution.py:55
  49.9 4.3 slice_subtract_fusion.5
  54.2 2.1 fusion.33
  58.8 8.2 %fusion.10 = f32[5,32,16,256]{3,1,2,0:T(8,128)S(1)} fusion(f32[5,34,18,258]{3,1,2,0:T(8,128)S(1)} %maximum_multiply_fusion, f32[5,32,16,256]{3,1,2,0:T(8,128)} %copy-done.6, f32[5,32,16,256]{3,1,2,0:T(8,128)} %copy-done.7, f32[5,32,16,256]{3,1,2,0:T(8,128)} %copy-done.5, f32[5,32,16,256]{3,2,1,0:T(8,128)} %param.6, f32[32,16,256]{2,0,1:T(8,128)} %get-tuple-element.39, ...), kind=kLoop, calls=%fused_computation.17 | loop fusion | flops 11141120 | bytes 33554452 | tf_op jit(solution)/shard_map/add | solution.py:70
  67.3 5.7 %collective-permute-start.7 = (f32[5,1,16,256]{3,2,1,0:T(8,128)S(1)}, f32[5,1,16,256]{3,2,1,0:T(8,128)S(1)}, u32[]{:S(2)}, u32[]{:S(2)}) collective-permute-start(f32[5,1,16,256]{3,2,1,0:T(8,128)S(1)} %copy.116), channel_id=1, source_target_pairs={{16,0},{32,16},{48,32},{64,48},{80,64},{96,80},{112,96},{128,112},... | collective-permute-start | bytes 245768 | tf_op jit(solution)/shard_map/ppermute | solution.py:22
  73.0 2.7 collective-permute-done.6
  76.3 2.2 fusion.45
  78.5 2.1 copy.119
  80.6 5.0 %collective-permute-start.8 = (f32[5,34,16,1]{1,2,3,0:T(8,128)S(1)}, f32[5,34,16,1]{1,2,3,0:T(8,128)S(1)}, u32[]{:S(2)}, u32[]{:S(2)}) collective-permute-start(f32[5,34,16,1]{1,2,3,0:T(8,128)S(1)} %copy.119), channel_id=1, source_target_pairs={{0,2},{2,4},{4,6},{6,8},{8,10},{10,12},{12,14},{14,0},{1,3},{3,5},... | collective-permute-start | bytes 32648 | tf_op jit(solution)/shard_map/ppermute | solution.py:19
  85.6 2.1 copy.120
  103.9 6.4 %collective-permute-done.11 = f32[5,34,1,258]{3,1,2,0:T(8,128)S(1)} collective-permute-done((f32[5,34,1,258]{3,1,2,0:T(8,128)S(1)}, f32[5,34,1,258]{3,1,2,0:T(8,128)S(1)}, u32[]{:S(2)}, u32[]{:S(2)}) %collective-permute-start.11) | collective-permute-done | bytes 175472 | tf_op jit(solution)/shard_map/ppermute | solution.py:22
  110.3 6.0 %maximum_multiply_fusion.1 = f32[5,34,18,258]{3,1,2,0:T(8,128)S(1)} fusion(f32[5,34,1,258]{3,1,2,0:T(8,128)S(1)} %collective-permute-done.11, f32[5,34,16,1]{3,1,2,0:T(8,128)} %copy.122, f32[5,1,16,256]{3,1,2,0:T(1,128)S(1)} %copy.118, f32[5,32,16,256]{3,1,2,0:T(8,128)} %copy-done, f32[5,1,16,256]{3,1,2,0:T(1,128)S(1)} %copy.117, f32[5,34,16,1]{3,1,2,0:T(8,128)} %copy.121, ...), kind=kLoop, calls=%fused_computation.3 | loop fusion | flops 5526360 | bytes 6315912 | tf_op jit(solution)/shard_map/mul | solution.py:55
  116.4 4.3 slice_subtract_fusion.2
  124.3 9.6 %fusion.5 = f32[5,32,16,256]{3,1,2,0:T(8,128)} fusion(f32[5,34,18,258]{3,1,2,0:T(8,128)S(1)} %maximum_multiply_fusion.1, f32[5,32,16,256]{3,1,2,0:T(8,128)} %copy-done.3, f32[5,32,16,256]{3,1,2,0:T(8,128)} %copy-done.4, f32[5,32,16,256]{3,1,2,0:T(8,128)} %copy-done.2, f32[5,32,16,256]{3,1,2,0:T(8,128)} %copy-done, f32[5,32,16,256]{3,2,1,0:T(8,128)} %param.6, ...), kind=kLoop, calls=%fused_computation.11 | loop fusion | flops 12451840 | bytes 36175892 | tf_op jit(solution)/shard_map/mul | solution.py:71
  136.2 53.3 %reshape.86 = f32[3,8,4,4,4,64,4]{6,5,4,3,2,1,0:T(8,128)} reshape(f32[3,32,16,256]{3,2,1,0:T(8,128)S(1)} %copy.123) | data formatting | bytes 3145728 | tf_op jit(solution)/shard_map/reshape | solution.py:73
  189.5 2.8 constant_dynamic-slice_fusion
  194.3 4.4 all-to-all-start
  198.7 2.4 reshape.90
  201.2 4.8 %copy.133 = f32[5,32,16,256]{3,2,1,0:T(8,128)} copy(f32[5,32,16,256]{3,1,2,0:T(8,128)} %fusion.5) | data formatting | bytes 5242880
  217.3 2.6 fusion.25
  220.0 79.2 %psum.21 = f32[64,16]{0,1:T(8,128)S(1)} all-reduce(f32[64,16]{0,1:T(8,128)S(1)} %fusion.25), channel_id=1, replica_groups=mesh['gx'=16,'gz'=8,'ga'=2] {'gx','gz','ga'}, use_global_device_ids=true, to_apply=%region_2.3 | all-reduce | flops 1024 | bytes 8192 | tf_op jit(solution)/shard_map/psum | solution.py:88
  301.4 72.6 %psum.22 = f32[64,16]{0,1:T(8,128)S(1)} all-reduce(f32[64,16]{0,1:T(8,128)S(1)} %convolution_bitcast_fusion.1), channel_id=1, replica_groups=mesh['gx'=16,'gz'=8,'ga'=2] {'gx','gz','ga'}, use_global_device_ids=true, to_apply=%region_3.4 | all-reduce | flops 1024 | bytes 8192 | tf_op jit(solution)/shard_map/psum | solution.py:90
  376.4 73.6 %psum.23 = f32[16,16]{0,1:T(8,128)S(1)} all-reduce(f32[16,16]{0,1:T(8,128)S(1)} %fusion.50), channel_id=1, replica_groups=mesh['gx'=16,'gz'=8,'ga'=2] {'gx','gz','ga'}, use_global_device_ids=true, to_apply=%region_4.5 | all-reduce | flops 256 | bytes 2048 | tf_op jit(solution)/shard_map/psum | solution.py:93
  (101 shorter events, 53.6 us)
Async XLA Ops:
  1.6 11.3 %collective-permute-start = (f32[5,1,16,256]{3,2,1,0:T(8,128)S(1)}, f32[5,1,16,256]{3,2,1,0:T(8,128)S(1)}, u32[]{:S(2)}, u32[]{:S(2)}) collective-permute-start(f32[5,1,16,256]{3,2,1,0:T(8,128)S(1)} %get-tuple-element.51), channel_id=1, source_target_pairs={{0,16},{16,32},{32,48},{48,64},{64,80},{80,96},{96,112},{112,128},... | collective-permute-start | bytes 245768 | tf_op jit(solution)/shard_map/ppermute | solution.py:19
  3.7 11.2 %collective-permute-start.1 = (f32[5,1,16,256]{3,2,1,0:T(8,128)S(1)}, f32[5,1,16,256]{3,2,1,0:T(8,128)S(1)}, u32[]{:S(2)}, u32[]{:S(2)}) collective-permute-start(f32[5,1,16,256]{3,2,1,0:T(8,128)S(1)} %get-tuple-element.50), channel_id=1, source_target_pairs={{16,0},{32,16},{48,32},{64,48},{80,64},{96,80},{112,96},{128,112},... | collective-permute-start | bytes 245768 | tf_op jit(solution)/shard_map/ppermute | solution.py:22
  14.9 1.6 copy-start.8
  17.2 7.1 %collective-permute-start.2 = (f32[5,34,16,1]{1,2,3,0:T(8,128)S(1)}, f32[5,34,16,1]{1,2,3,0:T(8,128)S(1)}, u32[]{:S(2)}, u32[]{:S(2)}) collective-permute-start(f32[5,34,16,1]{1,2,3,0:T(8,128)S(1)} %copy.140), channel_id=1, source_target_pairs={{0,2},{2,4},{4,6},{6,8},{8,10},{10,12},{12,14},{14,0},{1,3},{3,5},... | collective-permute-start | bytes 32648 | tf_op jit(solution)/shard_map/ppermute | solution.py:19
  20.9 5.6 %collective-permute-start.3 = (f32[5,34,16,1]{1,2,3,0:T(8,128)S(1)}, f32[5,34,16,1]{1,2,3,0:T(8,128)S(1)}, u32[]{:S(2)}, u32[]{:S(2)}) collective-permute-start(f32[5,34,16,1]{1,2,3,0:T(8,128)S(1)} %copy.141), channel_id=1, source_target_pairs={{2,0},{4,2},{6,4},{8,6},{10,8},{12,10},{14,12},{0,14},{3,1},{5,3},... | collective-permute-start | bytes 32648 | tf_op jit(solution)/shard_map/ppermute | solution.py:22
  24.3 14.2 %copy-start.1 = (f32[5,34,16,256]{3,1,2,0:T(8,128)}, f32[5,34,16,256]{3,1,2,0:T(8,128)S(1)}, u32[]{:S(2)}) copy-start(f32[5,34,16,256]{3,1,2,0:T(8,128)S(1)} %copy.111) | copy-start | bytes 8355844
  30.5 8.0 %collective-permute-start.4 = (f32[5,34,1,258]{3,1,2,0:T(8,128)}, f32[5,34,1,258]{3,1,2,0:T(8,128)}, u32[]{:S(2)}, u32[]{:S(2)}) collective-permute-start(f32[5,34,1,258]{3,1,2,0:T(8,128)} %get-tuple-element.28), channel_id=1, source_target_pairs={{0,1},{1,0},{2,3},{3,2},{4,5},{5,4},{6,7},{7,6},{8,9},{9,8},{10,11... | collective-permute-start | bytes 526328 | tf_op jit(solution)/shard_map/ppermute | solution.py:19
  32.4 12.7 %collective-permute-start.5 = (f32[5,34,1,258]{3,1,2,0:T(8,128)}, f32[5,34,1,258]{3,1,2,0:T(8,128)}, u32[]{:S(2)}, u32[]{:S(2)}) collective-permute-start(f32[5,34,1,258]{3,1,2,0:T(8,128)} %get-tuple-element.29), channel_id=1, source_target_pairs={{1,0},{0,1},{3,2},{2,3},{5,4},{4,5},{7,6},{6,7},{9,8},{8,9},{11,10... | collective-permute-start | bytes 526328 | tf_op jit(solution)/shard_map/ppermute | solution.py:22
  32.9 12.2 %copy-start.14 = (f32[18]{0:T(128)}, f32[18]{0:T(128)S(1)}, u32[]{:S(2)}) copy-start(f32[18]{0:T(128)S(1)} %and_convert_fusion) | copy-start | bytes 220
  54.2 2.8 copy-start.5
  54.2 2.8 copy-start.6
  54.2 3.7 copy-start.7
  56.3 2.5 copy-start.12
  67.0 25.9 %copy-start = (f32[5,32,16,256]{3,1,2,0:T(8,128)}, f32[5,32,16,256]{3,1,2,0:T(8,128)S(1)}, u32[]{:S(2)}) copy-start(f32[5,32,16,256]{3,1,2,0:T(8,128)S(1)} %fusion.10) | copy-start | bytes 7864324
  67.2 8.5 %collective-permute-start.6 = (f32[5,1,16,256]{3,2,1,0:T(8,128)S(1)}, f32[5,1,16,256]{3,2,1,0:T(8,128)S(1)}, u32[]{:S(2)}, u32[]{:S(2)}) collective-permute-start(f32[5,1,16,256]{3,2,1,0:T(8,128)S(1)} %copy.115), channel_id=1, source_target_pairs={{0,16},{16,32},{32,48},{48,64},{64,80},{80,96},{96,112},{112,128},... | collective-permute-start | bytes 245768 | tf_op jit(solution)/shard_map/ppermute | solution.py:19
  67.3 8.4 %collective-permute-start.7 = (f32[5,1,16,256]{3,2,1,0:T(8,128)S(1)}, f32[5,1,16,256]{3,2,1,0:T(8,128)S(1)}, u32[]{:S(2)}, u32[]{:S(2)}) collective-permute-start(f32[5,1,16,256]{3,2,1,0:T(8,128)S(1)} %copy.116), channel_id=1, source_target_pairs={{16,0},{32,16},{48,32},{64,48},{80,64},{96,80},{112,96},{128,112},... | collective-permute-start | bytes 245768 | tf_op jit(solution)/shard_map/ppermute | solution.py:22
  80.6 7.0 %collective-permute-start.8 = (f32[5,34,16,1]{1,2,3,0:T(8,128)S(1)}, f32[5,34,16,1]{1,2,3,0:T(8,128)S(1)}, u32[]{:S(2)}, u32[]{:S(2)}) collective-permute-start(f32[5,34,16,1]{1,2,3,0:T(8,128)S(1)} %copy.119), channel_id=1, source_target_pairs={{0,2},{2,4},{4,6},{6,8},{8,10},{10,12},{12,14},{14,0},{1,3},{3,5},... | collective-permute-start | bytes 32648 | tf_op jit(solution)/shard_map/ppermute | solution.py:19
  87.7 3.4 collective-permute-start.9
  93.0 3.2 copy-start.11
  94.4 9.5 %collective-permute-start.10 = (f32[5,34,1,258]{3,1,2,0:T(8,128)S(1)}, f32[5,34,1,258]{3,1,2,0:T(8,128)S(1)}, u32[]{:S(2)}, u32[]{:S(2)}) collective-permute-start(f32[5,34,1,258]{3,1,2,0:T(8,128)S(1)} %get-tuple-element.30), channel_id=1, source_target_pairs={{0,1},{1,0},{2,3},{3,2},{4,5},{5,4},{6,7},{7,6},{8,9},{9,8},{10,11... | collective-permute-start | bytes 526328 | tf_op jit(solution)/shard_map/ppermute | solution.py:19
  95.9 14.5 %collective-permute-start.11 = (f32[5,34,1,258]{3,1,2,0:T(8,128)S(1)}, f32[5,34,1,258]{3,1,2,0:T(8,128)S(1)}, u32[]{:S(2)}, u32[]{:S(2)}) collective-permute-start(f32[5,34,1,258]{3,1,2,0:T(8,128)S(1)} %get-tuple-element.31), channel_id=1, source_target_pairs={{1,0},{0,1},{3,2},{2,3},{5,4},{4,5},{7,6},{6,7},{9,8},{8,9},{11,10... | collective-permute-start | bytes 526328 | tf_op jit(solution)/shard_map/ppermute | solution.py:22
  120.7 2.6 copy-start.2
  120.7 2.6 copy-start.3
  120.7 3.4 copy-start.4
  122.6 1.7 copy-start.13
  133.9 1.4 slice-start
  194.3 11.6 %all-to-all-start = ((f32[8,1,768]{2,1,0:T(1,128)}), f32[8,1,768]{2,1,0:T(1,128)}, u32[]{:S(2)}, u32[]{:S(2)}) async-start(f32[8,1,768]{2,1,0:T(1,128)} %reshape.94), calls=%async_computation | async-start | bytes 49152 | tf_op jit(solution)/shard_map/all_to_all | solution.py:79
  201.1 11.7 %copy-start.10 = (f32[16,3,1,4,512]{4,3,2,1,0:T(4,128)S(1)}, f32[16,3,1,4,512]{4,3,2,1,0:T(4,128)}, u32[]{:S(2)}) copy-start(f32[16,3,1,4,512]{4,3,2,1,0:T(4,128)} %param.11) | copy-start | bytes 1179652
  205.9 11.4 %copy-start.9 = (f32[64,3,1,4,512]{4,3,2,1,0:T(4,128)S(1)}, f32[64,3,1,4,512]{4,3,2,1,0:T(4,128)}, u32[]{:S(2)}) copy-start(f32[64,3,1,4,512]{4,3,2,1,0:T(4,128)} %param.10) | copy-start | bytes 4718596
where the time goes:
time: 463 us; the launch traced here: 457 us
  blocking collectives  225 us (49%)
  local copies, waits for them, and re-layouts  102 us (22%)
  other arithmetic  57.4 us (12%)
  starting transfers between devices  31.4 us (7%)
  waiting for transfers between devices  25.8 us (6%)
  between operations  7.7 us (2%)
  matrix products  6.87 us (1%)
    psum x1, blocking collectives, on_device(): lax.psum(inner(matrix_q, matrix_b), ('gx', 'gz', 'ga')) / row_total  79.2 us
    psum x1, blocking collectives, on_device(): lax.psum(inner(residual_two, residual_two), ('gx', 'gz', 'ga')) / row_total  73.6 us
    psum x1, blocking collectives, on_device(): lax.psum(inner(matrix_q, residual_one), ('gx', 'gz', 'ga')) / row_total  72.6 us
    reshape x1, local copies, waits for them, and re-layouts, on_device(): fields_out[:3]  53.3 us
    unnamed x39, local copies, waits for them, and re-layouts  15 us
    ppermute x6, waiting for transfers between devices, extended_2(): lax.ppermute(lax.slice_in_dim(block, 0, width, axis=dim), axis, backward)  14.5 us
    ppermute x6, starting transfers between devices, extended_2(): lax.ppermute(lax.slice_in_dim(block, block.shape[dim] - width, None, axis...  13.5 us
    ppermute x6, starting transfers between devices, extended_2(): lax.ppermute(lax.slice_in_dim(block, 0, width, axis=dim), axis, backward)  13.5 us
  transfers between devices with their start and end apart: 13, of which 7 were waited for; matrix products, arithmetic and copies ran while one was open for 4% of the time, Pallas kernels for 0%

commit v1 on v0

v1 whole, which is shorter than its diff:
```python
import jax
import jax.numpy as jnp
from jax import lax
from jax.experimental import pallas as pl
from jax.experimental.pallas import tpu as pltpu
from jax.sharding import PartitionSpec as P

STRIDE = 4
LANES = 128

time_step = 0.1
smagorinsky = 0.02

VMEM = pl.BlockSpec(memory_space=pltpu.VMEM)
SMEM = pl.BlockSpec(memory_space=pltpu.SMEM)
HIGH = lax.Precision.HIGHEST
AXES = ("gx", "gz", "ga")


def params(mib):
    return pltpu.CompilerParams(vmem_limit_bytes=mib * 1024 * 1024)


def struct(*shape):
    return jax.ShapeDtypeStruct(shape, jnp.float32)


def iota(shape, dim):
    return lax.broadcasted_iota(jnp.int32, shape, dim)


def dot(left, right, left_dim, right_dim):
    return lax.dot_general(
        left,
        right,
        (((left_dim,), (right_dim,)), ((), ())),
        precision=HIGH,
        preferred_element_type=jnp.float32,
    )


def put_row(x, upper, top, bottom, ref, field, half):
    row = jnp.where(upper, bottom[0:1, :], top[7:8, :])
    rows = pl.ds(pl.multiple_of(x // 8 * 8, 8), 8)
    lanes = slice(half * LANES, (half + 1) * LANES)
    here = iota((8, LANES), 0) == x % 8
    ref[field, rows, lanes] = jnp.where(here, row, ref[field, rows, lanes])


def put_columns(x, lane, value, ref, field, tile, from_end):
    shift = (x + 1) % LANES if from_end else x
    rows = slice(tile * 8, tile * 8 + 8)
    ref[field, rows, :] = jnp.where(lane == x, pltpu.roll(value, shift, 1), ref[field, rows, :])


def pack_kernel(fields, x_low, x_high, y_row, z_low, z_high):
    count, cells, height, _ = fields.shape
    upper = lax.axis_index("ga") > 0
    lane = iota((8, LANES), 1)
    y_row[...] = jnp.zeros_like(y_row)
    x_low[...] = fields[:, 0]
    x_high[...] = fields[:, cells - 1]
    z_low[...] = jnp.zeros_like(z_low)
    z_high[...] = jnp.zeros_like(z_high)

    def body(x, carry):
        for f in range(count):
            for half in range(2):
                lanes = slice(half * LANES, (half + 1) * LANES)
                bottom = fields[f, x, 0:8, lanes]
                top = fields[f, x, height - 8 : height, lanes]
                put_row(x, upper, top, bottom, y_row, f, half)
                for tile, value in ((0, bottom), (1, top)):
                    put_columns(
                        x, lane, value, (z_low, z_high)[half], f, tile, half == 1
                    )
        return carry

    lax.fori_loop(0, cells, body, 0)


def stage_plane(x, current, before, after, y_halo, z_before, z_after, diffusivity, upper):
    count = current.shape[0]
    lane = iota((8, LANES), 1)
    sub = iota((8, LANES), 0)
    first_lane, last_lane = lane == 0, lane == LANES - 1
    first_sub, last_sub = sub == 0, sub == 7
    below = jnp.where(upper, 1.0, 0.0)
    above = 1.0 - below
    row_shift = (jnp.where(upper, 8, 15) - x % 8) % 8
    centre, slope_x, slope_y, slope_z, laplace = {}, {}, {}, {}, {}
    for f in range(count):
        for tile in range(2):
            for half in range(2):
                centre[f, tile, half] = current[
                    f, x, tile * 8 : tile * 8 + 8, half * LANES : (half + 1) * LANES
                ]
        for half in range(2):
            lanes = slice(half * LANES, (half + 1) * LANES)
            row = y_halo[f, pl.ds(pl.multiple_of(x // 8 * 8, 8), 8), lanes]
            row = pltpu.roll(row, row_shift, 0)
            row_low, row_high = row * below, row * above
            down = [pltpu.roll(centre[f, tile, half], 1, 0) for tile in range(2)]
            up = [pltpu.roll(centre[f, tile, half], 7, 0) for tile in range(2)]
            y_minus = (
                jnp.where(first_sub, row_low, down[0]),
                jnp.where(first_sub, down[0], down[1]),
            )
            y_plus = (
                jnp.where(last_sub, up[1], up[0]),
                jnp.where(last_sub, row_high, up[1]),
            )
            for tile in range(2):
                slope_y[f, tile, half] = y_plus[tile] - y_minus[tile]
                laplace[f, tile, half] = y_plus[tile] + y_minus[tile]
        for tile in range(2):
            rows = slice(tile * 8, tile * 8 + 8)
            from_low = pltpu.roll(z_before[f, rows, :], (LANES - x) % LANES, 1)
            from_high = pltpu.roll(z_after[f, rows, :], LANES - 1 - x, 1)
            right = [pltpu.roll(centre[f, tile, half], 1, 1) for half in range(2)]
            left = [pltpu.roll(centre[f, tile, half], LANES - 1, 1) for half in range(2)]
            z_minus = (
                jnp.where(first_lane, from_low, right[0]),
                jnp.where(first_lane, right[0], right[1]),
            )
            z_plus = (
                jnp.where(last_lane, left[1], left[0]),
                jnp.where(last_lane, from_high, left[1]),
            )
            for half in range(2):
                lanes = slice(half * LANES, (half + 1) * LANES)
                slope_z[f, tile, half] = z_plus[half] - z_minus[half]
                x_minus, x_plus = before(f, rows, lanes), after(f, rows, lanes)
                slope_x[f, tile, half] = x_plus - x_minus
                laplace[f, tile, half] = (
                    laplace[f, tile, half]
                    + (z_plus[half] + z_minus[half])
                    + (x_plus + x_minus)
                    - 6.0 * centre[f, tile, half]
                )
    rates = {}
    for tile in range(2):
        for half in range(2):
            at = (tile, half)
            strain = 0.0
            for f in range(3):
                strain = strain + (
                    slope_x[f, *at] * slope_x[f, *at]
                    + slope_y[f, *at] * slope_y[f, *at]
                    + slope_z[f, *at] * slope_z[f, *at]
                )
            eddy = smagorinsky * jnp.sqrt(0.25 * strain)
            speeds = [0.5 * centre[f, *at] for f in range(3)]
            for f in range(count):
                advect = (
                    speeds[0] * slope_x[f, *at]
                    + speeds[1] * slope_y[f, *at]
                    + speeds[2] * slope_z[f, *at]
                )
                rates[f, *at] = (diffusivity[f] + eddy) * laplace[f, *at] - advect
    return centre, rates


def planes(current, halos, diffusivity, finish):
    x_before, x_after, y_halo, z_before, z_after = halos
    cells = current.shape[1]
    upper = lax.axis_index("ga") > 0

    def one(x, before, after):
        centre, rates = stage_plane(
            x, current, before, after, y_halo, z_before, z_after, diffusivity, upper
        )
        finish(x, centre, rates)

    def inside(offset, x):
        return lambda f, rows, lanes: current[f, x + offset, rows, lanes]

    def outside(ref):
        return lambda f, rows, lanes: ref[f, rows, lanes]

    one(0, outside(x_before), inside(1, 0))

    def body(x, carry):
        one(x, inside(-1, x), inside(1, x))
        return carry

    lax.fori_loop(1, cells - 1, body, 0)
    one(cells - 1, inside(-1, cells - 1), outside(x_after))


def first_kernel(
    diffusivity, current, x_before, x_after, y_halo, z_before, z_after,
    first, x_low, x_high, y_row, z_low, z_high,
):
    count, cells = current.shape[:2]
    upper = lax.axis_index("ga") > 0
    lane = iota((8, LANES), 1)
    y_row[...] = jnp.zeros_like(y_row)
    z_low[...] = jnp.zeros_like(z_low)
    z_high[...] = jnp.zeros_like(z_high)

    def finish(x, centre, rates):
        for f in range(count):
            new = {}
            for tile in range(2):
                for half in range(2):
                    rows = slice(tile * 8, tile * 8 + 8)
                    lanes = slice(half * LANES, (half + 1) * LANES)
                    value = centre[f, tile, half] + time_step * rates[f, tile, half]
                    new[tile, half] = value
                    first[f, x, rows, lanes] = value
                    if isinstance(x, int):
                        (x_low if x == 0 else x_high)[f, rows, lanes] = value
            for half in range(2):
                put_row(x, upper, new[1, half], new[0, half], y_row, f, half)
            for tile in range(2):
                put_columns(x, lane, new[tile, 0], z_low, f, tile, False)
                put_columns(x, lane, new[tile, 1], z_high, f, tile, True)

    planes(current, (x_before, x_after, y_halo, z_before, z_after), diffusivity, finish)


def second_kernel(
    diffusivity, offsets, start, current, x_before, x_after, y_halo, z_before, z_after,
    result, snapshot, picked,
):
    count, cells, height, width = current.shape

    def finish(x, centre, rates):
        for f in range(count):
            for tile in range(2):
                for half in range(2):
                    rows = slice(tile * 8, tile * 8 + 8)
                    lanes = slice(half * LANES, (half + 1) * LANES)
                    result[f, x, rows, lanes] = 0.5 * (
                        start[f, x, rows, lanes]
                        + centre[f, tile, half]
                        + time_step * rates[f, tile, half]
                    )

    planes(current, (x_before, x_after, y_halo, z_before, z_after), diffusivity, finish)
    levels = height // STRIDE
    picked[...] = jnp.zeros_like(picked)
    for column in range(cells // STRIDE):
        for f in range(3):
            for tile in range(2):
                plane = result[f, column * STRIDE + offsets[2], tile * 8 : tile * 8 + 8, :]
                plane = pltpu.roll(plane, (8 - offsets[1]) % 8, 0)
                for part in range(2):
                    row = column * 16 + f * levels + tile * 2 + part
                    picked[row : row + 1, :] = plane[part * STRIDE : part * STRIDE + 1, :]
    points = width // STRIDE
    choose = iota((width, LANES), 0) == STRIDE * (iota((width, LANES), 1) % points) + offsets[0]
    snapshot[...] = dot(picked[...], choose.astype(jnp.float32), 1, 0)


def gram_kernel(basis, held, joined, message):
    rank, _, _, levels, points = basis.shape
    columns = held.shape[0]
    total = rank + columns
    for c in range(3):
        for level in range(levels):
            lanes = slice((c * levels + level) * points, (c * levels + level + 1) * points)
            joined[0:rank, lanes] = basis[:, c, 0, level, :]
            joined[rank:total, lanes] = held[:, c, 0, level, :]

    def body(step, gram):
        part = joined[:, pl.ds(pl.multiple_of(step * points, LANES), points)]
        return gram + dot(part, part, 1, 1)

    gram = lax.fori_loop(0, 3 * levels, body, jnp.zeros((total, total), jnp.float32))
    gram = jnp.concatenate([gram, jnp.zeros((total, LANES - total), jnp.float32)], axis=1)
    for piece in range(3):
        message[piece * total : (piece + 1) * total, :] = pltpu.roll(
            gram, (LANES - 27 * piece) % LANES, 1
        )
    message[3 * total :, :] = jnp.zeros((message.shape[0] - 3 * total, LANES), jnp.float32)


def product_kernel(relayed, joined, pieces, message, column, partial):
    total = joined.shape[0]
    groups = total // 8
    lane = iota((8, LANES), 1)
    low = iota((1, LANES), 1) < LANES // 2
    sums = [jnp.zeros((8, LANES), jnp.float32) for _ in range(groups + 1)]
    for row in range(12):
        for pair in range(4):
            tile = row * 4 + pair
            lanes = slice(tile * LANES, (tile + 1) * LANES)
            values = jnp.where(
                low,
                relayed[2 * pair, row : row + 1, :],
                relayed[2 * pair + 1, row : row + 1, :],
            )
            values = jnp.broadcast_to(values, (8, LANES))
            column[:, lanes] = values
            for group in range(groups):
                sums[group] += joined[group * 8 : group * 8 + 8, lanes] * values
            sums[groups] += values * values
    partial[...] = jnp.zeros_like(partial)
    for group in range(groups + 1):
        partial[group * 8 : group * 8 + 8, :] = sums[group]
    products = dot(jnp.ones((8, LANES), jnp.float32), partial[...], 1, 1)
    own = jnp.sum(pieces[...].reshape(-1, 8, LANES), axis=0)
    own = jnp.broadcast_to(jnp.sum(own, axis=0, keepdims=True), (8, LANES))
    values = jnp.where(lane < 96, products, pltpu.roll(own, 96, 1))
    count = message.shape[0]
    message[...] = jnp.broadcast_to(values[None], (count // 8, 8, LANES)).reshape(count, LANES)


def final_kernel(column_id, gathered, joined, column, coefficients, r_factor, columns_out):
    total = joined.shape[0]
    rank, count = coefficients.shape
    _, _, _, levels, points = columns_out.shape
    rows_total = float(gathered.shape[0] * joined.shape[1])
    chosen = column_id[0]
    received = gathered[...]
    sums = jnp.sum(received.reshape(-1, 8, LANES), axis=0)
    sums = jnp.sum(sums, axis=0, keepdims=True) / rows_total
    lane = iota((total, LANES), 1)
    pieces = [
        pltpu.roll(received[piece * total : (piece + 1) * total, :], (27 * piece + 32) % LANES, 1)
        for piece in range(3)
    ]
    gram = jnp.where(lane < 27, pieces[0], jnp.where(lane < 54, pieces[1], pieces[2])) / rows_total
    down = jnp.broadcast_to(sums, (LANES, LANES)).T
    modes = gram[:rank, :rank]
    shifted = pltpu.roll(gram, LANES - rank, 1)
    first = jnp.where(lane[:rank] == chosen, down[:rank], shifted[:rank])[:, :count]
    block_lane, block_sub = iota((count, LANES), 1), iota((count, LANES), 0)
    square = jnp.broadcast_to(sums[:, total : total + 1], (1, LANES))
    across = jnp.where(
        block_lane[0:1] == chosen, square, pltpu.roll(sums, LANES - rank, 1)
    )
    block = jnp.where(block_lane == chosen, down[rank:total], shifted[rank:total])
    block = jnp.where(block_sub == chosen, jnp.broadcast_to(across, (count, LANES)), block)
    second = first - dot(modes, first, 1, 0)
    both = first + second
    third = first - dot(modes, both, 1, 0)
    coefficients[...] = both
    square = dot(
        jnp.concatenate([first, both], axis=0), jnp.concatenate([both, third], axis=0), 0, 0
    )
    square = jnp.concatenate([square, jnp.zeros((count, LANES - count), jnp.float32)], axis=1)
    state = jnp.where(block_lane < count, block - square, 0.0)
    state = jnp.where(block_lane == block_sub + count, 1.0, state)
    for step in range(count - 1):
        row = state[step : step + 1, :]
        scale = state[:, step : step + 1] / row[:, step : step + 1]
        scale = jnp.where(block_sub > step, jnp.broadcast_to(scale, (count, LANES)), 0.0)
        state = state - scale * row
    diagonal = jnp.sum(jnp.where(block_lane == block_sub, state, 0.0), axis=1, keepdims=True)
    state = state / jnp.sqrt(diagonal)
    r_factor[...] = jnp.where(block_lane >= block_sub, state, 0.0)[:, :count]
    inverse = pltpu.roll(state, LANES - count, 1)
    inverse = jnp.where(block_lane < count, inverse, 0.0)
    onto_modes = dot(inverse[:, :count], both, 1, 1)
    own = jnp.sum(jnp.where(block_lane == chosen, inverse, 0.0), axis=1, keepdims=True)
    onto_block = pltpu.roll(jnp.where(block_lane == chosen, 0.0, inverse), rank, 1)
    onto_modes = jnp.concatenate(
        [-onto_modes, jnp.zeros((count, LANES - rank), jnp.float32)], axis=1
    )
    weights = jnp.where(block_lane < rank, onto_modes, onto_block)[:, :total]
    for c in range(3):
        for level in range(levels):
            lanes = slice((c * levels + level) * points, (c * levels + level + 1) * points)
            columns_out[:, c, 0, level, :] = (
                dot(weights, joined[:, lanes], 1, 0) + own * column[0:1, lanes]
            )


def shifted(value, axis, step):
    count = lax.axis_size(axis)
    return lax.ppermute(value, axis, [(i, (i + step) % count) for i in range(count)])


def exchange(faces):
    x_low, x_high, y_row, z_low, z_high = faces
    return (
        shifted(x_high, "gx", 1),
        shifted(x_low, "gx", -1),
        shifted(y_row, "ga", 1),
        shifted(z_high, "gz", 1),
        shifted(z_low, "gz", -1),
    )


def on_device(fields, diffusivity, subsample_offsets, column_id, pod_basis, held_block):
    count, cells, height, width = fields.shape
    rank, columns = pod_basis.shape[0], held_block.shape[0]
    devices = 1
    for axis in AXES:
        devices *= lax.axis_size(axis)
    points = held_block.shape[-1]
    length = 3 * held_block.shape[3] * points
    faces = (
        struct(count, height, width),
        struct(count, height, width),
        struct(count, cells, width),
        struct(count, height, LANES),
        struct(count, height, LANES),
    )

    packed = pl.pallas_call(
        pack_kernel, in_specs=[VMEM], out_specs=[VMEM] * 5, out_shape=faces,
        compiler_params=params(16),
    )(fields)
    halos = exchange(packed)

    joined, gram_message = pl.pallas_call(
        gram_kernel, in_specs=[VMEM] * 2, out_specs=[VMEM] * 2,
        out_shape=(struct(rank + columns, length), struct(devices, LANES)),
        compiler_params=params(24),
    )(pod_basis, held_block)
    pieces = lax.all_to_all(gram_message, AXES, 0, 0, tiled=True)

    first, *packed = pl.pallas_call(
        first_kernel, in_specs=[SMEM] + [VMEM] * 6, out_specs=[VMEM] * 6,
        out_shape=(struct(*fields.shape),) + faces,
        compiler_params=params(24),
    )(diffusivity, fields, *halos)
    halos = exchange(packed)

    fields_out, snapshot = pl.pallas_call(
        second_kernel, in_specs=[SMEM] * 2 + [VMEM] * 7, out_specs=[VMEM] * 2,
        out_shape=(struct(*fields.shape), struct(LANES, LANES)),
        scratch_shapes=[pltpu.VMEM((LANES, width), jnp.float32)],
        compiler_params=params(24),
    )(diffusivity, subsample_offsets, fields, first, *halos)
    relayed = lax.all_to_all(snapshot.reshape(8, 16, LANES), "gz", 0, 0, tiled=True)

    message, column = pl.pallas_call(
        product_kernel, in_specs=[VMEM] * 3, out_specs=[VMEM] * 2,
        out_shape=(struct(devices, LANES), struct(8, length)),
        scratch_shapes=[pltpu.VMEM((LANES, LANES), jnp.float32)],
        compiler_params=params(16),
    )(relayed, joined, pieces)
    gathered = lax.all_to_all(message, AXES, 0, 0, tiled=True)

    coefficients, r_factor, new_columns = pl.pallas_call(
        final_kernel, in_specs=[SMEM] + [VMEM] * 3, out_specs=[VMEM] * 3,
        out_shape=(
            struct(rank, columns), struct(columns, columns), struct(*held_block.shape)
        ),
        compiler_params=params(24),
    )(column_id, gathered, joined, column)
    return fields_out, coefficients, r_factor, new_columns


def solution(mesh):
    placed = (
        P(None, "gx", "ga", "gz"),
        P(),
        P(),
        P(),
        P(None, None, ("gx", "gz"), "ga", None),
        P(None, None, ("gx", "gz"), "ga", None),
    )
    return jax.shard_map(
        on_device,
        mesh=mesh,
        in_specs=placed,
        out_specs=(P(None, "gx", "ga", "gz"), P(), P(), P(None, None, ("gx", "gz"), "ga", None)),
        check_vma=False,
    )
```

time: 463 us -> 111 us (0.24); the launches traced: 457 us -> 110 us
  blocking collectives: 225 us -> 9.29 us
  local copies, waits for them, and re-layouts: 102 us -> 9.21 us
  other arithmetic: 57.4 us -> 0 us
  Pallas kernels: 0 us -> 27.2 us
  starting transfers between devices: 31.4 us -> 44 us
  matrix products: 6.87 us -> 0 us
  waiting for transfers between devices: 25.8 us -> 19.2 us
  between operations: 7.7 us -> 1.37 us
    psum x3 -> x0, blocking collectives: 225 us -> none  [the longest x1 79.2 us: on_device(): lax.psum(inner(matrix_q, matrix_b), ('gx', 'gz', 'ga')) / row_total]
    reshape x3 -> x0, local copies, waits for them, and re-layouts: 57 us -> none  [the longest x1 53.3 us: on_device(): fields_out[:3]]
    pallas_call x0 -> x6, Pallas kernels: none -> 27.2 us  [the longest x1 7.71 us: on_device(): pl.pallas_call(first_kernel, in_specs=[SMEM] + [VMEM] * 6, out_specs=[VME...]
    mul x7 -> x0, other arithmetic: 25.4 us -> none  [the longest x2 10.7 us: with_walls(): return extended * keep.astype(jnp.float32)[None, None, :, None]]
    all_to_all x1 -> x2, starting transfers between devices: 4.43 us -> 23.1 us  [the longest x1 14.2 us: on_device(): pieces = lax.all_to_all(gram_message, AXES, 0, 0, tiled=True)]
    ppermute x12 -> x10, waiting for transfers between devices: 25.8 us -> 7.16 us  [shifted(): lax.ppermute(value, axis, [(i, (i + step) % count) for i in range(count)])]
    all_to_all x1 -> x2, waiting for transfers between devices: 0.01 us -> 12 us  [the longest x1 12 us: on_device(): gathered = lax.all_to_all(message, AXES, 0, 0, tiled=True)]
    slice x12 -> x0, local copies, waits for them, and re-layouts: 10.8 us -> none  [the longest x5 4.88 us: extended_2(): lax.slice_in_dim(block, block.shape[dim] - width, None, axis=dim)]
  transfers between devices with their start and end apart: 13 -> 12, of which waited for: 7 -> 5; matrix products, arithmetic and copies ran while one was open for 4% -> 0% of each run, Pallas kernels for 0% -> 17%
where the time goes in v1:
time: 111 us; the launch traced here: 110 us
  starting transfers between devices  44 us (40%)
  Pallas kernels  27.2 us (25%)
  waiting for transfers between devices  19.2 us (17%)
  blocking collectives  9.29 us (8%)
  local copies, waits for them, and re-layouts  9.21 us (8%)
  between operations  1.37 us (1%)
    ppermute x10, starting transfers between devices, shifted(): lax.ppermute(value, axis, [(i, (i + step) % count) for i in range(count)])  20.9 us
    all_to_all x1, starting transfers between devices, on_device(): pieces = lax.all_to_all(gram_message, AXES, 0, 0, tiled=True)  14.2 us
    all_to_all x1, waiting for transfers between devices, on_device(): gathered = lax.all_to_all(message, AXES, 0, 0, tiled=True)  12 us
    all_to_all x1, blocking collectives, on_device(): lax.all_to_all(snapshot.reshape(8, 16, LANES), 'gz', 0, 0, tiled=True)  9.29 us
    unnamed x19, local copies, waits for them, and re-layouts  9.21 us
    all_to_all x1, starting transfers between devices, on_device(): gathered = lax.all_to_all(message, AXES, 0, 0, tiled=True)  8.88 us
    pallas_call x1, Pallas kernels, on_device(): pl.pallas_call(first_kernel, in_specs=[SMEM] + [VMEM] * 6, out_specs=[VME...  7.71 us
    ppermute x10, waiting for transfers between devices, shifted(): lax.ppermute(value, axis, [(i, (i + step) % count) for i in range(count)])  7.16 us
  transfers between devices with their start and end apart: 12, of which 5 were waited for; matrix products, arithmetic and copies ran while one was open for 0% of the time, Pallas kernels for 17%

profile of v1, /device:TPU:1, one launch (start us, length us, event | category | flops | bytes accessed | tf_op | source)
XLA Modules:
  0.0 110.2 jit_solution(18028208187457593073)
XLA Ops:
  0.6 1.7 %copy-done = f32[5,32,16,256]{3,2,1,0:T(8,128)S(1)} copy-done((f32[5,32,16,256]{3,2,1,0:T(8,128)S(1)}, f32[5,32,16,256]{3,2,1,0:T(8,128)}, u32[]{:S(2)}) %copy-start) | copy-done | bytes 2621464
  2.4 3.0 %shard_map.93 = (f32[5,16,256]{2,1,0:T(8,128)S(1)}, f32[5,16,256]{2,1,0:T(8,128)S(1)}, f32[5,32,256]{2,1,0:T(8,128)S(1)}, f32[5,16,128]{2,1,0:T(8,128)S(1)}, f32[5,16,128]{2,1,0:T(8,128)S(1)}) custom-call(f32[5,32,16,256]{3,2,1,0:T(8,128)S(1)} %copy-done), custom_call_target="tpu_custom_call" | custom-call | tf_op jit(solution)/shard_map/pallas_call | solution.py:404
  5.4 2.6 %collective-permute-start.2 = (f32[5,32,256]{2,1,0:T(8,128)S(1)}, f32[5,32,256]{2,1,0:T(8,128)S(1)}, u32[]{:S(2)}, u32[]{:S(2)}) collective-permute-start(f32[5,32,256]{2,1,0:T(8,128)S(1)} %get-tuple-element.26), channel_id=1, source_target_pairs={{0,1},{1,0},{2,3},{3,2},{4,5},{5,4},{6,7},{7,6},{8,9},{9,8},{10,11... | collective-permute-start | bytes 491528 | tf_op jit(solution)/shard_map/ppermute | solution.py:374
  7.9 1.4 %copy-done.5 = f32[64,3,1,4,512]{4,3,2,1,0:T(4,128)S(1)} copy-done((f32[64,3,1,4,512]{4,3,2,1,0:T(4,128)S(1)}, f32[64,3,1,4,512]{4,3,2,1,0:T(4,128)}, u32[]{:S(2)}) %copy-start.5) | copy-done | bytes 1572888
  9.3 1.0 copy-done.6
  10.3 4.6 %shard_map.96 = (f32[80,6144]{1,0:T(8,128)S(1)}, f32[256,128]{1,0:T(8,128)}) custom-call(f32[64,3,1,4,512]{4,3,2,1,0:T(4,128)S(1)} %copy-done.5, f32[16,3,1,4,512]{4,3,2,1,0:T(4,128)S(1)} %copy-done.6), custom_call_target="tpu_custom_call" | custom-call | tf_op jit(solution)/shard_map/pallas_call | solution.py:410
  14.9 1.3 %copy-done.2 = f32[80,6144]{1,0:T(8,128)} copy-done((f32[80,6144]{1,0:T(8,128)}, f32[80,6144]{1,0:T(8,128)S(1)}, u32[]{:S(2)}) %copy-start.2) | copy-done | bytes 1966104
  16.2 14.2 %all-to-all-start.1 = ((f32[256,1,128]{2,1,0:T(1,128)}), f32[256,1,128]{2,1,0:T(1,128)S(1)}, u32[]{:S(2)}, u32[]{:S(2)}) async-start(f32[256,1,128]{2,1,0:T(1,128)} %bitcast.2), calls=%async_computation.1 | async-start | bytes 262144 | tf_op jit(solution)/shard_map/all_to_all | solution.py:415
  30.5 1.5 %collective-permute-start = (f32[5,16,256]{2,1,0:T(8,128)S(1)}, f32[5,16,256]{2,1,0:T(8,128)S(1)}, u32[]{:S(2)}, u32[]{:S(2)}) collective-permute-start(f32[5,16,256]{2,1,0:T(8,128)S(1)} %get-tuple-element.24), channel_id=1, source_target_pairs={{0,16},{16,32},{32,48},{48,64},{64,80},{80,96},{96,112},{112,128},... | collective-permute-start | bytes 245768 | tf_op jit(solution)/shard_map/ppermute | solution.py:374
  31.9 5.8 %collective-permute-start.1 = (f32[5,16,256]{2,1,0:T(8,128)S(1)}, f32[5,16,256]{2,1,0:T(8,128)S(1)}, u32[]{:S(2)}, u32[]{:S(2)}) collective-permute-start(f32[5,16,256]{2,1,0:T(8,128)S(1)} %get-tuple-element.25), channel_id=1, source_target_pairs={{0,240},{16,0},{32,16},{48,32},{64,48},{80,64},{96,80},{112,96},{1... | collective-permute-start | bytes 245768 | tf_op jit(solution)/shard_map/ppermute | solution.py:374
  37.8 1.8 %collective-permute-start.3 = (f32[5,16,128]{2,1,0:T(8,128)S(1)}, f32[5,16,128]{2,1,0:T(8,128)S(1)}, u32[]{:S(2)}, u32[]{:S(2)}) collective-permute-start(f32[5,16,128]{2,1,0:T(8,128)S(1)} %get-tuple-element.27), channel_id=1, source_target_pairs={{0,2},{2,4},{4,6},{6,8},{8,10},{10,12},{12,14},{14,0},{1,3},{3,5},... | collective-permute-start | bytes 122888 | tf_op jit(solution)/shard_map/ppermute | solution.py:374
  39.5 0.0 collective-permute-start.4
  39.5 1.1 collective-permute-done.3.z_before
  40.6 2.6 %collective-permute-done.4.z_after = f32[5,16,128]{2,1,0:T(8,128)S(1)} collective-permute-done((f32[5,16,128]{2,1,0:T(8,128)S(1)}, f32[5,16,128]{2,1,0:T(8,128)S(1)}, u32[]{:S(2)}, u32[]{:S(2)}) %collective-permute-start.4) | collective-permute-done | bytes 40992 | tf_op jit(solution)/shard_map/ppermute | solution.py:374
  43.3 0.0 collective-permute-done.2.y_halo
  43.3 7.7 %shard_map.94 = (f32[5,32,16,256]{3,2,1,0:T(8,128)S(1)}, f32[5,16,256]{2,1,0:T(8,128)S(1)}, f32[5,16,256]{2,1,0:T(8,128)S(1)}, f32[5,32,256]{2,1,0:T(8,128)S(1)}...) custom-call(f32[5]{0:T(128)S(1)} %copy-done.7, f32[5,32,16,256]{3,2,1,0:T(8,128)S(1)} %copy-done.1, ...), custom_call_target="tpu_custom_call" | custom-call | tf_op jit(solution)/shard_map/pallas_call | solution.py:417
  51.0 1.1 collective-permute-start.7
  52.1 0.0 collective-permute-start.5
  52.1 5.7 %collective-permute-start.6 = (f32[5,16,256]{2,1,0:T(8,128)S(1)}, f32[5,16,256]{2,1,0:T(8,128)S(1)}, u32[]{:S(2)}, u32[]{:S(2)}) collective-permute-start(f32[5,16,256]{2,1,0:T(8,128)S(1)} %get-tuple-element.31), channel_id=1, source_target_pairs={{0,240},{16,0},{32,16},{48,32},{64,48},{80,64},{96,80},{112,96},{1... | collective-permute-start | bytes 245768 | tf_op jit(solution)/shard_map/ppermute | solution.py:374
  57.8 2.5 %collective-permute-start.8 = (f32[5,16,128]{2,1,0:T(8,128)S(1)}, f32[5,16,128]{2,1,0:T(8,128)S(1)}, u32[]{:S(2)}, u32[]{:S(2)}) collective-permute-start(f32[5,16,128]{2,1,0:T(8,128)S(1)} %get-tuple-element.33), channel_id=1, source_target_pairs={{0,2},{2,4},{4,6},{6,8},{8,10},{10,12},{12,14},{14,0},{1,3},{3,5},... | collective-permute-start | bytes 122888 | tf_op jit(solution)/shard_map/ppermute | solution.py:374
  60.3 1.1 collective-permute-done.8.z_before
  61.4 2.3 %collective-permute-done.9.z_after = f32[5,16,128]{2,1,0:T(8,128)S(1)} collective-permute-done((f32[5,16,128]{2,1,0:T(8,128)S(1)}, f32[5,16,128]{2,1,0:T(8,128)S(1)}, u32[]{:S(2)}, u32[]{:S(2)}) %collective-permute-start.9) | collective-permute-done | bytes 40992 | tf_op jit(solution)/shard_map/ppermute | solution.py:374
  63.7 0.0 collective-permute-done.6.x_after
  63.7 6.9 %shard_map.95 = (f32[5,32,16,256]{3,2,1,0:T(8,128)}, f32[128,128]{1,0:T(8,128)S(1)}) custom-call(f32[5]{0:T(128)S(1)} %copy-done.7, s32[3]{0:T(128)S(1)} %copy-done.8, f32[5,32,16,256]{3,2,1,0:T(8,128)S(1)} %copy-done.1, f32[5,32,16,256]{3,2,1,0:T(8,128)S(1)} %get-tuple-element.29.current, f32[5,16,256]{2,1,0:T(8,128)S(1)} %collective-permute-done.5.x_before, ...), custom_call_target="tpu_custom_call" | custom-call | tf_op jit(solution)/shard_map/pallas_call | solution.py:424
  70.6 9.3 %all_to_all.27.relayed = f32[8,16,128]{2,1,0:T(8,128)S(1)} all-to-all(f32[8,16,128]{2,1,0:T(8,128)S(1)} %bitcast.11), channel_id=1, replica_groups=mesh['gx'=16,'gz'=8,'ga'=2] {'gz'}, dimensions={0} | all-to-all | bytes 131072 | tf_op jit(solution)/shard_map/all_to_all | solution.py:430
  79.9 1.5 %copy-done.3 = f32[80,6144]{1,0:T(8,128)S(1)} copy-done((f32[80,6144]{1,0:T(8,128)S(1)}, f32[80,6144]{1,0:T(8,128)}, u32[]{:S(2)}) %copy-start.3) | copy-done | bytes 1966104
  81.4 1.0 shard_map.97
  82.5 8.9 %all-to-all-start.2 = ((f32[256,1,128]{2,1,0:T(1,128)}), f32[256,1,128]{2,1,0:T(1,128)S(1)}, u32[]{:S(2)}, u32[]{:S(2)}) async-start(f32[256,1,128]{2,1,0:T(1,128)} %bitcast.5), calls=%async_computation.2 | async-start | bytes 262144 | tf_op jit(solution)/shard_map/all_to_all | solution.py:438
  92.0 12.0 %all-to-all-done.2 = f32[256,1,128]{2,1,0:T(1,128)S(1)} async-done(((f32[256,1,128]{2,1,0:T(1,128)}), f32[256,1,128]{2,1,0:T(1,128)S(1)}, u32[]{:S(2)}, u32[]{:S(2)}) %all-to-all-start.2) | async-done | bytes 131104 | tf_op jit(solution)/shard_map/all_to_all | solution.py:438
  104.1 1.5 %copy-done.4 = f32[80,6144]{1,0:T(8,128)S(1)} copy-done((f32[80,6144]{1,0:T(8,128)S(1)}, f32[80,6144]{1,0:T(8,128)}, u32[]{:S(2)}) %copy-start.4) | copy-done | bytes 1966104
  105.6 4.0 %shard_map.98 = (f32[64,16]{1,0:T(8,128)S(1)}, f32[16,16]{1,0:T(8,128)}, f32[16,3,1,4,512]{4,3,2,1,0:T(4,128)}) custom-call(s32[1]{0:T(128)S(6)} %copy.14.column_id, f32[256,128]{1,0:T(8,128)S(1)} %bitcast.10, f32[80,6144]{1,0:T(8,128)S(1)} %copy-done.4, f32[8,6144]{1,0:T(8,128)S(1)} %get-tuple-element.40.column), custom_call_target="tpu_custom_call" | custom-call | tf_op jit(solution)/shard_map/pallas_call | solution.py:440
  109.6 0.7 copy.13
  (18 shorter events, 0.0 us)
Async XLA Ops:
  0.6 1.7 %copy-start = (f32[5,32,16,256]{3,2,1,0:T(8,128)S(1)}, f32[5,32,16,256]{3,2,1,0:T(8,128)}, u32[]{:S(2)}) copy-start(f32[5,32,16,256]{3,2,1,0:T(8,128)} %start.1) | copy-start | bytes 7864324
  2.4 40.9 %copy-start.1 = (f32[5,32,16,256]{3,2,1,0:T(8,128)S(1)}, f32[5,32,16,256]{3,2,1,0:T(8,128)}, u32[]{:S(2)}) copy-start(f32[5,32,16,256]{3,2,1,0:T(8,128)} %start.1) | copy-start | bytes 7864324
  2.4 40.9 %copy-start.7 = (f32[5]{0:T(128)S(1)}, f32[5]{0:T(128)}, u32[]{:S(2)}) copy-start(f32[5]{0:T(128)} %diffusivity.3) | copy-start | bytes 64
  5.4 37.9 %collective-permute-start.2 = (f32[5,32,256]{2,1,0:T(8,128)S(1)}, f32[5,32,256]{2,1,0:T(8,128)S(1)}, u32[]{:S(2)}, u32[]{:S(2)}) collective-permute-start(f32[5,32,256]{2,1,0:T(8,128)S(1)} %get-tuple-element.26), channel_id=1, source_target_pairs={{0,1},{1,0},{2,3},{3,2},{4,5},{5,4},{6,7},{7,6},{8,9},{9,8},{10,11... | collective-permute-start | bytes 491528 | tf_op jit(solution)/shard_map/ppermute | solution.py:374
  7.9 1.4 %copy-start.5 = (f32[64,3,1,4,512]{4,3,2,1,0:T(4,128)S(1)}, f32[64,3,1,4,512]{4,3,2,1,0:T(4,128)}, u32[]{:S(2)}) copy-start(f32[64,3,1,4,512]{4,3,2,1,0:T(4,128)} %basis.1) | copy-start | bytes 4718596
  9.3 1.0 copy-start.6
  10.3 53.4 %copy-start.8 = (s32[3]{0:T(128)S(1)}, s32[3]{0:T(128)}, u32[]{:S(2)}) copy-start(s32[3]{0:T(128)} %offsets.1) | copy-start | bytes 40
  14.9 1.3 %copy-start.2 = (f32[80,6144]{1,0:T(8,128)}, f32[80,6144]{1,0:T(8,128)S(1)}, u32[]{:S(2)}) copy-start(f32[80,6144]{1,0:T(8,128)S(1)} %get-tuple-element.37.joined) | copy-start | bytes 5898244
  16.2 54.4 %all-to-all-start.1 = ((f32[256,1,128]{2,1,0:T(1,128)}), f32[256,1,128]{2,1,0:T(1,128)S(1)}, u32[]{:S(2)}, u32[]{:S(2)}) async-start(f32[256,1,128]{2,1,0:T(1,128)} %bitcast.2), calls=%async_computation.1 | async-start | bytes 262144 | tf_op jit(solution)/shard_map/all_to_all | solution.py:415
  30.5 12.8 %collective-permute-start = (f32[5,16,256]{2,1,0:T(8,128)S(1)}, f32[5,16,256]{2,1,0:T(8,128)S(1)}, u32[]{:S(2)}, u32[]{:S(2)}) collective-permute-start(f32[5,16,256]{2,1,0:T(8,128)S(1)} %get-tuple-element.24), channel_id=1, source_target_pairs={{0,16},{16,32},{32,48},{48,64},{64,80},{80,96},{96,112},{112,128},... | collective-permute-start | bytes 245768 | tf_op jit(solution)/shard_map/ppermute | solution.py:374
  31.9 11.3 %collective-permute-start.1 = (f32[5,16,256]{2,1,0:T(8,128)S(1)}, f32[5,16,256]{2,1,0:T(8,128)S(1)}, u32[]{:S(2)}, u32[]{:S(2)}) collective-permute-start(f32[5,16,256]{2,1,0:T(8,128)S(1)} %get-tuple-element.25), channel_id=1, source_target_pairs={{0,240},{16,0},{32,16},{48,32},{64,48},{80,64},{96,80},{112,96},{1... | collective-permute-start | bytes 245768 | tf_op jit(solution)/shard_map/ppermute | solution.py:374
  37.8 2.9 %collective-permute-start.3 = (f32[5,16,128]{2,1,0:T(8,128)S(1)}, f32[5,16,128]{2,1,0:T(8,128)S(1)}, u32[]{:S(2)}, u32[]{:S(2)}) collective-permute-start(f32[5,16,128]{2,1,0:T(8,128)S(1)} %get-tuple-element.27), channel_id=1, source_target_pairs={{0,2},{2,4},{4,6},{6,8},{8,10},{10,12},{12,14},{14,0},{1,3},{3,5},... | collective-permute-start | bytes 122888 | tf_op jit(solution)/shard_map/ppermute | solution.py:374
  39.5 3.7 %collective-permute-start.4 = (f32[5,16,128]{2,1,0:T(8,128)S(1)}, f32[5,16,128]{2,1,0:T(8,128)S(1)}, u32[]{:S(2)}, u32[]{:S(2)}) collective-permute-start(f32[5,16,128]{2,1,0:T(8,128)S(1)} %get-tuple-element.28), channel_id=1, source_target_pairs={{0,14},{2,0},{4,2},{6,4},{8,6},{10,8},{12,10},{14,12},{1,15},{3,1}... | collective-permute-start | bytes 122888 | tf_op jit(solution)/shard_map/ppermute | solution.py:374
  51.0 12.7 %collective-permute-start.7 = (f32[5,32,256]{2,1,0:T(8,128)S(1)}, f32[5,32,256]{2,1,0:T(8,128)S(1)}, u32[]{:S(2)}, u32[]{:S(2)}) collective-permute-start(f32[5,32,256]{2,1,0:T(8,128)S(1)} %get-tuple-element.32), channel_id=1, source_target_pairs={{0,1},{1,0},{2,3},{3,2},{4,5},{5,4},{6,7},{7,6},{8,9},{9,8},{10,11... | collective-permute-start | bytes 491528 | tf_op jit(solution)/shard_map/ppermute | solution.py:374
  52.1 11.6 %collective-permute-start.5 = (f32[5,16,256]{2,1,0:T(8,128)S(1)}, f32[5,16,256]{2,1,0:T(8,128)S(1)}, u32[]{:S(2)}, u32[]{:S(2)}) collective-permute-start(f32[5,16,256]{2,1,0:T(8,128)S(1)} %get-tuple-element.30), channel_id=1, source_target_pairs={{0,16},{16,32},{32,48},{48,64},{64,80},{80,96},{96,112},{112,128},... | collective-permute-start | bytes 245768 | tf_op jit(solution)/shard_map/ppermute | solution.py:374
  52.1 11.6 %collective-permute-start.6 = (f32[5,16,256]{2,1,0:T(8,128)S(1)}, f32[5,16,256]{2,1,0:T(8,128)S(1)}, u32[]{:S(2)}, u32[]{:S(2)}) collective-permute-start(f32[5,16,256]{2,1,0:T(8,128)S(1)} %get-tuple-element.31), channel_id=1, source_target_pairs={{0,240},{16,0},{32,16},{48,32},{64,48},{80,64},{96,80},{112,96},{1... | collective-permute-start | bytes 245768 | tf_op jit(solution)/shard_map/ppermute | solution.py:374
  57.8 3.6 %collective-permute-start.8 = (f32[5,16,128]{2,1,0:T(8,128)S(1)}, f32[5,16,128]{2,1,0:T(8,128)S(1)}, u32[]{:S(2)}, u32[]{:S(2)}) collective-permute-start(f32[5,16,128]{2,1,0:T(8,128)S(1)} %get-tuple-element.33), channel_id=1, source_target_pairs={{0,2},{2,4},{4,6},{6,8},{8,10},{10,12},{12,14},{14,0},{1,3},{3,5},... | collective-permute-start | bytes 122888 | tf_op jit(solution)/shard_map/ppermute | solution.py:374
  60.3 3.4 %collective-permute-start.9 = (f32[5,16,128]{2,1,0:T(8,128)S(1)}, f32[5,16,128]{2,1,0:T(8,128)S(1)}, u32[]{:S(2)}, u32[]{:S(2)}) collective-permute-start(f32[5,16,128]{2,1,0:T(8,128)S(1)} %get-tuple-element.34), channel_id=1, source_target_pairs={{0,14},{2,0},{4,2},{6,4},{8,6},{10,8},{12,10},{14,12},{1,15},{3,1}... | collective-permute-start | bytes 122888 | tf_op jit(solution)/shard_map/ppermute | solution.py:374
  79.9 1.5 %copy-start.3 = (f32[80,6144]{1,0:T(8,128)S(1)}, f32[80,6144]{1,0:T(8,128)}, u32[]{:S(2)}) copy-start(f32[80,6144]{1,0:T(8,128)} %copy-done.2) | copy-start | bytes 5898244
  82.5 21.6 %all-to-all-start.2 = ((f32[256,1,128]{2,1,0:T(1,128)}), f32[256,1,128]{2,1,0:T(1,128)S(1)}, u32[]{:S(2)}, u32[]{:S(2)}) async-start(f32[256,1,128]{2,1,0:T(1,128)} %bitcast.5), calls=%async_computation.2 | async-start | bytes 262144 | tf_op jit(solution)/shard_map/all_to_all | solution.py:438
  104.0 1.5 %copy-start.4 = (f32[80,6144]{1,0:T(8,128)S(1)}, f32[80,6144]{1,0:T(8,128)}, u32[]{:S(2)}) copy-start(f32[80,6144]{1,0:T(8,128)} %copy-done.2) | copy-start | bytes 5898244

commit v2 on v1

--- a/solution.py
+++ b/solution.py
@@ -7,6 +7,8 @@
 
 STRIDE = 4
 LANES = 128
+PACK_UNROLL = 4
+PLANE_UNROLL = 3
 
 time_step = 0.1
 smagorinsky = 0.02
@@ -76,7 +78,7 @@
                     )
         return carry
 
-    lax.fori_loop(0, cells, body, 0)
+    lax.fori_loop(0, cells, body, 0, unroll=PACK_UNROLL)
 
 
 def stage_plane(x, current, before, after, y_halo, z_before, z_after, diffusivity, upper):
@@ -184,12 +186,12 @@
         one(x, inside(-1, x), inside(1, x))
         return carry
 
-    lax.fori_loop(1, cells - 1, body, 0)
+    lax.fori_loop(1, cells - 1, body, 0, unroll=PLANE_UNROLL)
     one(cells - 1, inside(-1, cells - 1), outside(x_after))
 
 
 def first_kernel(
-    diffusivity, current, x_before, x_after, y_halo, z_before, z_after,
+    diffusivity, folded, current, x_before, x_after, y_halo, z_before, z_after,
     first, x_low, x_high, y_row, z_low, z_high,
 ):
     count, cells = current.shape[:2]
@@ -198,6 +200,10 @@
     y_row[...] = jnp.zeros_like(y_row)
     z_low[...] = jnp.zeros_like(z_low)
     z_high[...] = jnp.zeros_like(z_high)
+    for group in range(3):
+        lanes = slice(group % 2 * LANES, (group % 2 + 1) * LANES)
+        given = jnp.where(upper, folded[group * 8 : group * 8 + 8], folded[group * 8 + 24 : group * 8 + 32])
+        y_row[group // 2, cells:, lanes] = given
 
     def finish(x, centre, rates):
         for f in range(count):
@@ -221,7 +227,7 @@
 
 
 def second_kernel(
-    diffusivity, offsets, start, current, x_before, x_after, y_halo, z_before, z_after,
+    diffusivity, offsets, folded, start, current, x_before, x_after, y_halo, z_before, z_after,
     result, snapshot, picked,
 ):
     count, cells, height, width = current.shape
@@ -252,12 +258,21 @@
     points = width // STRIDE
     choose = iota((width, LANES), 0) == STRIDE * (iota((width, LANES), 1) % points) + offsets[0]
     snapshot[...] = dot(picked[...], choose.astype(jnp.float32), 1, 0)
-
-
-def gram_kernel(basis, held, joined, message):
+    upper = lax.axis_index("ga") > 0
+    for group in range(3):
+        lanes = slice(group % 2 * LANES, (group % 2 + 1) * LANES)
+        kept = jnp.where(upper, folded[group * 8 + 24 : group * 8 + 32], folded[group * 8 : group * 8 + 8])
+        kept = kept + y_halo[group // 2, cells:, lanes]
+        for column in range(cells // STRIDE):
+            row = column * 16 + 12 + group
+            snapshot[row : row + 1, :] = kept[column : column + 1]
+
+
+def gram_kernel(basis, held, joined, folded):
     rank, _, _, levels, points = basis.shape
     columns = held.shape[0]
     total = rank + columns
+    half = total // 2
     for c in range(3):
         for level in range(levels):
             lanes = slice((c * levels + level) * points, (c * levels + level + 1) * points)
@@ -270,17 +285,18 @@
 
     gram = lax.fori_loop(0, 3 * levels, body, jnp.zeros((total, total), jnp.float32))
     gram = jnp.concatenate([gram, jnp.zeros((total, LANES - total), jnp.float32)], axis=1)
-    for piece in range(3):
-        message[piece * total : (piece + 1) * total, :] = pltpu.roll(
-            gram, (LANES - 27 * piece) % LANES, 1
-        )
-    message[3 * total :, :] = jnp.zeros((message.shape[0] - 3 * total, LANES), jnp.float32)
-
-
-def product_kernel(relayed, joined, pieces, message, column, partial):
+    lane, sub = iota((half, LANES), 1), iota((half, LANES), 0)
+    lower = pltpu.roll(gram[half:], LANES - half, 1)
+    diagonal = jnp.sum(jnp.where(lane == sub, lower, 0.0), axis=1, keepdims=True)
+    values = jnp.where((lane < sub), lower, gram[:half])
+    values = jnp.where(lane == total, jnp.broadcast_to(diagonal, (half, LANES)), values)
+    folded[0:half, :] = jnp.where(lane <= total, values, 0.0)
+    folded[half:, :] = jnp.zeros((folded.shape[0] - half, LANES), jnp.float32)
+
+
+def product_kernel(relayed, joined, message, column, partial):
     total = joined.shape[0]
     groups = total // 8
-    lane = iota((8, LANES), 1)
     low = iota((1, LANES), 1) < LANES // 2
     sums = [jnp.zeros((8, LANES), jnp.float32) for _ in range(groups + 1)]
     for row in range(12):
@@ -301,28 +317,49 @@
     for group in range(groups + 1):
         partial[group * 8 : group * 8 + 8, :] = sums[group]
     products = dot(jnp.ones((8, LANES), jnp.float32), partial[...], 1, 1)
-    own = jnp.sum(pieces[...].reshape(-1, 8, LANES), axis=0)
-    own = jnp.broadcast_to(jnp.sum(own, axis=0, keepdims=True), (8, LANES))
-    values = jnp.where(lane < 96, products, pltpu.roll(own, 96, 1))
+    own = jnp.sum(relayed[:, 8:16, :], axis=0)
     count = message.shape[0]
-    message[...] = jnp.broadcast_to(values[None], (count // 8, 8, LANES)).reshape(count, LANES)
-
-
-def final_kernel(column_id, gathered, joined, column, coefficients, r_factor, columns_out):
+    lane, which = iota((24, LANES), 1), iota((24, LANES), 0) % 3
+    values = jnp.zeros((24, LANES), jnp.float32)
+    for piece in range(3):
+        moved = pltpu.roll(products, 88 - 40 * piece if piece < 2 else 8, 1)[0:1]
+        row = jnp.where(lane[0:1] < 88, own[4 + piece : 5 + piece], moved)
+        values = jnp.where(which == piece, row, values)
+    message[...] = jnp.broadcast_to(values[None], (count // 24, 24, LANES)).reshape(count, LANES)
+
+
+def final_kernel(
+    column_id, gathered, joined, column, coefficients, r_factor, columns_out, stacked
+):
     total = joined.shape[0]
-    rank, count = coefficients.shape
+    count, rank = coefficients.shape
     _, _, _, levels, points = columns_out.shape
-    rows_total = float(gathered.shape[0] * joined.shape[1])
+    rows_total = float(gathered.shape[0] // 3 * joined.shape[1])
     chosen = column_id[0]
-    received = gathered[...]
-    sums = jnp.sum(received.reshape(-1, 8, LANES), axis=0)
-    sums = jnp.sum(sums, axis=0, keepdims=True) / rows_total
+    half = total // 2
+    stacked[...] = jnp.sum(gathered[...].reshape(-1, 48, LANES), axis=0)
+    pieces = [
+        [stacked[pl.ds(part * 3 + piece, 8, stride=6), :] for piece in range(3)]
+        for part in range(2)
+    ]
+    sums = [jnp.sum(pieces[0][i] + pieces[1][i], axis=0, keepdims=True) for i in range(3)]
+    sums = [pltpu.roll(row, shift, 1) for row, shift in zip(sums, (40, 80, 120))]
+    lane = iota((1, LANES), 1)
+    sums = jnp.where(lane < 40, sums[0], jnp.where(lane < 80, sums[1], sums[2])) / rows_total
+    folded = jnp.concatenate(pieces[0] + pieces[1][:2], axis=0) / rows_total
+    turned = jnp.concatenate([folded, jnp.zeros((LANES - half, LANES), jnp.float32)], axis=0).T
+    lane, sub = iota((half, LANES), 1), iota((half, LANES), 0)
+    diagonal = jnp.broadcast_to(folded[:, total : total + 1], (half, LANES))
+    upper = jnp.where((lane >= sub), folded, turned[:half])
+    lower = jnp.where(lane < sub, folded, jnp.where(lane > sub, turned[:half], diagonal))
+    gram = jnp.concatenate(
+        [
+            upper,
+            jnp.where(lane < half, turned[half:total], pltpu.roll(lower, half, 1)),
+        ],
+        axis=0,
+    )
     lane = iota((total, LANES), 1)
-    pieces = [
-        pltpu.roll(received[piece * total : (piece + 1) * total, :], (27 * piece + 32) % LANES, 1)
-        for piece in range(3)
-    ]
-    gram = jnp.where(lane < 27, pieces[0], jnp.where(lane < 54, pieces[1], pieces[2])) / rows_total
     down = jnp.broadcast_to(sums, (LANES, LANES)).T
     modes = gram[:rank, :rank]
     shifted = pltpu.roll(gram, LANES - rank, 1)
@@ -337,7 +374,6 @@
     second = first - dot(modes, first, 1, 0)
     both = first + second
     third = first - dot(modes, both, 1, 0)
-    coefficients[...] = both
     square = dot(
         jnp.concatenate([first, both], axis=0), jnp.concatenate([both, third], axis=0), 0, 0
     )
@@ -352,6 +388,9 @@
     diagonal = jnp.sum(jnp.where(block_lane == block_sub, state, 0.0), axis=1, keepdims=True)
     state = state / jnp.sqrt(diagonal)
     r_factor[...] = jnp.where(block_lane >= block_sub, state, 0.0)[:, :count]
+    padded = jnp.concatenate([both, jnp.zeros((rank, LANES - count), jnp.float32)], axis=1)
+    padded = jnp.concatenate([padded, jnp.zeros((LANES - rank, LANES), jnp.float32)], axis=0)
+    coefficients[...] = padded.T[:count, :rank]
     inverse = pltpu.roll(state, LANES - count, 1)
     inverse = jnp.where(block_lane < count, inverse, 0.0)
     onto_modes = dot(inverse[:, :count], both, 1, 1)
@@ -407,44 +446,44 @@
     )(fields)
     halos = exchange(packed)
 
-    joined, gram_message = pl.pallas_call(
+    joined, folded = pl.pallas_call(
         gram_kernel, in_specs=[VMEM] * 2, out_specs=[VMEM] * 2,
-        out_shape=(struct(rank + columns, length), struct(devices, LANES)),
+        out_shape=(struct(rank + columns, length), struct(48, LANES)),
         compiler_params=params(24),
     )(pod_basis, held_block)
-    pieces = lax.all_to_all(gram_message, AXES, 0, 0, tiled=True)
-
     first, *packed = pl.pallas_call(
-        first_kernel, in_specs=[SMEM] + [VMEM] * 6, out_specs=[VMEM] * 6,
-        out_shape=(struct(*fields.shape),) + faces,
+        first_kernel, in_specs=[SMEM] + [VMEM] * 7, out_specs=[VMEM] * 6,
+        out_shape=(struct(*fields.shape),) + faces[:2] + (struct(count, cells + 8, width),) + faces[3:],
         compiler_params=params(24),
-    )(diffusivity, fields, *halos)
+    )(diffusivity, folded, fields, *halos)
     halos = exchange(packed)
 
     fields_out, snapshot = pl.pallas_call(
-        second_kernel, in_specs=[SMEM] * 2 + [VMEM] * 7, out_specs=[VMEM] * 2,
+        second_kernel, in_specs=[SMEM] * 2 + [VMEM] * 8, out_specs=[VMEM] * 2,
         out_shape=(struct(*fields.shape), struct(LANES, LANES)),
         scratch_shapes=[pltpu.VMEM((LANES, width), jnp.float32)],
         compiler_params=params(24),
-    )(diffusivity, subsample_offsets, fields, first, *halos)
+    )(diffusivity, subsample_offsets, folded, fields, first, *halos)
     relayed = lax.all_to_all(snapshot.reshape(8, 16, LANES), "gz", 0, 0, tiled=True)
 
     message, column = pl.pallas_call(
-        product_kernel, in_specs=[VMEM] * 3, out_specs=[VMEM] * 2,
-        out_shape=(struct(devices, LANES), struct(8, length)),
+        product_kernel, in_specs=[VMEM] * 2, out_specs=[VMEM] * 2,
+        out_shape=(struct(devices * 3, LANES), struct(8, length)),
         scratch_shapes=[pltpu.VMEM((LANES, LANES), jnp.float32)],
         compiler_params=params(16),
-    )(relayed, joined, pieces)
-    gathered = lax.all_to_all(message, AXES, 0, 0, tiled=True)
+    )(relayed, joined)
+    message = message.reshape(devices * 3, 1, LANES)
+    gathered = lax.all_to_all(message, AXES, 0, 0, tiled=True).reshape(devices * 3, LANES)
 
     coefficients, r_factor, new_columns = pl.pallas_call(
         final_kernel, in_specs=[SMEM] + [VMEM] * 3, out_specs=[VMEM] * 3,
         out_shape=(
-            struct(rank, columns), struct(columns, columns), struct(*held_block.shape)
+            struct(columns, rank), struct(columns, columns), struct(*held_block.shape)
         ),
+        scratch_shapes=[pltpu.VMEM((48, LANES), jnp.float32)],
         compiler_params=params(24),
     )(column_id, gathered, joined, column)
-    return fields_out, coefficients, r_factor, new_columns
+    return fields_out, coefficients.T, r_factor, new_columns
 
 
 def solution(mesh):

time: 111 us -> 89.3 us (0.80)
  starting transfers between devices: 44 us -> 30.2 us
  local copies, waits for them, and re-layouts: 9.21 us -> 4.15 us
  Pallas kernels: 27.2 us -> 23 us
  waiting for transfers between devices: 19.2 us -> 20.4 us
    all_to_all x2 -> x1, starting transfers between devices: 23.1 us -> 8.77 us  [on_device(): lax.all_to_all(message, AXES, 0, 0, tiled=True).reshape(devices * 3, LANES)]
    unnamed x19 -> x12, local copies, waits for them, and re-layouts: 9.21 us -> 4.15 us
    all_to_all x2 -> x1, waiting for transfers between devices: 12 us -> 16.7 us  [on_device(): lax.all_to_all(message, AXES, 0, 0, tiled=True).reshape(devices * 3, LANES)]
    ppermute x10, waiting for transfers between devices: 7.16 us -> 3.71 us  [shifted(): lax.ppermute(value, axis, [(i, (i + step) % count) for i in range(count)])]
    pallas_call x3, Pallas kernels: 15.6 us -> 13.6 us  [the longest x1 6.32 us: on_device(): pl.pallas_call(first_kernel, in_specs=[SMEM] + [VMEM] * 7, out_specs=[VME...]
    pallas_call x1, Pallas kernels: 2.97 us -> 1.34 us  [on_device(): pl.pallas_call(pack_kernel, in_specs=[VMEM], out_specs=[VMEM] * 5, out_sh...]
  transfers between devices with their start and end apart: 12 -> 11, of which waited for: 5 -> 3; matrix products, arithmetic and copies ran while one was open for 0% -> 0% of each run, Pallas kernels for 17% -> 5%
where the time goes in v2:
time: 89.3 us; the launch traced here: 89 us
  starting transfers between devices  30.2 us (34%)
  Pallas kernels  23 us (26%)
  waiting for transfers between devices  20.4 us (23%)
  blocking collectives  9.81 us (11%)
  local copies, waits for them, and re-layouts  4.15 us (5%)
  between operations  1.39 us (2%)
    ppermute x10, starting transfers between devices, shifted(): lax.ppermute(value, axis, [(i, (i + step) % count) for i in range(count)])  21.4 us
    all_to_all x1, waiting for transfers between devices, on_device(): lax.all_to_all(message, AXES, 0, 0, tiled=True).reshape(devices * 3, LANES)  16.7 us
    all_to_all x1, blocking collectives, on_device(): lax.all_to_all(snapshot.reshape(8, 16, LANES), 'gz', 0, 0, tiled=True)  9.81 us
    all_to_all x1, starting transfers between devices, on_device(): lax.all_to_all(message, AXES, 0, 0, tiled=True).reshape(devices * 3, LANES)  8.77 us
    pallas_call x1, Pallas kernels, on_device(): pl.pallas_call(first_kernel, in_specs=[SMEM] + [VMEM] * 7, out_specs=[VME...  6.32 us
    pallas_call x1, Pallas kernels, on_device(): pl.pallas_call(second_kernel, in_specs=[SMEM] * 2 + [VMEM] * 8, out_specs...  6.09 us
    unnamed x12, local copies, waits for them, and re-layouts  4.15 us
    pallas_call x1, Pallas kernels, on_device(): pl.pallas_call(final_kernel, in_specs=[SMEM] + [VMEM] * 3, out_specs=[VME...  4.05 us
  transfers between devices with their start and end apart: 11, of which 3 were waited for; matrix products, arithmetic and copies ran while one was open for 0% of the time, Pallas kernels for 5%

profile of v2, /device:TPU:1, one launch (start us, length us, event | category | flops | bytes accessed | tf_op | source)
XLA Modules:
  0.0 89.0 jit_solution(3212208128930044778)
XLA Ops:
  0.6 1.7 %copy-done = f32[5,32,16,256]{3,2,1,0:T(8,128)S(1)} copy-done((f32[5,32,16,256]{3,2,1,0:T(8,128)S(1)}, f32[5,32,16,256]{3,2,1,0:T(8,128)}, u32[]{:S(2)}) %copy-start) | copy-done | bytes 2621464
  2.4 1.3 %shard_map.94 = (f32[5,16,256]{2,1,0:T(8,128)S(1)}, f32[5,16,256]{2,1,0:T(8,128)S(1)}, f32[5,32,256]{2,1,0:T(8,128)S(1)}, f32[5,16,128]{2,1,0:T(8,128)S(1)}, f32[5,16,128]{2,1,0:T(8,128)S(1)}) custom-call(f32[5,32,16,256]{3,2,1,0:T(8,128)S(1)} %copy-done), custom_call_target="tpu_custom_call" | custom-call | tf_op jit(solution)/shard_map/pallas_call | solution.py:443
  3.7 0.0 copy-start.5
  3.7 2.6 %collective-permute-start.2 = (f32[5,32,256]{2,1,0:T(8,128)S(1)}, f32[5,32,256]{2,1,0:T(8,128)S(1)}, u32[]{:S(2)}, u32[]{:S(2)}) collective-permute-start(f32[5,32,256]{2,1,0:T(8,128)S(1)} %get-tuple-element.27), channel_id=1, source_target_pairs={{0,1},{1,0},{2,3},{3,2},{4,5},{5,4},{6,7},{7,6},{8,9},{9,8},{10,11... | collective-permute-start | bytes 491528 | tf_op jit(solution)/shard_map/ppermute | solution.py:413
  6.3 1.2 %collective-permute-start = (f32[5,16,256]{2,1,0:T(8,128)S(1)}, f32[5,16,256]{2,1,0:T(8,128)S(1)}, u32[]{:S(2)}, u32[]{:S(2)}) collective-permute-start(f32[5,16,256]{2,1,0:T(8,128)S(1)} %get-tuple-element.25), channel_id=1, source_target_pairs={{0,16},{16,32},{32,48},{48,64},{64,80},{80,96},{96,112},{112,128},... | collective-permute-start | bytes 245768 | tf_op jit(solution)/shard_map/ppermute | solution.py:413
  7.5 6.1 %collective-permute-start.1 = (f32[5,16,256]{2,1,0:T(8,128)S(1)}, f32[5,16,256]{2,1,0:T(8,128)S(1)}, u32[]{:S(2)}, u32[]{:S(2)}) collective-permute-start(f32[5,16,256]{2,1,0:T(8,128)S(1)} %get-tuple-element.26), channel_id=1, source_target_pairs={{0,240},{16,0},{32,16},{48,32},{64,48},{80,64},{96,80},{112,96},{1... | collective-permute-start | bytes 245768 | tf_op jit(solution)/shard_map/ppermute | solution.py:413
  13.6 2.4 %collective-permute-start.3 = (f32[5,16,128]{2,1,0:T(8,128)S(1)}, f32[5,16,128]{2,1,0:T(8,128)S(1)}, u32[]{:S(2)}, u32[]{:S(2)}) collective-permute-start(f32[5,16,128]{2,1,0:T(8,128)S(1)} %get-tuple-element.28), channel_id=1, source_target_pairs={{0,2},{2,4},{4,6},{6,8},{8,10},{10,12},{12,14},{14,0},{1,3},{3,5},... | collective-permute-start | bytes 122888 | tf_op jit(solution)/shard_map/ppermute | solution.py:413
  16.0 0.0 collective-permute-start.4
  16.0 1.4 %copy-done.2 = f32[64,3,1,4,512]{4,3,2,1,0:T(4,128)S(1)} copy-done((f32[64,3,1,4,512]{4,3,2,1,0:T(4,128)S(1)}, f32[64,3,1,4,512]{4,3,2,1,0:T(4,128)}, u32[]{:S(2)}) %copy-start.2) | copy-done | bytes 1572888
  17.4 1.0 %copy-done.3 = f32[16,3,1,4,512]{4,3,2,1,0:T(4,128)S(1)} copy-done((f32[16,3,1,4,512]{4,3,2,1,0:T(4,128)S(1)}, f32[16,3,1,4,512]{4,3,2,1,0:T(4,128)}, u32[]{:S(2)}) %copy-start.3) | copy-done | bytes 393240
  18.4 4.0 %shard_map.93 = (f32[80,6144]{1,0:T(8,128)S(1)}, f32[48,128]{1,0:T(8,128)S(1)}) custom-call(f32[64,3,1,4,512]{4,3,2,1,0:T(4,128)S(1)} %copy-done.2, f32[16,3,1,4,512]{4,3,2,1,0:T(4,128)S(1)} %copy-done.3), custom_call_target="tpu_custom_call" | custom-call | tf_op jit(solution)/shard_map/pallas_call | solution.py:449
  22.5 0.0 collective-permute-done.3.z_before
  22.5 0.0 collective-permute-done.4.z_after
  22.5 0.0 collective-permute-done.x_before
  22.5 0.0 collective-permute-done.1.x_after
  22.5 6.3 %shard_map.95 = (f32[5,32,16,256]{3,2,1,0:T(8,128)S(1)}, f32[5,16,256]{2,1,0:T(8,128)S(1)}, f32[5,16,256]{2,1,0:T(8,128)S(1)}, f32[5,40,256]{2,1,0:T(8,128)S(1)}...) custom-call(f32[5]{0:T(128)S(1)} %copy-done.4, f32[48,128]{1,0:T(8,128)S(1)} %get-tuple-element.24.folded, ...), custom_call_target="tpu_custom_call" | custom-call | tf_op jit(solution)/shard_map/pallas_call | solution.py:454
  28.9 0.8 collective-permute-start.7
  29.7 0.0 collective-permute-start.5
  29.7 5.7 %collective-permute-start.6 = (f32[5,16,256]{2,1,0:T(8,128)S(1)}, f32[5,16,256]{2,1,0:T(8,128)S(1)}, u32[]{:S(2)}, u32[]{:S(2)}) collective-permute-start(f32[5,16,256]{2,1,0:T(8,128)S(1)} %get-tuple-element.32), channel_id=1, source_target_pairs={{0,240},{16,0},{32,16},{48,32},{64,48},{80,64},{96,80},{112,96},{1... | collective-permute-start | bytes 245768 | tf_op jit(solution)/shard_map/ppermute | solution.py:413
  35.4 2.6 %collective-permute-start.8 = (f32[5,16,128]{2,1,0:T(8,128)S(1)}, f32[5,16,128]{2,1,0:T(8,128)S(1)}, u32[]{:S(2)}, u32[]{:S(2)}) collective-permute-start(f32[5,16,128]{2,1,0:T(8,128)S(1)} %get-tuple-element.34), channel_id=1, source_target_pairs={{0,2},{2,4},{4,6},{6,8},{8,10},{10,12},{12,14},{14,0},{1,3},{3,5},... | collective-permute-start | bytes 122888 | tf_op jit(solution)/shard_map/ppermute | solution.py:413
  37.9 0.0 collective-permute-start.9
  38.0 1.1 %collective-permute-done.8.z_before = f32[5,16,128]{2,1,0:T(8,128)S(1)} collective-permute-done((f32[5,16,128]{2,1,0:T(8,128)S(1)}, f32[5,16,128]{2,1,0:T(8,128)S(1)}, u32[]{:S(2)}, u32[]{:S(2)}) %collective-permute-start.8) | collective-permute-done | bytes 40992 | tf_op jit(solution)/shard_map/ppermute | solution.py:413
  39.0 2.6 %collective-permute-done.9.z_after = f32[5,16,128]{2,1,0:T(8,128)S(1)} collective-permute-done((f32[5,16,128]{2,1,0:T(8,128)S(1)}, f32[5,16,128]{2,1,0:T(8,128)S(1)}, u32[]{:S(2)}, u32[]{:S(2)}) %collective-permute-start.9) | collective-permute-done | bytes 40992 | tf_op jit(solution)/shard_map/ppermute | solution.py:413
  41.7 0.0 collective-permute-done.5.x_before
  41.7 0.0 collective-permute-done.6.x_after
  41.7 0.0 collective-permute-done.7.y_halo
  41.7 6.1 %shard_map.96 = (f32[5,32,16,256]{3,2,1,0:T(8,128)}, f32[128,128]{1,0:T(8,128)S(1)}) custom-call(f32[5]{0:T(128)S(1)} %copy-done.4, s32[3]{0:T(128)S(1)} %copy-done.5, f32[48,128]{1,0:T(8,128)S(1)} %get-tuple-element.24.folded, f32[5,32,16,256]{3,2,1,0:T(8,128)S(1)} %copy-done.1, f32[5,32,16,256]{3,2,1,0:T(8,128)S(1)} %get-tuple-element.30.current, ...), custom_call_target="tpu_custom_call" | custom-call | tf_op jit(solution)/shard_map/pallas_call | solution.py:461
  47.8 9.8 %all_to_all.10.relayed = f32[8,16,128]{2,1,0:T(8,128)S(1)} all-to-all(f32[8,16,128]{2,1,0:T(8,128)S(1)} %bitcast.7), channel_id=1, replica_groups=mesh['gx'=16,'gz'=8,'ga'=2] {'gz'}, dimensions={0} | all-to-all | bytes 131072 | tf_op jit(solution)/shard_map/all_to_all | solution.py:467
  57.6 1.2 %shard_map.97 = (f32[768,128]{1,0:T(8,128)}, f32[8,6144]{1,0:T(8,128)S(1)}) custom-call(f32[8,16,128]{2,1,0:T(8,128)S(1)} %all_to_all.10.relayed, f32[80,6144]{1,0:T(8,128)S(1)} %get-tuple-element.38.joined), custom_call_target="tpu_custom_call" | custom-call | tf_op jit(solution)/shard_map/pallas_call | solution.py:469
  58.8 8.8 %all-to-all-start.1 = ((f32[768,1,128]{2,1,0:T(1,128)}), f32[768,1,128]{2,1,0:T(1,128)S(1)}, u32[]{:S(2)}, u32[]{:S(2)}) async-start(f32[768,1,128]{2,1,0:T(1,128)} %bitcast.2), calls=%async_computation.1 | async-start | bytes 786432 | tf_op jit(solution)/shard_map/all_to_all | solution.py:476
  68.2 16.7 %all-to-all-done.1 = f32[768,1,128]{2,1,0:T(1,128)S(1)} async-done(((f32[768,1,128]{2,1,0:T(1,128)}), f32[768,1,128]{2,1,0:T(1,128)S(1)}, u32[]{:S(2)}, u32[]{:S(2)}) %all-to-all-start.1) | async-done | bytes 393248 | tf_op jit(solution)/shard_map/all_to_all | solution.py:476
  84.9 4.1 %shard_map.98 = (f32[16,64]{1,0:T(8,128)}, f32[16,16]{1,0:T(8,128)}, f32[16,3,1,4,512]{4,3,2,1,0:T(4,128)}) custom-call(s32[1]{0:T(128)S(6)} %copy.11.column_id, f32[768,128]{1,0:T(8,128)S(1)} %bitcast.6, f32[80,6144]{1,0:T(8,128)S(1)} %get-tuple-element.38.joined, f32[8,6144]{1,0:T(8,128)S(1)} %get-tuple-element.40.column), custom_call_target="tpu_custom_call" | custom-call | tf_op jit(solution)/shard_map/pallas_call | solution.py:478
  (9 shorter events, 0.0 us)
Async XLA Ops:
  0.6 1.7 %copy-start = (f32[5,32,16,256]{3,2,1,0:T(8,128)S(1)}, f32[5,32,16,256]{3,2,1,0:T(8,128)}, u32[]{:S(2)}) copy-start(f32[5,32,16,256]{3,2,1,0:T(8,128)} %start.1) | copy-start | bytes 7864324
  2.4 20.1 %copy-start.1 = (f32[5,32,16,256]{3,2,1,0:T(8,128)S(1)}, f32[5,32,16,256]{3,2,1,0:T(8,128)}, u32[]{:S(2)}) copy-start(f32[5,32,16,256]{3,2,1,0:T(8,128)} %start.1) | copy-start | bytes 7864324
  2.4 20.2 %copy-start.4 = (f32[5]{0:T(128)S(1)}, f32[5]{0:T(128)}, u32[]{:S(2)}) copy-start(f32[5]{0:T(128)} %diffusivity.3) | copy-start | bytes 64
  3.7 38.0 %copy-start.5 = (s32[3]{0:T(128)S(1)}, s32[3]{0:T(128)}, u32[]{:S(2)}) copy-start(s32[3]{0:T(128)} %offsets.1) | copy-start | bytes 40
  3.7 18.8 %collective-permute-start.2 = (f32[5,32,256]{2,1,0:T(8,128)S(1)}, f32[5,32,256]{2,1,0:T(8,128)S(1)}, u32[]{:S(2)}, u32[]{:S(2)}) collective-permute-start(f32[5,32,256]{2,1,0:T(8,128)S(1)} %get-tuple-element.27), channel_id=1, source_target_pairs={{0,1},{1,0},{2,3},{3,2},{4,5},{5,4},{6,7},{7,6},{8,9},{9,8},{10,11... | collective-permute-start | bytes 491528 | tf_op jit(solution)/shard_map/ppermute | solution.py:413
  6.3 16.2 %collective-permute-start = (f32[5,16,256]{2,1,0:T(8,128)S(1)}, f32[5,16,256]{2,1,0:T(8,128)S(1)}, u32[]{:S(2)}, u32[]{:S(2)}) collective-permute-start(f32[5,16,256]{2,1,0:T(8,128)S(1)} %get-tuple-element.25), channel_id=1, source_target_pairs={{0,16},{16,32},{32,48},{48,64},{64,80},{80,96},{96,112},{112,128},... | collective-permute-start | bytes 245768 | tf_op jit(solution)/shard_map/ppermute | solution.py:413
  7.5 15.0 %collective-permute-start.1 = (f32[5,16,256]{2,1,0:T(8,128)S(1)}, f32[5,16,256]{2,1,0:T(8,128)S(1)}, u32[]{:S(2)}, u32[]{:S(2)}) collective-permute-start(f32[5,16,256]{2,1,0:T(8,128)S(1)} %get-tuple-element.26), channel_id=1, source_target_pairs={{0,240},{16,0},{32,16},{48,32},{64,48},{80,64},{96,80},{112,96},{1... | collective-permute-start | bytes 245768 | tf_op jit(solution)/shard_map/ppermute | solution.py:413
  13.6 8.9 %collective-permute-start.3 = (f32[5,16,128]{2,1,0:T(8,128)S(1)}, f32[5,16,128]{2,1,0:T(8,128)S(1)}, u32[]{:S(2)}, u32[]{:S(2)}) collective-permute-start(f32[5,16,128]{2,1,0:T(8,128)S(1)} %get-tuple-element.28), channel_id=1, source_target_pairs={{0,2},{2,4},{4,6},{6,8},{8,10},{10,12},{12,14},{14,0},{1,3},{3,5},... | collective-permute-start | bytes 122888 | tf_op jit(solution)/shard_map/ppermute | solution.py:413
  16.0 6.4 %collective-permute-start.4 = (f32[5,16,128]{2,1,0:T(8,128)S(1)}, f32[5,16,128]{2,1,0:T(8,128)S(1)}, u32[]{:S(2)}, u32[]{:S(2)}) collective-permute-start(f32[5,16,128]{2,1,0:T(8,128)S(1)} %get-tuple-element.29), channel_id=1, source_target_pairs={{0,14},{2,0},{4,2},{6,4},{8,6},{10,8},{12,10},{14,12},{1,15},{3,1}... | collective-permute-start | bytes 122888 | tf_op jit(solution)/shard_map/ppermute | solution.py:413
  16.0 1.4 %copy-start.2 = (f32[64,3,1,4,512]{4,3,2,1,0:T(4,128)S(1)}, f32[64,3,1,4,512]{4,3,2,1,0:T(4,128)}, u32[]{:S(2)}) copy-start(f32[64,3,1,4,512]{4,3,2,1,0:T(4,128)} %basis.1) | copy-start | bytes 4718596
  17.4 1.0 %copy-start.3 = (f32[16,3,1,4,512]{4,3,2,1,0:T(4,128)S(1)}, f32[16,3,1,4,512]{4,3,2,1,0:T(4,128)}, u32[]{:S(2)}) copy-start(f32[16,3,1,4,512]{4,3,2,1,0:T(4,128)} %held.1) | copy-start | bytes 1179652
  28.9 12.8 %collective-permute-start.7 = (f32[5,40,256]{2,1,0:T(8,128)S(1)}, f32[5,40,256]{2,1,0:T(8,128)S(1)}, u32[]{:S(2)}, u32[]{:S(2)}) collective-permute-start(f32[5,40,256]{2,1,0:T(8,128)S(1)} %get-tuple-element.33), channel_id=1, source_target_pairs={{0,1},{1,0},{2,3},{3,2},{4,5},{5,4},{6,7},{7,6},{8,9},{9,8},{10,11... | collective-permute-start | bytes 614408 | tf_op jit(solution)/shard_map/ppermute | solution.py:413
  29.7 12.0 %collective-permute-start.5 = (f32[5,16,256]{2,1,0:T(8,128)S(1)}, f32[5,16,256]{2,1,0:T(8,128)S(1)}, u32[]{:S(2)}, u32[]{:S(2)}) collective-permute-start(f32[5,16,256]{2,1,0:T(8,128)S(1)} %get-tuple-element.31), channel_id=1, source_target_pairs={{0,16},{16,32},{32,48},{48,64},{64,80},{80,96},{96,112},{112,128},... | collective-permute-start | bytes 245768 | tf_op jit(solution)/shard_map/ppermute | solution.py:413
  29.7 12.0 %collective-permute-start.6 = (f32[5,16,256]{2,1,0:T(8,128)S(1)}, f32[5,16,256]{2,1,0:T(8,128)S(1)}, u32[]{:S(2)}, u32[]{:S(2)}) collective-permute-start(f32[5,16,256]{2,1,0:T(8,128)S(1)} %get-tuple-element.32), channel_id=1, source_target_pairs={{0,240},{16,0},{32,16},{48,32},{64,48},{80,64},{96,80},{112,96},{1... | collective-permute-start | bytes 245768 | tf_op jit(solution)/shard_map/ppermute | solution.py:413
  35.4 3.7 %collective-permute-start.8 = (f32[5,16,128]{2,1,0:T(8,128)S(1)}, f32[5,16,128]{2,1,0:T(8,128)S(1)}, u32[]{:S(2)}, u32[]{:S(2)}) collective-permute-start(f32[5,16,128]{2,1,0:T(8,128)S(1)} %get-tuple-element.34), channel_id=1, source_target_pairs={{0,2},{2,4},{4,6},{6,8},{8,10},{10,12},{12,14},{14,0},{1,3},{3,5},... | collective-permute-start | bytes 122888 | tf_op jit(solution)/shard_map/ppermute | solution.py:413
  37.9 3.7 %collective-permute-start.9 = (f32[5,16,128]{2,1,0:T(8,128)S(1)}, f32[5,16,128]{2,1,0:T(8,128)S(1)}, u32[]{:S(2)}, u32[]{:S(2)}) collective-permute-start(f32[5,16,128]{2,1,0:T(8,128)S(1)} %get-tuple-element.35), channel_id=1, source_target_pairs={{0,14},{2,0},{4,2},{6,4},{8,6},{10,8},{12,10},{14,12},{1,15},{3,1}... | collective-permute-start | bytes 122888 | tf_op jit(solution)/shard_map/ppermute | solution.py:413
  58.8 26.2 %all-to-all-start.1 = ((f32[768,1,128]{2,1,0:T(1,128)}), f32[768,1,128]{2,1,0:T(1,128)S(1)}, u32[]{:S(2)}, u32[]{:S(2)}) async-start(f32[768,1,128]{2,1,0:T(1,128)} %bitcast.2), calls=%async_computation.1 | async-start | bytes 786432 | tf_op jit(solution)/shard_map/all_to_all | solution.py:476

commit v3 on v2

v3 whole, which is shorter than its diff:
```python
import functools

import jax
import jax.numpy as jnp
from jax import lax
from jax.experimental import pallas as pl
from jax.experimental.pallas import tpu as pltpu
from jax.sharding import PartitionSpec as P

STRIDE = 4
LANES = 128
PACK_UNROLL = 4
BLOCK = 3

time_step = 0.1
smagorinsky = 0.02

VMEM = pl.BlockSpec(memory_space=pltpu.VMEM)
ANY = pl.BlockSpec(memory_space=pl.ANY)
SMEM = pl.BlockSpec(memory_space=pltpu.SMEM)
HIGH = lax.Precision.HIGHEST
AXES = ("zh", "x", "y", "core", "zl")


def params(mib):
    return pltpu.CompilerParams(vmem_limit_bytes=mib * 1024 * 1024)


def struct(*shape):
    return jax.ShapeDtypeStruct(shape, jnp.float32)


def iota(shape, dim):
    return lax.broadcasted_iota(jnp.int32, shape, dim)


def dot(left, right, left_dim, right_dim):
    return lax.dot_general(
        left,
        right,
        (((left_dim,), (right_dim,)), ((), ())),
        precision=HIGH,
        preferred_element_type=jnp.float32,
    )


def put_row(x, upper, top, bottom, ref, field, half):
    row = jnp.where(upper, bottom[0:1, :], top[7:8, :])
    rows = pl.ds(pl.multiple_of(x // 8 * 8, 8), 8)
    lanes = slice(half * LANES, (half + 1) * LANES)
    here = iota((8, LANES), 0) == x % 8
    ref[field, rows, lanes] = jnp.where(here, row, ref[field, rows, lanes])


def put_columns(x, lane, value, ref, field, tile, from_end):
    shift = (x + 1) % LANES if from_end else x
    rows = slice(tile * 8, tile * 8 + 8)
    ref[field, rows, :] = jnp.where(lane == x, pltpu.roll(value, shift, 1), ref[field, rows, :])


def split(value):
    high = value.astype(jnp.bfloat16)
    value = value - high.astype(jnp.float32)
    middle = value.astype(jnp.bfloat16)
    return high, middle, (value - middle.astype(jnp.float32)).astype(jnp.bfloat16)


def matmul(left, right, right_dim):
    return lax.dot_general(
        left, right, (((1,), (right_dim,)), ((), ())), preferred_element_type=jnp.float32
    )


def pack_kernel(source, x_low, x_high, y_row, z_low, z_high, fields, semaphores):
    count, cells, height, _ = fields.shape
    upper = lax.axis_index("zl") > 0
    lane = iota((8, LANES), 1)
    parts = semaphores.shape[0]
    each = cells // parts
    copies = [
        pltpu.make_async_copy(
            source.at[:, part * each : (part + 1) * each],
            fields.at[:, part * each : (part + 1) * each],
            semaphores.at[part],
        )
        for part in range(parts)
    ]
    for copy in copies:
        copy.start()
    y_row[...] = jnp.zeros_like(y_row)
    z_low[...] = jnp.zeros_like(z_low)
    z_high[...] = jnp.zeros_like(z_high)

    def body(x, carry):
        for f in range(count):
            for half in range(2):
                lanes = slice(half * LANES, (half + 1) * LANES)
                bottom = fields[f, x, 0:8, lanes]
                top = fields[f, x, height - 8 : height, lanes]
                put_row(x, upper, top, bottom, y_row, f, half)
                for tile, value in ((0, bottom), (1, top)):
                    put_columns(x, lane, value, (z_low, z_high)[half], f, tile, half == 1)
        return carry

    for part in range(parts):
        copies[part].wait()
        lax.fori_loop(part * each, (part + 1) * each, body, 0, unroll=PACK_UNROLL)
    x_low[...] = fields[:, 0]
    x_high[...] = fields[:, cells - 1]


def half_plane(x, half, current, before, after, y_halo, z_before, z_after, diffusivity, upper):
    count = current.shape[0]
    lane = iota((8, LANES), 1)
    sub = iota((8, LANES), 0)
    first_lane, last_lane = lane == 0, lane == LANES - 1
    first_sub, last_sub = sub == 0, sub == 7
    below = jnp.where(upper, 1.0, 0.0)
    above = 1.0 - below
    row_shift = (jnp.where(upper, 8, 15) - x % 8) % 8
    tile_rows = (slice(0, 8), slice(8, 16))
    lanes = slice(half * LANES, (half + 1) * LANES)
    other_lanes = slice((1 - half) * LANES, (2 - half) * LANES)
    centre = {
        (f, tile): current[f, x, tile_rows[tile], lanes] for f in range(count) for tile in range(2)
    }
    speeds = [[0.5 * centre[f, tile] for f in range(3)] for tile in range(2)]
    strain = [0.0, 0.0]
    laplace, rest = {}, {}
    for f in range(count):
        row = y_halo[f, pl.ds(pl.multiple_of(x // 8 * 8, 8), 8), lanes]
        row = pltpu.roll(row, row_shift, 0)
        down = [pltpu.roll(centre[f, tile], 1, 0) for tile in range(2)]
        up = [pltpu.roll(centre[f, tile], 7, 0) for tile in range(2)]
        y_minus = (
            jnp.where(first_sub, row * below, down[0]),
            jnp.where(first_sub, down[0], down[1]),
        )
        y_plus = (
            jnp.where(last_sub, up[1], up[0]),
            jnp.where(last_sub, row * above, up[1]),
        )
        for tile in range(2):
            rows = tile_rows[tile]
            value = centre[f, tile]
            other = current[f, x, rows, other_lanes]
            if half == 0:
                edge_low = pltpu.roll(z_before[f, rows, :], (LANES - x) % LANES, 1)
                edge_high = pltpu.roll(other, LANES - 1, 1)
            else:
                edge_low = pltpu.roll(other, 1, 1)
                edge_high = pltpu.roll(z_after[f, rows, :], LANES - 1 - x, 1)
            z_minus = jnp.where(first_lane, edge_low, pltpu.roll(value, 1, 1))
            z_plus = jnp.where(last_lane, edge_high, pltpu.roll(value, LANES - 1, 1))
            x_minus, x_plus = before(f, rows, lanes), after(f, rows, lanes)
            slope_x = x_plus - x_minus
            slope_y = y_plus[tile] - y_minus[tile]
            slope_z = z_plus - z_minus
            laplace[f, tile] = (
                (x_plus + x_minus)
                + (y_plus[tile] + y_minus[tile])
                + (z_plus + z_minus)
                - 6.0 * value
            )
            if f < 3:
                strain[tile] = strain[tile] + (
                    slope_x * slope_x + slope_y * slope_y + slope_z * slope_z
                )
            advect = (
                speeds[tile][0] * slope_x + speeds[tile][1] * slope_y + speeds[tile][2] * slope_z
            )
            rest[f, tile] = diffusivity[f] * laplace[f, tile] - advect
    rates = {}
    for tile in range(2):
        eddy = smagorinsky * jnp.sqrt(0.25 * strain[tile])
        for f in range(count):
            rates[f, tile] = eddy * laplace[f, tile] + rest[f, tile]
    return centre, rates


def planes(current, halos, diffusivity, finish, after_three, after_first=lambda: None):
    x_before, x_after, y_halo, z_before, z_after = halos
    cells = current.shape[1]
    upper = lax.axis_index("zl") > 0

    def one(x, before, after):
        for half in range(2):
            finish(
                x,
                half,
                *half_plane(
                    x, half, current, before, after, y_halo, z_before, z_after, diffusivity, upper
                ),
            )

    def inside(offset, x):
        return lambda f, rows, lanes: current[f, x + offset, rows, lanes]

    def outside(ref):
        return lambda f, rows, lanes: ref[f, rows, lanes]

    one(0, outside(x_before), inside(1, 0))
    after_first()
    blocks = (cells - 2) // BLOCK

    def body(step, carry):
        for i in range(BLOCK):
            x = step * BLOCK + 1 + i
            one(x, inside(-1, x), inside(1, x))
        after_three(step)
        return carry

    lax.fori_loop(0, blocks, body, 0)
    one(cells - 1, inside(-1, cells - 1), outside(x_after))


def first_kernel(
    diffusivity, basis, held, current, x_before, x_after, y_halo, z_before, z_after,
    first, x_low, x_high, y_row, z_low, z_high, joined, folded, sums, squares, semaphores,
):
    count, cells = current.shape[:2]
    rank, _, _, levels, points = basis.shape
    total = rank + held.shape[0]
    upper = lax.axis_index("zl") > 0
    lane = iota((8, LANES), 1)
    copies = []
    for chunk in range(3 * levels):
        lanes = slice(chunk * points, (chunk + 1) * points)
        for i, (source, rows) in enumerate(
            ((basis, slice(0, rank)), (held, slice(rank, total)))
        ):
            copies.append(
                pltpu.make_async_copy(
                    source.at[:, chunk // levels, 0, chunk % levels, :],
                    joined.at[rows, lanes],
                    semaphores.at[2 * chunk + i],
                )
            )
    for copy in copies:
        copy.start()
    y_row[...] = jnp.zeros_like(y_row)
    z_low[...] = jnp.zeros_like(z_low)
    z_high[...] = jnp.zeros_like(z_high)
    sums[...] = jnp.zeros_like(sums)
    squares[...] = jnp.zeros_like(squares)

    def finish(x, half, centre, rates):
        lanes = slice(half * LANES, (half + 1) * LANES)
        for f in range(count):
            new = []
            for tile in range(2):
                rows = slice(tile * 8, tile * 8 + 8)
                value = centre[f, tile] + time_step * rates[f, tile]
                new.append(value)
                first[f, x, rows, lanes] = value
                if isinstance(x, int):
                    (x_low if x == 0 else x_high)[f, rows, lanes] = value
                put_columns(x, lane, value, (z_low, z_high)[half], f, tile, half == 1)
            put_row(x, upper, new[1], new[0], y_row, f, half)

    def gram(chunk):
        part = joined[:, pl.ds(pl.multiple_of(chunk * points, LANES), points)]
        high, middle, low = split(part)
        sums[...] += matmul(jnp.concatenate([high, middle, low], axis=0), high, 1)
        squares[...] += matmul(middle, middle, 1)

    def arrived():
        for copy in copies:
            copy.wait()

    halos = (x_before, x_after, y_halo, z_before, z_after)
    planes(current, halos, diffusivity, finish, gram, arrived)
    for chunk in range((cells - 2) // BLOCK, 3 * levels):
        gram(chunk)
    half = total // 2
    wide = jnp.zeros((total, LANES - total), jnp.float32)
    cross = jnp.concatenate([sums[total : 2 * total] + sums[2 * total :], wide], axis=1)
    tall = jnp.concatenate([cross, jnp.zeros((LANES - total, LANES), jnp.float32)], axis=0)
    values = jnp.concatenate([sums[:total] + squares[...], wide], axis=1)
    values = values + (cross + tall.T[:total])
    lane, sub = iota((half, LANES), 1), iota((half, LANES), 0)
    lower = pltpu.roll(values[half:], LANES - half, 1)
    diagonal = jnp.sum(jnp.where(lane == sub, lower, 0.0), axis=1, keepdims=True)
    values = jnp.where(lane < sub, lower, values[:half])
    values = jnp.where(lane == total, jnp.broadcast_to(diagonal, (half, LANES)), values)
    folded[0:half, :] = jnp.where(lane <= total, values, 0.0)
    folded[half:, :] = jnp.zeros((folded.shape[0] - half, LANES), jnp.float32)
    for group in range(3):
        lanes = slice(group % 2 * LANES, (group % 2 + 1) * LANES)
        y_row[group // 2, cells:, lanes] = jnp.where(
            upper, folded[group * 8 : group * 8 + 8], folded[group * 8 + 24 : group * 8 + 32]
        )


def second_kernel(
    diffusivity, offsets, folded, start, current, x_before, x_after, y_halo, z_before, z_after,
    target, snapshot, picked, result, semaphores,
):
    count, cells, height, width = current.shape
    blocks = (cells - 2) // BLOCK

    def finish(x, half, centre, rates):
        lanes = slice(half * LANES, (half + 1) * LANES)
        for f in range(count):
            for tile in range(2):
                rows = slice(tile * 8, tile * 8 + 8)
                result[f, x, rows, lanes] = 0.5 * (
                    start[f, x, rows, lanes] + centre[f, tile] + time_step * rates[f, tile]
                )

    def copied(first, planes_count, index):
        part = pl.ds(first, planes_count)
        return pltpu.make_async_copy(result.at[:, part], target.at[:, part], semaphores.at[index])

    def send(step):
        copied(step * BLOCK + 1, BLOCK, step).start()

    planes(current, (x_before, x_after, y_halo, z_before, z_after), diffusivity, finish, send)
    copied(0, 1, blocks).start()
    copied(cells - 1, 1, blocks + 1).start()
    levels = height // STRIDE
    picked[...] = jnp.zeros_like(picked)
    for column in range(cells // STRIDE):
        for f in range(3):
            for tile in range(2):
                plane = result[f, column * STRIDE + offsets[2], tile * 8 : tile * 8 + 8, :]
                plane = pltpu.roll(plane, (8 - offsets[1]) % 8, 0)
                for part in range(2):
                    row = column * 16 + f * levels + tile * 2 + part
                    picked[row : row + 1, :] = plane[part * STRIDE : part * STRIDE + 1, :]
    points = width // STRIDE
    choose = iota((width, LANES), 0) == STRIDE * (iota((width, LANES), 1) % points) + offsets[0]
    snapshot[...] = dot(picked[...], choose.astype(jnp.float32), 1, 0)
    upper = lax.axis_index("zl") > 0
    for group in range(3):
        lanes = slice(group % 2 * LANES, (group % 2 + 1) * LANES)
        kept = jnp.where(
            upper, folded[group * 8 + 24 : group * 8 + 32], folded[group * 8 : group * 8 + 8]
        )
        kept = kept + y_halo[group // 2, cells:, lanes]
        for column in range(cells // STRIDE):
            row = column * 16 + 12 + group
            snapshot[row : row + 1, :] = kept[column : column + 1]

    def settle(step, carry):
        copied(step * BLOCK + 1, BLOCK, step).wait()
        return carry

    lax.fori_loop(0, blocks, settle, 0)
    copied(0, 1, blocks).wait()
    copied(cells - 1, 1, blocks + 1).wait()


def product_kernel(relayed, joined, message, column, partial):
    total = joined.shape[0]
    groups = total // 8
    low = iota((1, LANES), 1) < LANES // 2
    sums = [jnp.zeros((8, LANES), jnp.float32) for _ in range(groups + 1)]
    for row in range(12):
        for pair in range(4):
            tile = row * 4 + pair
            lanes = slice(tile * LANES, (tile + 1) * LANES)
            values = jnp.where(
                low,
                relayed[2 * pair, row : row + 1, :],
                relayed[2 * pair + 1, row : row + 1, :],
            )
            values = jnp.broadcast_to(values, (8, LANES))
            column[:, lanes] = values
            for group in range(groups):
                sums[group] += joined[group * 8 : group * 8 + 8, lanes] * values
            sums[groups] += values * values
    partial[...] = jnp.zeros_like(partial)
    for group in range(groups + 1):
        partial[group * 8 : group * 8 + 8, :] = sums[group]
    products = dot(jnp.ones((8, LANES), jnp.float32), partial[...], 1, 1)
    own = jnp.sum(relayed[:, 8:16, :], axis=0)
    lane, which = iota((24, LANES), 1), iota((24, LANES), 0) % 3
    values = jnp.zeros((24, LANES), jnp.float32)
    for piece in range(3):
        moved = pltpu.roll(products, 88 - 40 * piece if piece < 2 else 8, 1)[0:1]
        row = jnp.where(lane[0:1] < 88, own[4 + piece : 5 + piece], moved)
        values = jnp.where(which == piece, row, values)
    message[...] = values


def middle_kernel(received, message):
    rows = sum(received[6 * part : 6 * part + 6, :] for part in range(4))
    tile = jnp.concatenate([rows] * 4, axis=0)
    count = message.shape[0]
    message[...] = jnp.broadcast_to(tile[None], (count // 24, 24, LANES)).reshape(count, LANES)


def final_kernel(
    rows_total, column_id, gathered, joined, column,
    coefficients, r_factor, columns_out, stacked, results, semaphores,
):
    total = joined.shape[0]
    count, rank = coefficients.shape
    _, _, _, levels, points = columns_out.shape
    chosen = column_id[0]
    half = total // 2
    stacked[...] = jnp.sum(gathered[...].reshape(-1, 48, LANES), axis=0)
    pieces = [
        [stacked[pl.ds(part * 3 + piece, 8, stride=6), :] for piece in range(3)]
        for part in range(2)
    ]
    sums = [jnp.sum(pieces[0][i] + pieces[1][i], axis=0, keepdims=True) for i in range(3)]
    sums = [pltpu.roll(row, shift, 1) for row, shift in zip(sums, (40, 80, 120))]
    lane = iota((1, LANES), 1)
    sums = jnp.where(lane < 40, sums[0], jnp.where(lane < 80, sums[1], sums[2])) / rows_total
    folded = jnp.concatenate(pieces[0] + pieces[1][:2], axis=0) / rows_total
    turned = jnp.concatenate([folded, jnp.zeros((LANES - half, LANES), jnp.float32)], axis=0).T
    lane, sub = iota((half, LANES), 1), iota((half, LANES), 0)
    diagonal = jnp.broadcast_to(folded[:, total : total + 1], (half, LANES))
    upper = jnp.where((lane >= sub), folded, turned[:half])
    lower = jnp.where(lane < sub, folded, jnp.where(lane > sub, turned[:half], diagonal))
    gram = jnp.concatenate(
        [
            upper,
            jnp.where(lane < half, turned[half:total], pltpu.roll(lower, half, 1)),
        ],
        axis=0,
    )
    lane = iota((total, LANES), 1)
    down = jnp.broadcast_to(sums, (LANES, LANES)).T
    modes = gram[:rank, :rank]
    shifted = pltpu.roll(gram, LANES - rank, 1)
    first = jnp.where(lane[:rank] == chosen, down[:rank], shifted[:rank])[:, :count]
    block_lane, block_sub = iota((count, LANES), 1), iota((count, LANES), 0)
    square = jnp.broadcast_to(sums[:, total : total + 1], (1, LANES))
    across = jnp.where(
        block_lane[0:1] == chosen, square, pltpu.roll(sums, LANES - rank, 1)
    )
    block = jnp.where(block_lane == chosen, down[rank:total], shifted[rank:total])
    block = jnp.where(block_sub == chosen, jnp.broadcast_to(across, (count, LANES)), block)
    second = first - dot(modes, first, 1, 0)
    both = first + second
    third = first - dot(modes, both, 1, 0)
    square = dot(
        jnp.concatenate([first, both], axis=0), jnp.concatenate([both, third], axis=0), 0, 0
    )
    square = jnp.concatenate([square, jnp.zeros((count, LANES - count), jnp.float32)], axis=1)
    state = jnp.where(block_lane < count, block - square, 0.0)
    state = jnp.where(block_lane == block_sub + count, 1.0, state)
    for step in range(count - 1):
        row = state[step : step + 1, :]
        scale = state[:, step : step + 1] / row[:, step : step + 1]
        scale = jnp.where(block_sub > step, jnp.broadcast_to(scale, (count, LANES)), 0.0)
        state = state - scale * row
    diagonal = jnp.sum(jnp.where(block_lane == block_sub, state, 0.0), axis=1, keepdims=True)
    state = state / jnp.sqrt(diagonal)
    r_factor[...] = jnp.where(block_lane >= block_sub, state, 0.0)[:, :count]
    padded = jnp.concatenate([both, jnp.zeros((rank, LANES - count), jnp.float32)], axis=1)
    padded = jnp.concatenate([padded, jnp.zeros((LANES - rank, LANES), jnp.float32)], axis=0)
    coefficients[...] = padded.T[:count, :rank]
    inverse = pltpu.roll(state, LANES - count, 1)
    inverse = jnp.where(block_lane < count, inverse, 0.0)
    onto_modes = dot(inverse[:, :count], both, 1, 1)
    own = jnp.sum(jnp.where(block_lane == chosen, inverse, 0.0), axis=1, keepdims=True)
    onto_block = pltpu.roll(jnp.where(block_lane == chosen, 0.0, inverse), rank, 1)
    onto_modes = jnp.concatenate(
        [-onto_modes, jnp.zeros((count, LANES - rank), jnp.float32)], axis=1
    )
    weights = jnp.where(block_lane < rank, onto_modes, onto_block)[:, :total]
    weights = jnp.concatenate(split(weights), axis=0)
    copies = []
    for chunk in range(3 * levels):
        lanes = slice(chunk * points, (chunk + 1) * points)
        high, middle, low = split(joined[:, lanes])
        first = matmul(weights, high, 0)
        second = matmul(weights[: 2 * count], middle, 0)
        third = matmul(weights[:count], low, 0)
        results[chunk] = (
            (first[:count] + own * column[0:1, lanes])
            + (first[count : 2 * count] + second[:count])
            + (first[2 * count :] + second[count:] + third)
        )
        copies.append(
            pltpu.make_async_copy(
                results.at[chunk],
                columns_out.at[:, chunk // levels, 0, chunk % levels, :],
                semaphores.at[chunk],
            )
        )
        copies[-1].start()
    for copy in copies:
        copy.wait()


def shifted(value, axes, step):
    axes = axes if isinstance(axes, tuple) else (axes,)
    count = 1
    for axis in axes:
        count *= lax.axis_size(axis)
    return lax.ppermute(value, axes, [(i, (i + step) % count) for i in range(count)])


def exchange(faces):
    x_low, x_high, y_row, z_low, z_high = faces
    return (
        shifted(x_high, ("zh", "x"), 1),
        shifted(x_low, ("zh", "x"), -1),
        shifted(y_row, "zl", 1),
        shifted(z_high, ("y", "core"), 1),
        shifted(z_low, ("y", "core"), -1),
    )


def everyone(message, axes):
    rows = message.shape[0]
    message = lax.all_to_all(message.reshape(rows, 1, LANES), axes, 0, 0, tiled=True)
    return message.reshape(rows, LANES)


def on_device(fields, diffusivity, subsample_offsets, column_id, pod_basis, held_block):
    count, cells, height, width = fields.shape
    rank, columns = pod_basis.shape[0], held_block.shape[0]
    devices = 1
    for axis in AXES:
        devices *= lax.axis_size(axis)
    points = held_block.shape[-1]
    chunks = 3 * held_block.shape[3]
    length = chunks * points
    total = rank + columns
    faces = (
        struct(count, height, width),
        struct(count, height, width),
        struct(count, cells, width),
        struct(count, height, LANES),
        struct(count, height, LANES),
    )
    block_space = pltpu.VMEM(fields.shape, jnp.float32)

    packed = pl.pallas_call(
        pack_kernel, in_specs=[ANY], out_specs=[VMEM] * 5, out_shape=faces,
        scratch_shapes=[block_space, pltpu.SemaphoreType.DMA((4,))],
        compiler_params=params(16),
    )(fields)
    halos = exchange(packed)

    first, *packed, joined, folded = pl.pallas_call(
        first_kernel, in_specs=[SMEM] + [ANY] * 2 + [VMEM] * 6, out_specs=[VMEM] * 8,
        out_shape=(struct(*fields.shape),) + faces[:2] + (struct(count, cells + 8, width),)
        + faces[3:] + (struct(total, length), struct(48, LANES)),
        scratch_shapes=[
            pltpu.VMEM((3 * total, total), jnp.float32),
            pltpu.VMEM((total, total), jnp.float32),
            pltpu.SemaphoreType.DMA((2 * chunks,)),
        ],
        compiler_params=params(24),
    )(diffusivity, pod_basis, held_block, fields, *halos)
    halos = exchange(packed)

    fields_out, snapshot = pl.pallas_call(
        second_kernel, in_specs=[SMEM] * 2 + [VMEM] * 8, out_specs=[ANY, VMEM],
        out_shape=(struct(*fields.shape), struct(LANES, LANES)),
        scratch_shapes=[
            pltpu.VMEM((LANES, width), jnp.float32), block_space, pltpu.SemaphoreType.DMA((12,)),
        ],
        compiler_params=params(24),
    )(diffusivity, subsample_offsets, folded, fields, first, *halos)
    relayed = lax.all_to_all(snapshot.reshape(8, 16, LANES), ("y", "core"), 0, 0, tiled=True)

    message, column = pl.pallas_call(
        product_kernel, in_specs=[VMEM] * 2, out_specs=[VMEM] * 2,
        out_shape=(struct(24, LANES), struct(8, length)),
        scratch_shapes=[pltpu.VMEM((LANES, LANES), jnp.float32)],
        compiler_params=params(16),
    )(relayed, joined)
    message = pl.pallas_call(
        middle_kernel, in_specs=[VMEM], out_specs=VMEM, out_shape=struct(192, LANES),
        compiler_params=params(4),
    )(everyone(message, ("zh", "zl")))
    gathered = everyone(message, ("x", "y", "core"))

    coefficients, r_factor, new_columns = pl.pallas_call(
        functools.partial(final_kernel, float(devices * length)),
        in_specs=[SMEM] + [VMEM] * 3, out_specs=[VMEM] * 2 + [ANY],
        out_shape=(
            struct(columns, rank), struct(columns, columns), struct(*held_block.shape)
        ),
        scratch_shapes=[
            pltpu.VMEM((48, LANES), jnp.float32),
            pltpu.VMEM((chunks, columns, points), jnp.float32),
            pltpu.SemaphoreType.DMA((chunks,)),
        ],
        compiler_params=params(24),
    )(column_id, gathered, joined, column)
    return fields_out, coefficients.T, r_factor, new_columns


def solution(mesh):
    mesh = jax.sharding.Mesh(mesh.devices.reshape(4, 4, 4, 2, 2), AXES)
    block = P(None, ("zh", "x"), "zl", ("y", "core"))
    rows = P(None, None, ("zh", "x", "y", "core"), "zl", None)
    return jax.shard_map(
        on_device,
        mesh=mesh,
        in_specs=(block, P(), P(), P(), rows, rows),
        out_specs=(block, P(), P(), rows),
        check_vma=False,
    )
```

time: 89.3 us -> 92 us (1.030)
  blocking collectives: 9.81 us -> 20 us
  waiting for transfers between devices: 20.4 us -> 14.6 us
  starting transfers between devices: 30.2 us -> 27.9 us
    all_to_all x1 -> x2, blocking collectives: 9.81 us -> 20 us  [the longest x1 11.1 us: everyone(): lax.all_to_all(message.reshape(rows, 1, LANES), axes, 0, 0, tiled=True)]
    all_to_all x1, waiting for transfers between devices: 16.7 us -> 6.81 us  [everyone(): lax.all_to_all(message.reshape(rows, 1, LANES), axes, 0, 0, tiled=True)]
    ppermute x10, waiting for transfers between devices: 3.71 us -> 7.83 us  [shifted(): lax.ppermute(value, axes, [(i, (i + step) % count) for i in range(count)])]
    all_to_all x1, starting transfers between devices: 8.77 us -> 6.16 us  [everyone(): lax.all_to_all(message.reshape(rows, 1, LANES), axes, 0, 0, tiled=True)]
    pallas_call x4, Pallas kernels: 15.7 us -> 17.8 us  [the longest x1 9.98 us: on_device(): pl.pallas_call(first_kernel, in_specs=[SMEM] + [ANY] * 2 + [VMEM] * 6, ou...]
  transfers between devices with their start and end apart: 11 -> 11, of which waited for: 3 -> 6; matrix products, arithmetic and copies ran while one was open for 0% -> 0% of each run, Pallas kernels for 5% -> 0%
where the time goes in v3:
time: 92 us; the launch traced here: 91.7 us
  starting transfers between devices  27.9 us (30%)
  Pallas kernels  23.7 us (26%)
  blocking collectives  20 us (22%)
  waiting for transfers between devices  14.6 us (16%)
  local copies, waits for them, and re-layouts  4.15 us (5%)
  between operations  1.39 us (2%)
    ppermute x10, starting transfers between devices, shifted(): lax.ppermute(value, axes, [(i, (i + step) % count) for i in range(count)])  21.7 us
    all_to_all x1, blocking collectives, everyone(): lax.all_to_all(message.reshape(rows, 1, LANES), axes, 0, 0, tiled=True)  11.1 us
    pallas_call x1, Pallas kernels, on_device(): pl.pallas_call(first_kernel, in_specs=[SMEM] + [ANY] * 2 + [VMEM] * 6, ou...  9.98 us
    all_to_all x1, blocking collectives, on_device(): lax.all_to_all(snapshot.reshape(8, 16, LANES), ('y', 'core'), 0, 0, tiled...  8.93 us
    ppermute x10, waiting for transfers between devices, shifted(): lax.ppermute(value, axes, [(i, (i + step) % count) for i in range(count)])  7.83 us
    all_to_all x1, waiting for transfers between devices, everyone(): lax.all_to_all(message.reshape(rows, 1, LANES), axes, 0, 0, tiled=True)  6.81 us
    all_to_all x1, starting transfers between devices, everyone(): lax.all_to_all(message.reshape(rows, 1, LANES), axes, 0, 0, tiled=True)  6.16 us
    pallas_call x1, Pallas kernels, on_device(): pl.pallas_call(functools.partial(final_kernel, float(devices * length)),...  5.69 us
  transfers between devices with their start and end apart: 11, of which 6 were waited for; matrix products, arithmetic and copies ran while one was open for 0% of the time, Pallas kernels for 0%

profile of v3, /device:TPU:1, one launch (start us, length us, event | category | flops | bytes accessed | tf_op | source)
XLA Modules:
  0.0 91.7 jit_solution(16805181036769023936)
XLA Ops:
  0.6 1.7 %copy-done = f32[5,32,16,256]{3,2,1,0:T(8,128)S(1)} copy-done((f32[5,32,16,256]{3,2,1,0:T(8,128)S(1)}, f32[5,32,16,256]{3,2,1,0:T(8,128)}, u32[]{:S(2)}) %copy-start) | copy-done | bytes 2621464
  2.4 1.5 %shard_map.93 = (f32[5,16,256]{2,1,0:T(8,128)S(1)}, f32[5,16,256]{2,1,0:T(8,128)S(1)}, f32[5,32,256]{2,1,0:T(8,128)S(1)}, f32[5,16,128]{2,1,0:T(8,128)S(1)}, f32[5,16,128]{2,1,0:T(8,128)S(1)}) custom-call(f32[5,32,16,256]{3,2,1,0:T(8,128)S(1)} %copy-done), custom_call_target="tpu_custom_call" | custom-call | tf_op jit(solution)/shard_map/pallas_call | solution.py:535
  3.9 0.0 copy-start.5
  3.9 2.6 %collective-permute-start.2 = (f32[5,32,256]{2,1,0:T(8,128)S(1)}, f32[5,32,256]{2,1,0:T(8,128)S(1)}, u32[]{:S(2)}, u32[]{:S(2)}) collective-permute-start(f32[5,32,256]{2,1,0:T(8,128)S(1)} %get-tuple-element.26), channel_id=1, source_target_pairs={{0,1},{1,0},{2,3},{3,2},{4,5},{5,4},{6,7},{7,6},{8,9},{9,8},{10,11... | collective-permute-start | bytes 491528 | tf_op jit(solution)/shard_map/ppermute | solution.py:496
  6.5 1.2 %collective-permute-start = (f32[5,16,256]{2,1,0:T(8,128)S(1)}, f32[5,16,256]{2,1,0:T(8,128)S(1)}, u32[]{:S(2)}, u32[]{:S(2)}) collective-permute-start(f32[5,16,256]{2,1,0:T(8,128)S(1)} %get-tuple-element.24), channel_id=1, source_target_pairs={{0,16},{16,32},{32,48},{48,64},{64,80},{80,96},{96,112},{112,128},... | collective-permute-start | bytes 245768 | tf_op jit(solution)/shard_map/ppermute | solution.py:496
  7.7 6.1 %collective-permute-start.1 = (f32[5,16,256]{2,1,0:T(8,128)S(1)}, f32[5,16,256]{2,1,0:T(8,128)S(1)}, u32[]{:S(2)}, u32[]{:S(2)}) collective-permute-start(f32[5,16,256]{2,1,0:T(8,128)S(1)} %get-tuple-element.25), channel_id=1, source_target_pairs={{0,240},{16,0},{32,16},{48,32},{64,48},{80,64},{96,80},{112,96},{1... | collective-permute-start | bytes 245768 | tf_op jit(solution)/shard_map/ppermute | solution.py:496
  13.8 2.4 %collective-permute-start.3 = (f32[5,16,128]{2,1,0:T(8,128)S(1)}, f32[5,16,128]{2,1,0:T(8,128)S(1)}, u32[]{:S(2)}, u32[]{:S(2)}) collective-permute-start(f32[5,16,128]{2,1,0:T(8,128)S(1)} %get-tuple-element.27), channel_id=1, source_target_pairs={{0,2},{2,4},{4,6},{6,8},{8,10},{10,12},{12,14},{14,0},{1,3},{3,5},... | collective-permute-start | bytes 122888 | tf_op jit(solution)/shard_map/ppermute | solution.py:496
  16.2 0.0 collective-permute-start.4
  16.2 1.1 %collective-permute-done.3.z_before = f32[5,16,128]{2,1,0:T(8,128)S(1)} collective-permute-done((f32[5,16,128]{2,1,0:T(8,128)S(1)}, f32[5,16,128]{2,1,0:T(8,128)S(1)}, u32[]{:S(2)}, u32[]{:S(2)}) %collective-permute-start.3) | collective-permute-done | bytes 40992 | tf_op jit(solution)/shard_map/ppermute | solution.py:496
  17.3 2.3 %collective-permute-done.4.z_after = f32[5,16,128]{2,1,0:T(8,128)S(1)} collective-permute-done((f32[5,16,128]{2,1,0:T(8,128)S(1)}, f32[5,16,128]{2,1,0:T(8,128)S(1)}, u32[]{:S(2)}, u32[]{:S(2)}) %collective-permute-start.4) | collective-permute-done | bytes 40992 | tf_op jit(solution)/shard_map/ppermute | solution.py:496
  19.6 1.0 %collective-permute-done.x_before = f32[5,16,256]{2,1,0:T(8,128)S(1)} collective-permute-done((f32[5,16,256]{2,1,0:T(8,128)S(1)}, f32[5,16,256]{2,1,0:T(8,128)S(1)}, u32[]{:S(2)}, u32[]{:S(2)}) %collective-permute-start) | collective-permute-done | bytes 81952 | tf_op jit(solution)/shard_map/ppermute | solution.py:496
  20.6 0.0 collective-permute-done.2.y_halo
  20.6 0.0 copy-start.2
  20.6 1.4 %copy-done.2 = f32[64,3,1,4,512]{4,3,2,1,0:T(4,128)S(1)} copy-done((f32[64,3,1,4,512]{4,3,2,1,0:T(4,128)S(1)}, f32[64,3,1,4,512]{4,3,2,1,0:T(4,128)}, u32[]{:S(2)}) %copy-start.2) | copy-done | bytes 1572888
  22.0 1.0 %copy-done.3 = f32[16,3,1,4,512]{4,3,2,1,0:T(4,128)S(1)} copy-done((f32[16,3,1,4,512]{4,3,2,1,0:T(4,128)S(1)}, f32[16,3,1,4,512]{4,3,2,1,0:T(4,128)}, u32[]{:S(2)}) %copy-start.3) | copy-done | bytes 393240
  23.0 10.0 %shard_map.94 = (f32[5,32,16,256]{3,2,1,0:T(8,128)S(1)}, f32[5,16,256]{2,1,0:T(8,128)S(1)}, f32[5,16,256]{2,1,0:T(8,128)S(1)}, f32[5,40,256]{2,1,0:T(8,128)S(1)}...) custom-call(f32[5]{0:T(128)S(1)} %copy-done.4, ...), custom_call_target="tpu_custom_call" | custom-call | tf_op jit(solution)/shard_map/pallas_call | solution.py:542
  33.0 0.1 collective-permute-start.7
  33.1 0.1 collective-permute-start.5
  33.2 5.7 %collective-permute-start.6 = (f32[5,16,256]{2,1,0:T(8,128)S(1)}, f32[5,16,256]{2,1,0:T(8,128)S(1)}, u32[]{:S(2)}, u32[]{:S(2)}) collective-permute-start(f32[5,16,256]{2,1,0:T(8,128)S(1)} %get-tuple-element.32), channel_id=1, source_target_pairs={{0,240},{16,0},{32,16},{48,32},{64,48},{80,64},{96,80},{112,96},{1... | collective-permute-start | bytes 245768 | tf_op jit(solution)/shard_map/ppermute | solution.py:496
  38.9 3.6 %collective-permute-start.8 = (f32[5,16,128]{2,1,0:T(8,128)S(1)}, f32[5,16,128]{2,1,0:T(8,128)S(1)}, u32[]{:S(2)}, u32[]{:S(2)}) collective-permute-start(f32[5,16,128]{2,1,0:T(8,128)S(1)} %get-tuple-element.34), channel_id=1, source_target_pairs={{0,2},{2,4},{4,6},{6,8},{8,10},{10,12},{12,14},{14,0},{1,3},{3,5},... | collective-permute-start | bytes 122888 | tf_op jit(solution)/shard_map/ppermute | solution.py:496
  42.5 1.1 %collective-permute-done.8.z_before = f32[5,16,128]{2,1,0:T(8,128)S(1)} collective-permute-done((f32[5,16,128]{2,1,0:T(8,128)S(1)}, f32[5,16,128]{2,1,0:T(8,128)S(1)}, u32[]{:S(2)}, u32[]{:S(2)}) %collective-permute-start.8) | collective-permute-done | bytes 40992 | tf_op jit(solution)/shard_map/ppermute | solution.py:496
  43.6 2.3 %collective-permute-done.9.z_after = f32[5,16,128]{2,1,0:T(8,128)S(1)} collective-permute-done((f32[5,16,128]{2,1,0:T(8,128)S(1)}, f32[5,16,128]{2,1,0:T(8,128)S(1)}, u32[]{:S(2)}, u32[]{:S(2)}) %collective-permute-start.9) | collective-permute-done | bytes 40992 | tf_op jit(solution)/shard_map/ppermute | solution.py:496
  45.9 0.0 collective-permute-done.5.x_before
  45.9 0.0 collective-permute-done.6.x_after
  45.9 5.4 %shard_map.95 = (f32[5,32,16,256]{3,2,1,0:T(8,128)}, f32[128,128]{1,0:T(8,128)S(1)}) custom-call(f32[5]{0:T(128)S(1)} %copy-done.4, s32[3]{0:T(128)S(1)} %copy-done.5, f32[48,128]{1,0:T(8,128)S(1)} %get-tuple-element.29.folded, f32[5,32,16,256]{3,2,1,0:T(8,128)S(1)} %copy-done.1, f32[5,32,16,256]{3,2,1,0:T(8,128)S(1)} %get-tuple-element.30.current, ...), custom_call_target="tpu_custom_call" | custom-call | tf_op jit(solution)/shard_map/pallas_call | solution.py:555
  51.3 8.9 %all_to_all.15.relayed = f32[8,16,128]{2,1,0:T(8,128)S(1)} all-to-all(f32[8,16,128]{2,1,0:T(8,128)S(1)} %bitcast.11), channel_id=1, replica_groups=mesh['zh'=4,'x'=4,'y'=4,'core'=2,'zl'=2] {'y','core'}, dimensions={0} | all-to-all | bytes 131072 | tf_op jit(solution)/shard_map/all_to_all | solution.py:563
  60.3 0.4 shard_map.96
  60.7 11.1 %all_to_all.16 = f32[24,1,128]{2,1,0:T(1,128)S(1)} all-to-all(f32[24,1,128]{2,1,0:T(1,128)S(1)} %bitcast.13), channel_id=1, replica_groups=mesh['zh'=4,'x'=4,'y'=4,'core'=2,'zl'=2] {'zh','zl'}, dimensions={0} | all-to-all | bytes 24576 | tf_op jit(solution)/shard_map/all_to_all | solution.py:512
  71.7 0.7 shard_map.97
  72.4 6.2 %all-to-all-start.2 = ((f32[192,1,128]{2,1,0:T(1,128)}), f32[192,1,128]{2,1,0:T(1,128)S(1)}, u32[]{:S(2)}, u32[]{:S(2)}) async-start(f32[192,1,128]{2,1,0:T(1,128)} %bitcast.5), calls=%async_computation.2 | async-start | bytes 196608 | tf_op jit(solution)/shard_map/all_to_all | solution.py:512
  79.2 6.8 %all-to-all-done.2 = f32[192,1,128]{2,1,0:T(1,128)S(1)} async-done(((f32[192,1,128]{2,1,0:T(1,128)}), f32[192,1,128]{2,1,0:T(1,128)S(1)}, u32[]{:S(2)}, u32[]{:S(2)}) %all-to-all-start.2) | async-done | bytes 98336 | tf_op jit(solution)/shard_map/all_to_all | solution.py:512
  86.0 5.7 %shard_map.98 = (f32[16,64]{1,0:T(8,128)}, f32[16,16]{1,0:T(8,128)}, f32[16,3,1,4,512]{4,3,2,1,0:T(4,128)}) custom-call(s32[1]{0:T(128)S(6)} %copy.12.column_id, f32[192,128]{1,0:T(8,128)S(1)} %bitcast.10, f32[80,6144]{1,0:T(8,128)S(1)} %get-tuple-element.38.joined, f32[8,6144]{1,0:T(8,128)S(1)} %get-tuple-element.40.column), custom_call_target="tpu_custom_call" | custom-call | tf_op jit(solution)/shard_map/pallas_call | solution.py:577
  (10 shorter events, 0.0 us)
Async XLA Ops:
  0.6 1.7 %copy-start = (f32[5,32,16,256]{3,2,1,0:T(8,128)S(1)}, f32[5,32,16,256]{3,2,1,0:T(8,128)}, u32[]{:S(2)}) copy-start(f32[5,32,16,256]{3,2,1,0:T(8,128)} %start.1) | copy-start | bytes 7864324
  2.4 18.2 %copy-start.1 = (f32[5,32,16,256]{3,2,1,0:T(8,128)S(1)}, f32[5,32,16,256]{3,2,1,0:T(8,128)}, u32[]{:S(2)}) copy-start(f32[5,32,16,256]{3,2,1,0:T(8,128)} %start.1) | copy-start | bytes 7864324
  2.4 18.2 %copy-start.4 = (f32[5]{0:T(128)S(1)}, f32[5]{0:T(128)}, u32[]{:S(2)}) copy-start(f32[5]{0:T(128)} %diffusivity.3) | copy-start | bytes 64
  3.9 42.0 %copy-start.5 = (s32[3]{0:T(128)S(1)}, s32[3]{0:T(128)}, u32[]{:S(2)}) copy-start(s32[3]{0:T(128)} %offsets.1) | copy-start | bytes 40
  3.9 16.7 %collective-permute-start.2 = (f32[5,32,256]{2,1,0:T(8,128)S(1)}, f32[5,32,256]{2,1,0:T(8,128)S(1)}, u32[]{:S(2)}, u32[]{:S(2)}) collective-permute-start(f32[5,32,256]{2,1,0:T(8,128)S(1)} %get-tuple-element.26), channel_id=1, source_target_pairs={{0,1},{1,0},{2,3},{3,2},{4,5},{5,4},{6,7},{7,6},{8,9},{9,8},{10,11... | collective-permute-start | bytes 491528 | tf_op jit(solution)/shard_map/ppermute | solution.py:496
  6.5 14.1 %collective-permute-start = (f32[5,16,256]{2,1,0:T(8,128)S(1)}, f32[5,16,256]{2,1,0:T(8,128)S(1)}, u32[]{:S(2)}, u32[]{:S(2)}) collective-permute-start(f32[5,16,256]{2,1,0:T(8,128)S(1)} %get-tuple-element.24), channel_id=1, source_target_pairs={{0,16},{16,32},{32,48},{48,64},{64,80},{80,96},{96,112},{112,128},... | collective-permute-start | bytes 245768 | tf_op jit(solution)/shard_map/ppermute | solution.py:496
  7.7 12.9 %collective-permute-start.1 = (f32[5,16,256]{2,1,0:T(8,128)S(1)}, f32[5,16,256]{2,1,0:T(8,128)S(1)}, u32[]{:S(2)}, u32[]{:S(2)}) collective-permute-start(f32[5,16,256]{2,1,0:T(8,128)S(1)} %get-tuple-element.25), channel_id=1, source_target_pairs={{0,240},{16,0},{32,16},{48,32},{64,48},{80,64},{96,80},{112,96},{1... | collective-permute-start | bytes 245768 | tf_op jit(solution)/shard_map/ppermute | solution.py:496
  13.8 3.5 %collective-permute-start.3 = (f32[5,16,128]{2,1,0:T(8,128)S(1)}, f32[5,16,128]{2,1,0:T(8,128)S(1)}, u32[]{:S(2)}, u32[]{:S(2)}) collective-permute-start(f32[5,16,128]{2,1,0:T(8,128)S(1)} %get-tuple-element.27), channel_id=1, source_target_pairs={{0,2},{2,4},{4,6},{6,8},{8,10},{10,12},{12,14},{14,0},{1,3},{3,5},... | collective-permute-start | bytes 122888 | tf_op jit(solution)/shard_map/ppermute | solution.py:496
  16.2 3.4 %collective-permute-start.4 = (f32[5,16,128]{2,1,0:T(8,128)S(1)}, f32[5,16,128]{2,1,0:T(8,128)S(1)}, u32[]{:S(2)}, u32[]{:S(2)}) collective-permute-start(f32[5,16,128]{2,1,0:T(8,128)S(1)} %get-tuple-element.28), channel_id=1, source_target_pairs={{0,14},{2,0},{4,2},{6,4},{8,6},{10,8},{12,10},{14,12},{1,15},{3,1}... | collective-permute-start | bytes 122888 | tf_op jit(solution)/shard_map/ppermute | solution.py:496
  20.6 1.4 %copy-start.2 = (f32[64,3,1,4,512]{4,3,2,1,0:T(4,128)S(1)}, f32[64,3,1,4,512]{4,3,2,1,0:T(4,128)}, u32[]{:S(2)}) copy-start(f32[64,3,1,4,512]{4,3,2,1,0:T(4,128)} %basis.1) | copy-start | bytes 4718596
  22.0 1.0 %copy-start.3 = (f32[16,3,1,4,512]{4,3,2,1,0:T(4,128)S(1)}, f32[16,3,1,4,512]{4,3,2,1,0:T(4,128)}, u32[]{:S(2)}) copy-start(f32[16,3,1,4,512]{4,3,2,1,0:T(4,128)} %held.1) | copy-start | bytes 1179652
  33.0 12.9 %collective-permute-start.7 = (f32[5,40,256]{2,1,0:T(8,128)S(1)}, f32[5,40,256]{2,1,0:T(8,128)S(1)}, u32[]{:S(2)}, u32[]{:S(2)}) collective-permute-start(f32[5,40,256]{2,1,0:T(8,128)S(1)} %get-tuple-element.33), channel_id=1, source_target_pairs={{0,1},{1,0},{2,3},{3,2},{4,5},{5,4},{6,7},{7,6},{8,9},{9,8},{10,11... | collective-permute-start | bytes 614408 | tf_op jit(solution)/shard_map/ppermute | solution.py:496
  33.1 12.8 %collective-permute-start.5 = (f32[5,16,256]{2,1,0:T(8,128)S(1)}, f32[5,16,256]{2,1,0:T(8,128)S(1)}, u32[]{:S(2)}, u32[]{:S(2)}) collective-permute-start(f32[5,16,256]{2,1,0:T(8,128)S(1)} %get-tuple-element.31), channel_id=1, source_target_pairs={{0,16},{16,32},{32,48},{48,64},{64,80},{80,96},{96,112},{112,128},... | collective-permute-start | bytes 245768 | tf_op jit(solution)/shard_map/ppermute | solution.py:496
  33.2 12.7 %collective-permute-start.6 = (f32[5,16,256]{2,1,0:T(8,128)S(1)}, f32[5,16,256]{2,1,0:T(8,128)S(1)}, u32[]{:S(2)}, u32[]{:S(2)}) collective-permute-start(f32[5,16,256]{2,1,0:T(8,128)S(1)} %get-tuple-element.32), channel_id=1, source_target_pairs={{0,240},{16,0},{32,16},{48,32},{64,48},{80,64},{96,80},{112,96},{1... | collective-permute-start | bytes 245768 | tf_op jit(solution)/shard_map/ppermute | solution.py:496
  38.9 4.7 %collective-permute-start.8 = (f32[5,16,128]{2,1,0:T(8,128)S(1)}, f32[5,16,128]{2,1,0:T(8,128)S(1)}, u32[]{:S(2)}, u32[]{:S(2)}) collective-permute-start(f32[5,16,128]{2,1,0:T(8,128)S(1)} %get-tuple-element.34), channel_id=1, source_target_pairs={{0,2},{2,4},{4,6},{6,8},{8,10},{10,12},{12,14},{14,0},{1,3},{3,5},... | collective-permute-start | bytes 122888 | tf_op jit(solution)/shard_map/ppermute | solution.py:496
  42.5 3.4 %collective-permute-start.9 = (f32[5,16,128]{2,1,0:T(8,128)S(1)}, f32[5,16,128]{2,1,0:T(8,128)S(1)}, u32[]{:S(2)}, u32[]{:S(2)}) collective-permute-start(f32[5,16,128]{2,1,0:T(8,128)S(1)} %get-tuple-element.35), channel_id=1, source_target_pairs={{0,14},{2,0},{4,2},{6,4},{8,6},{10,8},{12,10},{14,12},{1,15},{3,1}... | collective-permute-start | bytes 122888 | tf_op jit(solution)/shard_map/ppermute | solution.py:496
  72.4 13.6 %all-to-all-start.2 = ((f32[192,1,128]{2,1,0:T(1,128)}), f32[192,1,128]{2,1,0:T(1,128)S(1)}, u32[]{:S(2)}, u32[]{:S(2)}) async-start(f32[192,1,128]{2,1,0:T(1,128)} %bitcast.5), calls=%async_computation.2 | async-start | bytes 196608 | tf_op jit(solution)/shard_map/all_to_all | solution.py:512

commit v4 on v3

--- a/solution.py
+++ b/solution.py
@@ -1,4 +1,5 @@
 import functools
+import itertools
 
 import jax
 import jax.numpy as jnp
@@ -71,22 +72,22 @@
     )
 
 
-def pack_kernel(source, x_low, x_high, y_row, z_low, z_high, fields, semaphores):
+def odd(axis):
+    return lax.rem(lax.axis_index(axis), 2) > 0
+
+
+def arrange(x_low, x_high, z_low, z_high, x_pair, x_next, z_pair, z_next):
+    x_odd, second = odd("x"), odd("core")
+    x_pair[...] = jnp.where(x_odd, x_low, x_high)
+    x_next[...] = jnp.where(x_odd, x_high, x_low)
+    z_pair[...] = jnp.where(second, z_low, z_high)
+    z_next[...] = jnp.where(second, z_high, z_low)
+
+
+def pack_kernel(fields, x_pair, x_next, y_row, z_pair, z_next, z_low, z_high):
     count, cells, height, _ = fields.shape
     upper = lax.axis_index("zl") > 0
     lane = iota((8, LANES), 1)
-    parts = semaphores.shape[0]
-    each = cells // parts
-    copies = [
-        pltpu.make_async_copy(
-            source.at[:, part * each : (part + 1) * each],
-            fields.at[:, part * each : (part + 1) * each],
-            semaphores.at[part],
-        )
-        for part in range(parts)
-    ]
-    for copy in copies:
-        copy.start()
     y_row[...] = jnp.zeros_like(y_row)
     z_low[...] = jnp.zeros_like(z_low)
     z_high[...] = jnp.zeros_like(z_high)
@@ -102,11 +103,11 @@
                     put_columns(x, lane, value, (z_low, z_high)[half], f, tile, half == 1)
         return carry
 
-    for part in range(parts):
-        copies[part].wait()
-        lax.fori_loop(part * each, (part + 1) * each, body, 0, unroll=PACK_UNROLL)
-    x_low[...] = fields[:, 0]
-    x_high[...] = fields[:, cells - 1]
+    lax.fori_loop(0, cells, body, 0, unroll=PACK_UNROLL)
+    arrange(
+        fields[:, 0], fields[:, cells - 1], z_low[...], z_high[...],
+        x_pair, x_next, z_pair, z_next,
+    )
 
 
 def half_plane(x, half, current, before, after, y_halo, z_before, z_after, diffusivity, upper):
@@ -178,10 +179,13 @@
     return centre, rates
 
 
-def planes(current, halos, diffusivity, finish, after_three, after_first=lambda: None):
-    x_before, x_after, y_halo, z_before, z_after = halos
+def planes(current, halos, diffusivity, finish, after_three=lambda step: None):
+    x_pair, x_next, y_halo, z_pair, z_next, z_before, z_after = halos
     cells = current.shape[1]
     upper = lax.axis_index("zl") > 0
+    x_odd, second = odd("x"), odd("core")
+    z_before[...] = jnp.where(second, z_pair[...], z_next[...])
+    z_after[...] = jnp.where(second, z_next[...], z_pair[...])
 
     def one(x, before, after):
         for half in range(2):
@@ -196,11 +200,10 @@
     def inside(offset, x):
         return lambda f, rows, lanes: current[f, x + offset, rows, lanes]
 
-    def outside(ref):
-        return lambda f, rows, lanes: ref[f, rows, lanes]
-
-    one(0, outside(x_before), inside(1, 0))
-    after_first()
+    def outside(here, there):
+        return lambda f, rows, lanes: jnp.where(x_odd, here[f, rows, lanes], there[f, rows, lanes])
+
+    one(0, outside(x_pair, x_next), inside(1, 0))
     blocks = (cells - 2) // BLOCK
 
     def body(step, carry):
@@ -211,18 +214,12 @@
         return carry
 
     lax.fori_loop(0, blocks, body, 0)
-    one(cells - 1, inside(-1, cells - 1), outside(x_after))
-
-
-def first_kernel(
-    diffusivity, basis, held, current, x_before, x_after, y_halo, z_before, z_after,
-    first, x_low, x_high, y_row, z_low, z_high, joined, folded, sums, squares, semaphores,
-):
-    count, cells = current.shape[:2]
+    one(cells - 1, inside(-1, cells - 1), outside(x_next, x_pair))
+
+
+def gram_kernel(basis, held, joined, folded, semaphores):
     rank, _, _, levels, points = basis.shape
     total = rank + held.shape[0]
-    upper = lax.axis_index("zl") > 0
-    lane = iota((8, LANES), 1)
     copies = []
     for chunk in range(3 * levels):
         lanes = slice(chunk * points, (chunk + 1) * points)
@@ -238,45 +235,19 @@
             )
     for copy in copies:
         copy.start()
-    y_row[...] = jnp.zeros_like(y_row)
-    z_low[...] = jnp.zeros_like(z_low)
-    z_high[...] = jnp.zeros_like(z_high)
-    sums[...] = jnp.zeros_like(sums)
-    squares[...] = jnp.zeros_like(squares)
-
-    def finish(x, half, centre, rates):
-        lanes = slice(half * LANES, (half + 1) * LANES)
-        for f in range(count):
-            new = []
-            for tile in range(2):
-                rows = slice(tile * 8, tile * 8 + 8)
-                value = centre[f, tile] + time_step * rates[f, tile]
-                new.append(value)
-                first[f, x, rows, lanes] = value
-                if isinstance(x, int):
-                    (x_low if x == 0 else x_high)[f, rows, lanes] = value
-                put_columns(x, lane, value, (z_low, z_high)[half], f, tile, half == 1)
-            put_row(x, upper, new[1], new[0], y_row, f, half)
-
-    def gram(chunk):
-        part = joined[:, pl.ds(pl.multiple_of(chunk * points, LANES), points)]
-        high, middle, low = split(part)
-        sums[...] += matmul(jnp.concatenate([high, middle, low], axis=0), high, 1)
-        squares[...] += matmul(middle, middle, 1)
-
-    def arrived():
-        for copy in copies:
-            copy.wait()
-
-    halos = (x_before, x_after, y_halo, z_before, z_after)
-    planes(current, halos, diffusivity, finish, gram, arrived)
-    for chunk in range((cells - 2) // BLOCK, 3 * levels):
-        gram(chunk)
+    sums = jnp.zeros((3 * total, total), jnp.float32)
+    squares = jnp.zeros((total, total), jnp.float32)
+    for chunk in range(3 * levels):
+        copies[2 * chunk].wait()
+        copies[2 * chunk + 1].wait()
+        high, middle, low = split(joined[:, chunk * points : (chunk + 1) * points])
+        sums += matmul(jnp.concatenate([high, middle, low], axis=0), high, 1)
+        squares += matmul(middle, middle, 1)
     half = total // 2
     wide = jnp.zeros((total, LANES - total), jnp.float32)
     cross = jnp.concatenate([sums[total : 2 * total] + sums[2 * total :], wide], axis=1)
     tall = jnp.concatenate([cross, jnp.zeros((LANES - total, LANES), jnp.float32)], axis=0)
-    values = jnp.concatenate([sums[:total] + squares[...], wide], axis=1)
+    values = jnp.concatenate([sums[:total] + squares, wide], axis=1)
     values = values + (cross + tall.T[:total])
     lane, sub = iota((half, LANES), 1), iota((half, LANES), 0)
     lower = pltpu.roll(values[half:], LANES - half, 1)
@@ -285,16 +256,46 @@
     values = jnp.where(lane == total, jnp.broadcast_to(diagonal, (half, LANES)), values)
     folded[0:half, :] = jnp.where(lane <= total, values, 0.0)
     folded[half:, :] = jnp.zeros((folded.shape[0] - half, LANES), jnp.float32)
+
+
+def first_kernel(
+    diffusivity, folded, current, x_pair_in, x_next_in, y_halo, z_pair_in, z_next_in,
+    first, x_pair, x_next, y_row, z_pair, z_next, z_before, z_after, z_low, z_high,
+):
+    count, cells = current.shape[:2]
+    upper = lax.axis_index("zl") > 0
+    lane = iota((8, LANES), 1)
+    y_row[...] = jnp.zeros_like(y_row)
+    z_low[...] = jnp.zeros_like(z_low)
+    z_high[...] = jnp.zeros_like(z_high)
     for group in range(3):
         lanes = slice(group % 2 * LANES, (group % 2 + 1) * LANES)
         y_row[group // 2, cells:, lanes] = jnp.where(
             upper, folded[group * 8 : group * 8 + 8], folded[group * 8 + 24 : group * 8 + 32]
         )
 
+    def finish(x, half, centre, rates):
+        lanes = slice(half * LANES, (half + 1) * LANES)
+        for f in range(count):
+            new = []
+            for tile in range(2):
+                value = centre[f, tile] + time_step * rates[f, tile]
+                new.append(value)
+                first[f, x, tile * 8 : tile * 8 + 8, lanes] = value
+                put_columns(x, lane, value, (z_low, z_high)[half], f, tile, half == 1)
+            put_row(x, upper, new[1], new[0], y_row, f, half)
+
+    halos = (x_pair_in, x_next_in, y_halo, z_pair_in, z_next_in, z_before, z_after)
+    planes(current, halos, diffusivity, finish)
+    arrange(
+        first[:, 0], first[:, cells - 1], z_low[...], z_high[...],
+        x_pair, x_next, z_pair, z_next,
+    )
+
 
 def second_kernel(
-    diffusivity, offsets, folded, start, current, x_before, x_after, y_halo, z_before, z_after,
-    target, snapshot, picked, result, semaphores,
+    diffusivity, offsets, folded, start, current, x_pair, x_next, y_halo, z_pair, z_next,
+    target, snapshot, z_before, z_after, picked, result, semaphores,
 ):
     count, cells, height, width = current.shape
     blocks = (cells - 2) // BLOCK
@@ -315,7 +316,8 @@
     def send(step):
         copied(step * BLOCK + 1, BLOCK, step).start()
 
-    planes(current, (x_before, x_after, y_halo, z_before, z_after), diffusivity, finish, send)
+    halos = (x_pair, x_next, y_halo, z_pair, z_next, z_before, z_after)
+    planes(current, halos, diffusivity, finish, send)
     copied(0, 1, blocks).start()
     copied(cells - 1, 1, blocks + 1).start()
     levels = height // STRIDE
@@ -381,19 +383,19 @@
         moved = pltpu.roll(products, 88 - 40 * piece if piece < 2 else 8, 1)[0:1]
         row = jnp.where(lane[0:1] < 88, own[4 + piece : 5 + piece], moved)
         values = jnp.where(which == piece, row, values)
-    message[...] = values
+    count = message.shape[0]
+    message[...] = jnp.broadcast_to(values[None], (count // 24, 24, LANES)).reshape(count, LANES)
 
 
 def middle_kernel(received, message):
-    rows = sum(received[6 * part : 6 * part + 6, :] for part in range(4))
-    tile = jnp.concatenate([rows] * 4, axis=0)
+    rows = jnp.sum(received[...].reshape(-1, 24, LANES), axis=0)
     count = message.shape[0]
-    message[...] = jnp.broadcast_to(tile[None], (count // 24, 24, LANES)).reshape(count, LANES)
+    message[...] = jnp.broadcast_to(rows[None], (count // 24, 24, LANES)).reshape(count, LANES)
 
 
 def final_kernel(
     rows_total, column_id, gathered, joined, column,
-    coefficients, r_factor, columns_out, stacked, results, semaphores,
+    coefficients, r_factor, columns_out, stacked,
 ):
     total = joined.shape[0]
     count, rank = coefficients.shape
@@ -402,7 +404,7 @@
     half = total // 2
     stacked[...] = jnp.sum(gathered[...].reshape(-1, 48, LANES), axis=0)
     pieces = [
-        [stacked[pl.ds(part * 3 + piece, 8, stride=6), :] for piece in range(3)]
+        [stacked[pl.ds(part * 24 + piece, 8, stride=3), :] for piece in range(3)]
         for part in range(2)
     ]
     sums = [jnp.sum(pieces[0][i] + pieces[1][i], axis=0, keepdims=True) for i in range(3)]
@@ -464,46 +466,47 @@
     )
     weights = jnp.where(block_lane < rank, onto_modes, onto_block)[:, :total]
     weights = jnp.concatenate(split(weights), axis=0)
-    copies = []
     for chunk in range(3 * levels):
         lanes = slice(chunk * points, (chunk + 1) * points)
         high, middle, low = split(joined[:, lanes])
         first = matmul(weights, high, 0)
         second = matmul(weights[: 2 * count], middle, 0)
         third = matmul(weights[:count], low, 0)
-        results[chunk] = (
+        columns_out[:, chunk // levels, 0, chunk % levels, :] = (
             (first[:count] + own * column[0:1, lanes])
             + (first[count : 2 * count] + second[:count])
             + (first[2 * count :] + second[count:] + third)
         )
-        copies.append(
-            pltpu.make_async_copy(
-                results.at[chunk],
-                columns_out.at[:, chunk // levels, 0, chunk % levels, :],
-                semaphores.at[chunk],
-            )
-        )
-        copies[-1].start()
-    for copy in copies:
-        copy.wait()
-
-
-def shifted(value, axes, step):
-    axes = axes if isinstance(axes, tuple) else (axes,)
-    count = 1
-    for axis in axes:
-        count *= lax.axis_size(axis)
-    return lax.ppermute(value, axes, [(i, (i + step) % count) for i in range(count)])
+
+
+def moved(value, axes, target):
+    sizes = [lax.axis_size(axis) for axis in axes]
+    places = list(itertools.product(*(range(size) for size in sizes)))
+    flat = {place: i for i, place in enumerate(places)}
+    pairs = [
+        (flat[place], flat[tuple(i % size for i, size in zip(target(*place), sizes))])
+        for place in places
+    ]
+    return lax.ppermute(value, axes, pairs)
 
 
 def exchange(faces):
-    x_low, x_high, y_row, z_low, z_high = faces
+    x_pair, x_next, y_row, z_pair, z_next = faces
+
+    def along(zh, x):
+        step = x + 1 if x % 2 else x - 1
+        return zh + step // 4, step
+
+    def swap(core):
+        return (core ^ 1,)
+
+    z_next = moved(z_next, ("y", "core"), lambda y, core: (y + 2 * core - 1, core))
     return (
-        shifted(x_high, ("zh", "x"), 1),
-        shifted(x_low, ("zh", "x"), -1),
-        shifted(y_row, "zl", 1),
-        shifted(z_high, ("y", "core"), 1),
-        shifted(z_low, ("y", "core"), -1),
+        moved(x_pair, ("x",), lambda x: (x ^ 1,)),
+        moved(x_next, ("zh", "x"), along),
+        moved(y_row, ("zl",), lambda zl: (zl + 1,)),
+        moved(z_pair, ("core",), swap),
+        moved(z_next, ("core",), swap),
     )
 
 
@@ -530,33 +533,35 @@
         struct(count, height, LANES),
         struct(count, height, LANES),
     )
-    block_space = pltpu.VMEM(fields.shape, jnp.float32)
+    edge = pltpu.VMEM((count, height, LANES), jnp.float32)
 
     packed = pl.pallas_call(
-        pack_kernel, in_specs=[ANY], out_specs=[VMEM] * 5, out_shape=faces,
-        scratch_shapes=[block_space, pltpu.SemaphoreType.DMA((4,))],
-        compiler_params=params(16),
+        pack_kernel, in_specs=[VMEM], out_specs=[VMEM] * 5, out_shape=faces,
+        scratch_shapes=[edge] * 2, compiler_params=params(16),
     )(fields)
     halos = exchange(packed)
 
-    first, *packed, joined, folded = pl.pallas_call(
-        first_kernel, in_specs=[SMEM] + [ANY] * 2 + [VMEM] * 6, out_specs=[VMEM] * 8,
+    joined, folded = pl.pallas_call(
+        gram_kernel, in_specs=[ANY] * 2, out_specs=[VMEM] * 2,
+        out_shape=(struct(total, length), struct(48, LANES)),
+        scratch_shapes=[pltpu.SemaphoreType.DMA((2 * chunks,))],
+        compiler_params=params(16),
+    )(pod_basis, held_block)
+
+    first, *packed = pl.pallas_call(
+        first_kernel, in_specs=[SMEM] + [VMEM] * 7, out_specs=[VMEM] * 6,
         out_shape=(struct(*fields.shape),) + faces[:2] + (struct(count, cells + 8, width),)
-        + faces[3:] + (struct(total, length), struct(48, LANES)),
-        scratch_shapes=[
-            pltpu.VMEM((3 * total, total), jnp.float32),
-            pltpu.VMEM((total, total), jnp.float32),
-            pltpu.SemaphoreType.DMA((2 * chunks,)),
-        ],
-        compiler_params=params(24),
-    )(diffusivity, pod_basis, held_block, fields, *halos)
+        + faces[3:],
+        scratch_shapes=[edge] * 4, compiler_params=params(24),
+    )(diffusivity, folded, fields, *halos)
     halos = exchange(packed)
 
     fields_out, snapshot = pl.pallas_call(
         second_kernel, in_specs=[SMEM] * 2 + [VMEM] * 8, out_specs=[ANY, VMEM],
         out_shape=(struct(*fields.shape), struct(LANES, LANES)),
         scratch_shapes=[
-            pltpu.VMEM((LANES, width), jnp.float32), block_space, pltpu.SemaphoreType.DMA((12,)),
+            edge, edge, pltpu.VMEM((LANES, width), jnp.float32),
+            pltpu.VMEM(fields.shape, jnp.float32), pltpu.SemaphoreType.DMA((12,)),
         ],
         compiler_params=params(24),
     )(diffusivity, subsample_offsets, folded, fields, first, *halos)
@@ -564,26 +569,24 @@
 
     message, column = pl.pallas_call(
         product_kernel, in_specs=[VMEM] * 2, out_specs=[VMEM] * 2,
-        out_shape=(struct(24, LANES), struct(8, length)),
+        out_shape=(struct(96, LANES), struct(8, length)),
         scratch_shapes=[pltpu.VMEM((LANES, LANES), jnp.float32)],
         compiler_params=params(16),
     )(relayed, joined)
     message = pl.pallas_call(
         middle_kernel, in_specs=[VMEM], out_specs=VMEM, out_shape=struct(192, LANES),
         compiler_params=params(4),
-    )(everyone(message, ("zh", "zl")))
-    gathered = everyone(message, ("x", "y", "core"))
+    )(everyone(message, ("x", "y", "core")))
+    gathered = everyone(message, ("zh", "zl"))
 
     coefficients, r_factor, new_columns = pl.pallas_call(
         functools.partial(final_kernel, float(devices * length)),
-        in_specs=[SMEM] + [VMEM] * 3, out_specs=[VMEM] * 2 + [ANY],
+        in_specs=[SMEM] + [VMEM] * 3, out_specs=[VMEM] * 3,
         out_shape=(
             struct(columns, rank), struct(columns, columns), struct(*held_block.shape)
         ),
         scratch_shapes=[
             pltpu.VMEM((48, LANES), jnp.float32),
-            pltpu.VMEM((chunks, columns, points), jnp.float32),
-            pltpu.SemaphoreType.DMA((chunks,)),
         ],
         compiler_params=params(24),
     )(column_id, gathered, joined, column)

time: 92 us -> 87 us (0.946)
  waiting for transfers between devices: 14.6 us -> 9.09 us
  blocking collectives: 20 us -> 22.6 us
  starting transfers between devices: 27.9 us -> 25.5 us
    ppermute x10 -> x12, waiting for transfers between devices: 7.83 us -> 2.28 us  [moved(): return lax.ppermute(value, axes, pairs)]
    all_to_all x1, blocking collectives: 8.93 us -> 11.8 us  [on_device(): lax.all_to_all(snapshot.reshape(8, 16, LANES), ('y', 'core'), 0, 0, tiled...]
    pallas_call x2 -> x3, Pallas kernels: 11.5 us -> 13.6 us  [the longest x1 7.71 us: on_device(): pl.pallas_call(first_kernel, in_specs=[SMEM] + [VMEM] * 7, out_specs=[VME...]
    all_to_all x1, starting transfers between devices: 6.16 us -> 4.23 us  [everyone(): lax.all_to_all(message.reshape(rows, 1, LANES), axes, 0, 0, tiled=True)]
    pallas_call x1, Pallas kernels: 5.69 us -> 3.78 us  [on_device(): pl.pallas_call(functools.partial(final_kernel, float(devices * length)),...]
    ppermute x10 -> x12, starting transfers between devices: 21.7 us -> 21.2 us  [moved(): return lax.ppermute(value, axes, pairs)]
  transfers between devices with their start and end apart: 11 -> 13, of which waited for: 6 -> 4; matrix products, arithmetic and copies ran while one was open for 0% -> 0% of each run, Pallas kernels for 0% -> 5%
where the time goes in v4:
time: 87 us; the launch traced here: 86.6 us
  starting transfers between devices  25.5 us (29%)
  Pallas kernels  23.9 us (27%)
  blocking collectives  22.6 us (26%)
  waiting for transfers between devices  9.09 us (10%)
  local copies, waits for them, and re-layouts  4.15 us (5%)
  between operations  1.4 us (2%)
    ppermute x12, starting transfers between devices, moved(): return lax.ppermute(value, axes, pairs)  21.2 us
    all_to_all x1, blocking collectives, on_device(): lax.all_to_all(snapshot.reshape(8, 16, LANES), ('y', 'core'), 0, 0, tiled...  11.8 us
    all_to_all x1, blocking collectives, everyone(): lax.all_to_all(message.reshape(rows, 1, LANES), axes, 0, 0, tiled=True)  10.8 us
    pallas_call x1, Pallas kernels, on_device(): pl.pallas_call(first_kernel, in_specs=[SMEM] + [VMEM] * 7, out_specs=[VME...  7.71 us
    all_to_all x1, waiting for transfers between devices, everyone(): lax.all_to_all(message.reshape(rows, 1, LANES), axes, 0, 0, tiled=True)  6.81 us
    pallas_call x1, Pallas kernels, on_device(): pl.pallas_call(second_kernel, in_specs=[SMEM] * 2 + [VMEM] * 8, out_specs...  5.48 us
    pallas_call x1, Pallas kernels, on_device(): pl.pallas_call(gram_kernel, in_specs=[ANY] * 2, out_specs=[VMEM] * 2, out...  4.51 us
    all_to_all x1, starting transfers between devices, everyone(): lax.all_to_all(message.reshape(rows, 1, LANES), axes, 0, 0, tiled=True)  4.23 us
  transfers between devices with their start and end apart: 13, of which 4 were waited for; matrix products, arithmetic and copies ran while one was open for 0% of the time, Pallas kernels for 5%

profile of v4, /device:TPU:1, one launch (start us, length us, event | category | flops | bytes accessed | tf_op | source)
XLA Modules:
  0.0 86.6 jit_solution(2547382709890013337)
XLA Ops:
  0.6 1.7 %copy-done = f32[5,32,16,256]{3,2,1,0:T(8,128)S(1)} copy-done((f32[5,32,16,256]{3,2,1,0:T(8,128)S(1)}, f32[5,32,16,256]{3,2,1,0:T(8,128)}, u32[]{:S(2)}) %copy-start) | copy-done | bytes 2621464
  2.4 1.3 %shard_map.94 = (f32[5,16,256]{2,1,0:T(8,128)S(1)}, f32[5,16,256]{2,1,0:T(8,128)S(1)}, f32[5,32,256]{2,1,0:T(8,128)S(1)}, f32[5,16,128]{2,1,0:T(8,128)S(1)}, f32[5,16,128]{2,1,0:T(8,128)S(1)}) custom-call(f32[5,32,16,256]{3,2,1,0:T(8,128)S(1)} %copy-done), custom_call_target="tpu_custom_call" | custom-call | tf_op jit(solution)/shard_map/pallas_call | solution.py:538
  3.7 0.0 copy-start.5
  3.7 2.6 %collective-permute-start.2 = (f32[5,32,256]{2,1,0:T(8,128)S(1)}, f32[5,32,256]{2,1,0:T(8,128)S(1)}, u32[]{:S(2)}, u32[]{:S(2)}) collective-permute-start(f32[5,32,256]{2,1,0:T(8,128)S(1)} %get-tuple-element.27), channel_id=1, source_target_pairs={{0,1},{1,0},{2,3},{3,2},{4,5},{5,4},{6,7},{7,6},{8,9},{9,8},{10,11... | collective-permute-start | bytes 491528 | tf_op jit(solution)/shard_map/ppermute | solution.py:490
  6.3 1.3 %collective-permute-start.4 = (f32[5,16,128]{2,1,0:T(8,128)S(1)}, f32[5,16,128]{2,1,0:T(8,128)S(1)}, u32[]{:S(2)}, u32[]{:S(2)}) collective-permute-start(f32[5,16,128]{2,1,0:T(8,128)S(1)} %get-tuple-element.29), channel_id=1, source_target_pairs={{0,12},{2,6},{4,0},{6,10},{8,4},{10,14},{12,8},{14,2},{1,13},{3,7}... | collective-permute-start | bytes 122888 | tf_op jit(solution)/shard_map/ppermute | solution.py:490
  7.6 1.2 %collective-permute-start = (f32[5,16,256]{2,1,0:T(8,128)S(1)}, f32[5,16,256]{2,1,0:T(8,128)S(1)}, u32[]{:S(2)}, u32[]{:S(2)}) collective-permute-start(f32[5,16,256]{2,1,0:T(8,128)S(1)} %get-tuple-element.25), channel_id=1, source_target_pairs={{0,16},{16,0},{32,48},{48,32},{1,17},{17,1},{33,49},{49,33},{2,18}... | collective-permute-start | bytes 245768 | tf_op jit(solution)/shard_map/ppermute | solution.py:490
  8.8 6.7 %collective-permute-start.1 = (f32[5,16,256]{2,1,0:T(8,128)S(1)}, f32[5,16,256]{2,1,0:T(8,128)S(1)}, u32[]{:S(2)}, u32[]{:S(2)}) collective-permute-start(f32[5,16,256]{2,1,0:T(8,128)S(1)} %get-tuple-element.26), channel_id=1, source_target_pairs={{0,240},{16,32},{32,16},{48,64},{64,48},{80,96},{96,80},{112,128},... | collective-permute-start | bytes 245768 | tf_op jit(solution)/shard_map/ppermute | solution.py:490
  15.4 3.2 %collective-permute-start.3 = (f32[5,16,128]{2,1,0:T(8,128)S(1)}, f32[5,16,128]{2,1,0:T(8,128)S(1)}, u32[]{:S(2)}, u32[]{:S(2)}) collective-permute-start(f32[5,16,128]{2,1,0:T(8,128)S(1)} %get-tuple-element.28), channel_id=1, source_target_pairs={{0,2},{2,0},{1,3},{3,1},{4,6},{6,4},{5,7},{7,5},{8,10},{10,8},{9,1... | collective-permute-start | bytes 122888 | tf_op jit(solution)/shard_map/ppermute | solution.py:490
  18.7 0.0 collective-permute-done.4
  18.7 0.0 collective-permute-start.5
  18.7 1.4 %copy-done.2 = f32[64,3,1,4,512]{4,3,2,1,0:T(4,128)S(1)} copy-done((f32[64,3,1,4,512]{4,3,2,1,0:T(4,128)S(1)}, f32[64,3,1,4,512]{4,3,2,1,0:T(4,128)}, u32[]{:S(2)}) %copy-start.2) | copy-done | bytes 1572888
  20.1 1.0 %copy-done.3 = f32[16,3,1,4,512]{4,3,2,1,0:T(4,128)S(1)} copy-done((f32[16,3,1,4,512]{4,3,2,1,0:T(4,128)S(1)}, f32[16,3,1,4,512]{4,3,2,1,0:T(4,128)}, u32[]{:S(2)}) %copy-start.3) | copy-done | bytes 393240
  21.1 4.5 %shard_map.93 = (f32[80,6144]{1,0:T(8,128)S(1)}, f32[48,128]{1,0:T(8,128)S(1)}) custom-call(f32[64,3,1,4,512]{4,3,2,1,0:T(4,128)S(1)} %copy-done.2, f32[16,3,1,4,512]{4,3,2,1,0:T(4,128)S(1)} %copy-done.3), custom_call_target="tpu_custom_call" | custom-call | tf_op jit(solution)/shard_map/pallas_call | solution.py:544
  25.6 0.0 collective-permute-done.3.z_pair_in
  25.6 0.0 collective-permute-done.5.z_next_in
  25.6 0.0 collective-permute-done.1.x_next_in
  25.7 7.7 %shard_map.95 = (f32[5,32,16,256]{3,2,1,0:T(8,128)S(1)}, f32[5,16,256]{2,1,0:T(8,128)S(1)}, f32[5,16,256]{2,1,0:T(8,128)S(1)}, f32[5,40,256]{2,1,0:T(8,128)S(1)}...) custom-call(f32[5]{0:T(128)S(1)} %copy-done.4, f32[48,128]{1,0:T(8,128)S(1)} %get-tuple-element.24.folded, ...), custom_call_target="tpu_custom_call" | custom-call | tf_op jit(solution)/shard_map/pallas_call | solution.py:551
  33.4 0.8 collective-permute-start.8
  34.2 1.7 %collective-permute-start.7 = (f32[5,16,256]{2,1,0:T(8,128)S(1)}, f32[5,16,256]{2,1,0:T(8,128)S(1)}, u32[]{:S(2)}, u32[]{:S(2)}) collective-permute-start(f32[5,16,256]{2,1,0:T(8,128)S(1)} %get-tuple-element.32), channel_id=1, source_target_pairs={{0,240},{16,32},{32,16},{48,64},{64,48},{80,96},{96,80},{112,128},... | collective-permute-start | bytes 245768 | tf_op jit(solution)/shard_map/ppermute | solution.py:490
  35.9 3.8 %collective-permute-start.9 = (f32[5,16,128]{2,1,0:T(8,128)S(1)}, f32[5,16,128]{2,1,0:T(8,128)S(1)}, u32[]{:S(2)}, u32[]{:S(2)}) collective-permute-start(f32[5,16,128]{2,1,0:T(8,128)S(1)} %get-tuple-element.34), channel_id=1, source_target_pairs={{0,2},{2,0},{1,3},{3,1},{4,6},{6,4},{5,7},{7,5},{8,10},{10,8},{9,1... | collective-permute-start | bytes 122888 | tf_op jit(solution)/shard_map/ppermute | solution.py:490
  39.7 0.0 collective-permute-start.11
  39.7 0.9 collective-permute-done.9.z_pair
  40.6 0.4 collective-permute-done.11.z_next
  40.9 1.0 %collective-permute-done.7.x_next = f32[5,16,256]{2,1,0:T(8,128)S(1)} collective-permute-done((f32[5,16,256]{2,1,0:T(8,128)S(1)}, f32[5,16,256]{2,1,0:T(8,128)S(1)}, u32[]{:S(2)}, u32[]{:S(2)}) %collective-permute-start.7) | collective-permute-done | bytes 81952 | tf_op jit(solution)/shard_map/ppermute | solution.py:490
  42.0 5.5 %shard_map.96 = (f32[5,32,16,256]{3,2,1,0:T(8,128)}, f32[128,128]{1,0:T(8,128)S(1)}) custom-call(f32[5]{0:T(128)S(1)} %copy-done.4, s32[3]{0:T(128)S(1)} %copy-done.5, f32[48,128]{1,0:T(8,128)S(1)} %get-tuple-element.24.folded, f32[5,32,16,256]{3,2,1,0:T(8,128)S(1)} %copy-done.1, f32[5,32,16,256]{3,2,1,0:T(8,128)S(1)} %get-tuple-element.30.current, ...), custom_call_target="tpu_custom_call" | custom-call | tf_op jit(solution)/shard_map/pallas_call | solution.py:559
  47.5 11.8 %all_to_all.15.relayed = f32[8,16,128]{2,1,0:T(8,128)S(1)} all-to-all(f32[8,16,128]{2,1,0:T(8,128)S(1)} %bitcast.12), channel_id=1, replica_groups=mesh['zh'=4,'x'=4,'y'=4,'core'=2,'zl'=2] {'y','core'}, dimensions={0} | all-to-all | bytes 131072 | tf_op jit(solution)/shard_map/all_to_all | solution.py:568
  59.2 0.4 shard_map.97
  59.7 10.8 %all_to_all.16 = f32[96,1,128]{2,1,0:T(1,128)S(1)} all-to-all(f32[96,1,128]{2,1,0:T(1,128)S(1)} %bitcast.13), channel_id=1, replica_groups=mesh['zh'=4,'x'=4,'y'=4,'core'=2,'zl'=2] {'x','y','core'}, dimensions={0} | all-to-all | bytes 98304 | tf_op jit(solution)/shard_map/all_to_all | solution.py:515
  70.5 0.7 shard_map.98
  71.1 4.2 %all-to-all-start.2 = ((f32[192,1,128]{2,1,0:T(1,128)}), f32[192,1,128]{2,1,0:T(1,128)S(1)}, u32[]{:S(2)}, u32[]{:S(2)}) async-start(f32[192,1,128]{2,1,0:T(1,128)} %bitcast.5), calls=%async_computation.2 | async-start | bytes 196608 | tf_op jit(solution)/shard_map/all_to_all | solution.py:515
  76.0 6.8 %all-to-all-done.2 = f32[192,1,128]{2,1,0:T(1,128)S(1)} async-done(((f32[192,1,128]{2,1,0:T(1,128)}), f32[192,1,128]{2,1,0:T(1,128)S(1)}, u32[]{:S(2)}, u32[]{:S(2)}) %all-to-all-start.2) | async-done | bytes 98336 | tf_op jit(solution)/shard_map/all_to_all | solution.py:515
  82.8 3.8 %shard_map.99 = (f32[16,64]{1,0:T(8,128)}, f32[16,16]{1,0:T(8,128)}, f32[16,3,1,4,512]{4,3,2,1,0:T(4,128)}) custom-call(s32[1]{0:T(128)S(6)} %copy.12.column_id, f32[192,128]{1,0:T(8,128)S(1)} %bitcast.10, f32[80,6144]{1,0:T(8,128)S(1)} %get-tuple-element.38.joined, f32[8,6144]{1,0:T(8,128)S(1)} %get-tuple-element.40.column), custom_call_target="tpu_custom_call" | custom-call | tf_op jit(solution)/shard_map/pallas_call | solution.py:582
  (15 shorter events, 0.0 us)
Async XLA Ops:
  0.6 1.7 %copy-start = (f32[5,32,16,256]{3,2,1,0:T(8,128)S(1)}, f32[5,32,16,256]{3,2,1,0:T(8,128)}, u32[]{:S(2)}) copy-start(f32[5,32,16,256]{3,2,1,0:T(8,128)} %start.1) | copy-start | bytes 7864324
  2.4 23.3 %copy-start.1 = (f32[5,32,16,256]{3,2,1,0:T(8,128)S(1)}, f32[5,32,16,256]{3,2,1,0:T(8,128)}, u32[]{:S(2)}) copy-start(f32[5,32,16,256]{3,2,1,0:T(8,128)} %start.1) | copy-start | bytes 7864324
  2.4 23.3 %copy-start.4 = (f32[5]{0:T(128)S(1)}, f32[5]{0:T(128)}, u32[]{:S(2)}) copy-start(f32[5]{0:T(128)} %diffusivity.3) | copy-start | bytes 64
  3.7 38.2 %copy-start.5 = (s32[3]{0:T(128)S(1)}, s32[3]{0:T(128)}, u32[]{:S(2)}) copy-start(s32[3]{0:T(128)} %offsets.1) | copy-start | bytes 40
  3.7 21.9 %collective-permute-start.2 = (f32[5,32,256]{2,1,0:T(8,128)S(1)}, f32[5,32,256]{2,1,0:T(8,128)S(1)}, u32[]{:S(2)}, u32[]{:S(2)}) collective-permute-start(f32[5,32,256]{2,1,0:T(8,128)S(1)} %get-tuple-element.27), channel_id=1, source_target_pairs={{0,1},{1,0},{2,3},{3,2},{4,5},{5,4},{6,7},{7,6},{8,9},{9,8},{10,11... | collective-permute-start | bytes 491528 | tf_op jit(solution)/shard_map/ppermute | solution.py:490
  6.3 12.4 %collective-permute-start.4 = (f32[5,16,128]{2,1,0:T(8,128)S(1)}, f32[5,16,128]{2,1,0:T(8,128)S(1)}, u32[]{:S(2)}, u32[]{:S(2)}) collective-permute-start(f32[5,16,128]{2,1,0:T(8,128)S(1)} %get-tuple-element.29), channel_id=1, source_target_pairs={{0,12},{2,6},{4,0},{6,10},{8,4},{10,14},{12,8},{14,2},{1,13},{3,7}... | collective-permute-start | bytes 122888 | tf_op jit(solution)/shard_map/ppermute | solution.py:490
  7.6 18.1 %collective-permute-start = (f32[5,16,256]{2,1,0:T(8,128)S(1)}, f32[5,16,256]{2,1,0:T(8,128)S(1)}, u32[]{:S(2)}, u32[]{:S(2)}) collective-permute-start(f32[5,16,256]{2,1,0:T(8,128)S(1)} %get-tuple-element.25), channel_id=1, source_target_pairs={{0,16},{16,0},{32,48},{48,32},{1,17},{17,1},{33,49},{49,33},{2,18}... | collective-permute-start | bytes 245768 | tf_op jit(solution)/shard_map/ppermute | solution.py:490
  8.8 16.9 %collective-permute-start.1 = (f32[5,16,256]{2,1,0:T(8,128)S(1)}, f32[5,16,256]{2,1,0:T(8,128)S(1)}, u32[]{:S(2)}, u32[]{:S(2)}) collective-permute-start(f32[5,16,256]{2,1,0:T(8,128)S(1)} %get-tuple-element.26), channel_id=1, source_target_pairs={{0,240},{16,32},{32,16},{48,64},{64,48},{80,96},{96,80},{112,128},... | collective-permute-start | bytes 245768 | tf_op jit(solution)/shard_map/ppermute | solution.py:490
  15.4 10.2 %collective-permute-start.3 = (f32[5,16,128]{2,1,0:T(8,128)S(1)}, f32[5,16,128]{2,1,0:T(8,128)S(1)}, u32[]{:S(2)}, u32[]{:S(2)}) collective-permute-start(f32[5,16,128]{2,1,0:T(8,128)S(1)} %get-tuple-element.28), channel_id=1, source_target_pairs={{0,2},{2,0},{1,3},{3,1},{4,6},{6,4},{5,7},{7,5},{8,10},{10,8},{9,1... | collective-permute-start | bytes 122888 | tf_op jit(solution)/shard_map/ppermute | solution.py:490
  18.7 6.9 %collective-permute-start.5 = (f32[5,16,128]{2,1,0:T(8,128)S(1)}, f32[5,16,128]{2,1,0:T(8,128)S(1)}, u32[]{:S(2)}, u32[]{:S(2)}) collective-permute-start(f32[5,16,128]{2,1,0:T(8,128)S(1)} %collective-permute-done.4), channel_id=1, source_target_pairs={{0,2},{2,0},{1,3},{3,1},{4,6},{6,4},{5,7},{7,5},{8,10},{10,8},{9,1... | collective-permute-start | bytes 122888 | tf_op jit(solution)/shard_map/ppermute | solution.py:490
  18.7 1.4 %copy-start.2 = (f32[64,3,1,4,512]{4,3,2,1,0:T(4,128)S(1)}, f32[64,3,1,4,512]{4,3,2,1,0:T(4,128)}, u32[]{:S(2)}) copy-start(f32[64,3,1,4,512]{4,3,2,1,0:T(4,128)} %basis.1) | copy-start | bytes 4718596
  20.1 1.0 %copy-start.3 = (f32[16,3,1,4,512]{4,3,2,1,0:T(4,128)S(1)}, f32[16,3,1,4,512]{4,3,2,1,0:T(4,128)}, u32[]{:S(2)}) copy-start(f32[16,3,1,4,512]{4,3,2,1,0:T(4,128)} %held.1) | copy-start | bytes 1179652
  33.4 8.6 %collective-permute-start.8 = (f32[5,40,256]{2,1,0:T(8,128)S(1)}, f32[5,40,256]{2,1,0:T(8,128)S(1)}, u32[]{:S(2)}, u32[]{:S(2)}) collective-permute-start(f32[5,40,256]{2,1,0:T(8,128)S(1)} %get-tuple-element.33), channel_id=1, source_target_pairs={{0,1},{1,0},{2,3},{3,2},{4,5},{5,4},{6,7},{7,6},{8,9},{9,8},{10,11... | collective-permute-start | bytes 614408 | tf_op jit(solution)/shard_map/ppermute | solution.py:490
  34.2 5.5 %collective-permute-start.10 = (f32[5,16,128]{2,1,0:T(8,128)S(1)}, f32[5,16,128]{2,1,0:T(8,128)S(1)}, u32[]{:S(2)}, u32[]{:S(2)}) collective-permute-start(f32[5,16,128]{2,1,0:T(8,128)S(1)} %get-tuple-element.35), channel_id=1, source_target_pairs={{0,12},{2,6},{4,0},{6,10},{8,4},{10,14},{12,8},{14,2},{1,13},{3,7}... | collective-permute-start | bytes 122888 | tf_op jit(solution)/shard_map/ppermute | solution.py:490
  34.2 6.7 %collective-permute-start.6 = (f32[5,16,256]{2,1,0:T(8,128)S(1)}, f32[5,16,256]{2,1,0:T(8,128)S(1)}, u32[]{:S(2)}, u32[]{:S(2)}) collective-permute-start(f32[5,16,256]{2,1,0:T(8,128)S(1)} %get-tuple-element.31), channel_id=1, source_target_pairs={{0,16},{16,0},{32,48},{48,32},{1,17},{17,1},{33,49},{49,33},{2,18}... | collective-permute-start | bytes 245768 | tf_op jit(solution)/shard_map/ppermute | solution.py:490
  34.2 7.7 %collective-permute-start.7 = (f32[5,16,256]{2,1,0:T(8,128)S(1)}, f32[5,16,256]{2,1,0:T(8,128)S(1)}, u32[]{:S(2)}, u32[]{:S(2)}) collective-permute-start(f32[5,16,256]{2,1,0:T(8,128)S(1)} %get-tuple-element.32), channel_id=1, source_target_pairs={{0,240},{16,32},{32,16},{48,64},{64,48},{80,96},{96,80},{112,128},... | collective-permute-start | bytes 245768 | tf_op jit(solution)/shard_map/ppermute | solution.py:490
  35.9 4.6 %collective-permute-start.9 = (f32[5,16,128]{2,1,0:T(8,128)S(1)}, f32[5,16,128]{2,1,0:T(8,128)S(1)}, u32[]{:S(2)}, u32[]{:S(2)}) collective-permute-start(f32[5,16,128]{2,1,0:T(8,128)S(1)} %get-tuple-element.34), channel_id=1, source_target_pairs={{0,2},{2,0},{1,3},{3,1},{4,6},{6,4},{5,7},{7,5},{8,10},{10,8},{9,1... | collective-permute-start | bytes 122888 | tf_op jit(solution)/shard_map/ppermute | solution.py:490
  39.7 1.2 %collective-permute-start.11 = (f32[5,16,128]{2,1,0:T(8,128)S(1)}, f32[5,16,128]{2,1,0:T(8,128)S(1)}, u32[]{:S(2)}, u32[]{:S(2)}) collective-permute-start(f32[5,16,128]{2,1,0:T(8,128)S(1)} %collective-permute-done.10), channel_id=1, source_target_pairs={{0,2},{2,0},{1,3},{3,1},{4,6},{6,4},{5,7},{7,5},{8,10},{10,8},{9,1... | collective-permute-start | bytes 122888 | tf_op jit(solution)/shard_map/ppermute | solution.py:490
  71.1 11.7 %all-to-all-start.2 = ((f32[192,1,128]{2,1,0:T(1,128)}), f32[192,1,128]{2,1,0:T(1,128)S(1)}, u32[]{:S(2)}, u32[]{:S(2)}) async-start(f32[192,1,128]{2,1,0:T(1,128)} %bitcast.5), calls=%async_computation.2 | async-start | bytes 196608 | tf_op jit(solution)/shard_map/all_to_all | solution.py:515

commit v5 on v4

--- a/solution.py
+++ b/solution.py
@@ -10,7 +10,6 @@
 
 STRIDE = 4
 LANES = 128
-PACK_UNROLL = 4
 BLOCK = 3
 
 time_step = 0.1
@@ -45,20 +44,6 @@
     )
 
 
-def put_row(x, upper, top, bottom, ref, field, half):
-    row = jnp.where(upper, bottom[0:1, :], top[7:8, :])
-    rows = pl.ds(pl.multiple_of(x // 8 * 8, 8), 8)
-    lanes = slice(half * LANES, (half + 1) * LANES)
-    here = iota((8, LANES), 0) == x % 8
-    ref[field, rows, lanes] = jnp.where(here, row, ref[field, rows, lanes])
-
-
-def put_columns(x, lane, value, ref, field, tile, from_end):
-    shift = (x + 1) % LANES if from_end else x
-    rows = slice(tile * 8, tile * 8 + 8)
-    ref[field, rows, :] = jnp.where(lane == x, pltpu.roll(value, shift, 1), ref[field, rows, :])
-
-
 def split(value):
     high = value.astype(jnp.bfloat16)
     value = value - high.astype(jnp.float32)
@@ -76,170 +61,173 @@
     return lax.rem(lax.axis_index(axis), 2) > 0
 
 
-def arrange(x_low, x_high, z_low, z_high, x_pair, x_next, z_pair, z_next):
-    x_odd, second = odd("x"), odd("core")
-    x_pair[...] = jnp.where(x_odd, x_low, x_high)
-    x_next[...] = jnp.where(x_odd, x_high, x_low)
-    z_pair[...] = jnp.where(second, z_low, z_high)
-    z_next[...] = jnp.where(second, z_high, z_low)
-
-
-def pack_kernel(fields, x_pair, x_next, y_row, z_pair, z_next, z_low, z_high):
+def pack(fields, rows, x_pair, x_next, y_row, z_pair, z_next):
     count, cells, height, _ = fields.shape
     upper = lax.axis_index("zl") > 0
-    lane = iota((8, LANES), 1)
-    y_row[...] = jnp.zeros_like(y_row)
-    z_low[...] = jnp.zeros_like(z_low)
-    z_high[...] = jnp.zeros_like(z_high)
-
-    def body(x, carry):
+    lane, sub = iota((8, LANES), 1), iota((8, LANES), 0)
+    keys = [(f, half, tile) for f in range(count) for half in range(2) for tile in range(2)]
+
+    def body(group, faces):
+        faces = dict(zip(keys, faces))
+        y_rows = {}
+        for i in range(8):
+            x = group * 8 + i
+            for f in range(count):
+                for half in range(2):
+                    lanes = slice(half * LANES, (half + 1) * LANES)
+                    values = (fields[f, x, 0:8, lanes], fields[f, x, height - 8 : height, lanes])
+                    row = pltpu.roll(jnp.where(upper, values[0], values[1]), rows[i], 0)
+                    y_rows[f, half] = row if i == 0 else jnp.where(sub == i, row, y_rows[f, half])
+                    shift = (x + half) % LANES
+                    for tile in range(2):
+                        face = pltpu.roll(values[tile], shift, 1)
+                        faces[f, half, tile] = jnp.where(lane == x, face, faces[f, half, tile])
         for f in range(count):
             for half in range(2):
-                lanes = slice(half * LANES, (half + 1) * LANES)
-                bottom = fields[f, x, 0:8, lanes]
-                top = fields[f, x, height - 8 : height, lanes]
-                put_row(x, upper, top, bottom, y_row, f, half)
-                for tile, value in ((0, bottom), (1, top)):
-                    put_columns(x, lane, value, (z_low, z_high)[half], f, tile, half == 1)
-        return carry
-
-    lax.fori_loop(0, cells, body, 0, unroll=PACK_UNROLL)
-    arrange(
-        fields[:, 0], fields[:, cells - 1], z_low[...], z_high[...],
-        x_pair, x_next, z_pair, z_next,
-    )
-
-
-def half_plane(x, half, current, before, after, y_halo, z_before, z_after, diffusivity, upper):
+                place = pl.ds(pl.multiple_of(group * 8, 8), 8)
+                y_row[f, place, half * LANES : (half + 1) * LANES] = y_rows[f, half]
+        return tuple(faces[key] for key in keys)
+
+    zero = jnp.zeros((8, LANES), jnp.float32)
+    faces = lax.fori_loop(0, cells // 8, body, tuple(zero for _ in keys))
+    x_odd, second = odd("x"), odd("core")
+    for (f, half, tile), face in zip(keys, faces):
+        if half == 0:
+            other = faces[keys.index((f, 1, tile))]
+            place = slice(tile * 8, tile * 8 + 8)
+            z_pair[f, place, :] = jnp.where(second, face, other)
+            z_next[f, place, :] = jnp.where(second, other, face)
+    low, high = fields[:, 0], fields[:, cells - 1]
+    x_pair[...] = jnp.where(x_odd, low, high)
+    x_next[...] = jnp.where(x_odd, high, low)
+
+
+def row_shifts(upper):
+    return [(i + jnp.where(upper, 0, 1)) % 8 for i in range(8)]
+
+
+def pack_kernel(fields, x_pair, x_next, y_row, z_pair, z_next):
+    rows = row_shifts(lax.axis_index("zl") > 0)
+    pack(fields, rows, x_pair, x_next, y_row, z_pair, z_next)
+
+
+def plane(x, current, before, after, y_low, y_high, z_before, z_after, diffusivity):
     count = current.shape[0]
-    lane = iota((8, LANES), 1)
-    sub = iota((8, LANES), 0)
+    lane, sub = iota((8, LANES), 1), iota((8, LANES), 0)
     first_lane, last_lane = lane == 0, lane == LANES - 1
     first_sub, last_sub = sub == 0, sub == 7
-    below = jnp.where(upper, 1.0, 0.0)
-    above = 1.0 - below
-    row_shift = (jnp.where(upper, 8, 15) - x % 8) % 8
     tile_rows = (slice(0, 8), slice(8, 16))
-    lanes = slice(half * LANES, (half + 1) * LANES)
-    other_lanes = slice((1 - half) * LANES, (2 - half) * LANES)
+    half_lanes = (slice(0, LANES), slice(LANES, 2 * LANES))
+    quarters = [(tile, half) for tile in range(2) for half in range(2)]
+    group = pl.ds(pl.multiple_of(x // 8 * 8, 8), 8)
+    to_first, to_last = (8 - x % 8) % 8, 7 - x % 8
     centre = {
-        (f, tile): current[f, x, tile_rows[tile], lanes] for f in range(count) for tile in range(2)
+        (f, tile, half): current[f, x, tile_rows[tile], half_lanes[half]]
+        for f in range(count)
+        for tile, half in quarters
     }
-    speeds = [[0.5 * centre[f, tile] for f in range(3)] for tile in range(2)]
-    strain = [0.0, 0.0]
-    laplace, rest = {}, {}
+    speeds = {
+        (f, *at): (0.5 * time_step) * centre[f, *at] for f in range(3) for at in quarters
+    }
+    strain = dict.fromkeys(quarters, 0.0)
+    laplace, advect = {}, {}
     for f in range(count):
-        row = y_halo[f, pl.ds(pl.multiple_of(x // 8 * 8, 8), 8), lanes]
-        row = pltpu.roll(row, row_shift, 0)
-        down = [pltpu.roll(centre[f, tile], 1, 0) for tile in range(2)]
-        up = [pltpu.roll(centre[f, tile], 7, 0) for tile in range(2)]
-        y_minus = (
-            jnp.where(first_sub, row * below, down[0]),
-            jnp.where(first_sub, down[0], down[1]),
-        )
-        y_plus = (
-            jnp.where(last_sub, up[1], up[0]),
-            jnp.where(last_sub, row * above, up[1]),
-        )
+        y_minus, y_plus, z_minus, z_plus = {}, {}, {}, {}
+        for half in range(2):
+            lanes = half_lanes[half]
+            low = pltpu.roll(y_low[f, group, lanes], to_first, 0)
+            high = pltpu.roll(y_high[f, group, lanes], to_last, 0)
+            down = [pltpu.roll(centre[f, tile, half], 1, 0) for tile in range(2)]
+            up = [pltpu.roll(centre[f, tile, half], 7, 0) for tile in range(2)]
+            y_minus[0, half] = jnp.where(first_sub, low, down[0])
+            y_minus[1, half] = jnp.where(first_sub, down[0], down[1])
+            y_plus[0, half] = jnp.where(last_sub, up[1], up[0])
+            y_plus[1, half] = jnp.where(last_sub, high, up[1])
         for tile in range(2):
-            rows = tile_rows[tile]
-            value = centre[f, tile]
-            other = current[f, x, rows, other_lanes]
-            if half == 0:
-                edge_low = pltpu.roll(z_before[f, rows, :], (LANES - x) % LANES, 1)
-                edge_high = pltpu.roll(other, LANES - 1, 1)
-            else:
-                edge_low = pltpu.roll(other, 1, 1)
-                edge_high = pltpu.roll(z_after[f, rows, :], LANES - 1 - x, 1)
-            z_minus = jnp.where(first_lane, edge_low, pltpu.roll(value, 1, 1))
-            z_plus = jnp.where(last_lane, edge_high, pltpu.roll(value, LANES - 1, 1))
+            low = pltpu.roll(z_before[f, tile_rows[tile], :], (LANES - x) % LANES, 1)
+            high = pltpu.roll(z_after[f, tile_rows[tile], :], LANES - 1 - x, 1)
+            right = [pltpu.roll(centre[f, tile, half], 1, 1) for half in range(2)]
+            left = [pltpu.roll(centre[f, tile, half], LANES - 1, 1) for half in range(2)]
+            z_minus[tile, 0] = jnp.where(first_lane, low, right[0])
+            z_minus[tile, 1] = jnp.where(first_lane, right[0], right[1])
+            z_plus[tile, 0] = jnp.where(last_lane, left[1], left[0])
+            z_plus[tile, 1] = jnp.where(last_lane, high, left[1])
+        for at in quarters:
+            rows, lanes = tile_rows[at[0]], half_lanes[at[1]]
             x_minus, x_plus = before(f, rows, lanes), after(f, rows, lanes)
             slope_x = x_plus - x_minus
-            slope_y = y_plus[tile] - y_minus[tile]
-            slope_z = z_plus - z_minus
-            laplace[f, tile] = (
+            slope_y = y_plus[at] - y_minus[at]
+            slope_z = z_plus[at] - z_minus[at]
+            laplace[f, *at] = (
                 (x_plus + x_minus)
-                + (y_plus[tile] + y_minus[tile])
-                + (z_plus + z_minus)
-                - 6.0 * value
+                + (y_plus[at] + y_minus[at])
+                + (z_plus[at] + z_minus[at])
+                - 6.0 * centre[f, *at]
             )
             if f < 3:
-                strain[tile] = strain[tile] + (
+                strain[at] = strain[at] + (
                     slope_x * slope_x + slope_y * slope_y + slope_z * slope_z
                 )
-            advect = (
-                speeds[tile][0] * slope_x + speeds[tile][1] * slope_y + speeds[tile][2] * slope_z
+            advect[f, *at] = (
+                speeds[0, *at] * slope_x + speeds[1, *at] * slope_y + speeds[2, *at] * slope_z
             )
-            rest[f, tile] = diffusivity[f] * laplace[f, tile] - advect
-    rates = {}
-    for tile in range(2):
-        eddy = smagorinsky * jnp.sqrt(0.25 * strain[tile])
+    steps = {}
+    for at in quarters:
+        eddy = (0.5 * time_step * smagorinsky) * jnp.sqrt(strain[at])
         for f in range(count):
-            rates[f, tile] = eddy * laplace[f, tile] + rest[f, tile]
-    return centre, rates
-
-
-def planes(current, halos, diffusivity, finish, after_three=lambda step: None):
-    x_pair, x_next, y_halo, z_pair, z_next, z_before, z_after = halos
-    cells = current.shape[1]
-    upper = lax.axis_index("zl") > 0
-    x_odd, second = odd("x"), odd("core")
-    z_before[...] = jnp.where(second, z_pair[...], z_next[...])
-    z_after[...] = jnp.where(second, z_next[...], z_pair[...])
-
-    def one(x, before, after):
-        for half in range(2):
-            finish(
-                x,
-                half,
-                *half_plane(
-                    x, half, current, before, after, y_halo, z_before, z_after, diffusivity, upper
-                ),
-            )
-
-    def inside(offset, x):
-        return lambda f, rows, lanes: current[f, x + offset, rows, lanes]
-
-    def outside(here, there):
+            mixing = time_step * diffusivity[f] + eddy
+            steps[f, *at] = mixing * laplace[f, *at] - advect[f, *at]
+    return centre, steps
+
+
+class Planes:
+    def __init__(self, current, halos, diffusivity, finish):
+        self.x_pair, self.x_next, y_halo, z_pair, z_next, y_low, y_high, z_before, z_after = halos
+        self.current, self.finish = current, finish
+        self.rest = (y_low, y_high, z_before, z_after, diffusivity)
+        cells = current.shape[1]
+        upper, second = lax.axis_index("zl") > 0, odd("core")
+        z_before[...] = jnp.where(second, z_pair[...], z_next[...])
+        z_after[...] = jnp.where(second, z_next[...], z_pair[...])
+        y_low[...] = jnp.where(upper, y_halo[:, :cells], 0.0)
+        y_high[...] = jnp.where(upper, 0.0, y_halo[:, :cells])
+
+    def one(self, x, before, after):
+        self.finish(x, *plane(x, self.current, before, after, *self.rest))
+
+    def inside(self, x):
+        return lambda f, rows, lanes: self.current[f, x, rows, lanes]
+
+    def outside(self, here, there):
+        x_odd = odd("x")
         return lambda f, rows, lanes: jnp.where(x_odd, here[f, rows, lanes], there[f, rows, lanes])
 
-    one(0, outside(x_pair, x_next), inside(1, 0))
-    blocks = (cells - 2) // BLOCK
-
-    def body(step, carry):
-        for i in range(BLOCK):
-            x = step * BLOCK + 1 + i
-            one(x, inside(-1, x), inside(1, x))
-        after_three(step)
-        return carry
-
-    lax.fori_loop(0, blocks, body, 0)
-    one(cells - 1, inside(-1, cells - 1), outside(x_next, x_pair))
-
-
-def gram_kernel(basis, held, joined, folded, semaphores):
+    def ends(self):
+        last = self.current.shape[1] - 1
+        self.one(0, self.outside(self.x_pair, self.x_next), self.inside(1))
+        self.one(last, self.inside(last - 1), self.outside(self.x_next, self.x_pair))
+
+    def interior(self, after_block=lambda step: None):
+        def body(step, carry):
+            for i in range(BLOCK):
+                x = step * BLOCK + 1 + i
+                self.one(x, self.inside(x - 1), self.inside(x + 1))
+            after_block(step)
+            return carry
+
+        lax.fori_loop(0, (self.current.shape[1] - 2) // BLOCK, body, 0)
+
+
+def gram_kernel(basis, held, joined, folded):
     rank, _, _, levels, points = basis.shape
     total = rank + held.shape[0]
-    copies = []
     for chunk in range(3 * levels):
         lanes = slice(chunk * points, (chunk + 1) * points)
-        for i, (source, rows) in enumerate(
-            ((basis, slice(0, rank)), (held, slice(rank, total)))
-        ):
-            copies.append(
-                pltpu.make_async_copy(
-                    source.at[:, chunk // levels, 0, chunk % levels, :],
-                    joined.at[rows, lanes],
-                    semaphores.at[2 * chunk + i],
-                )
-            )
-    for copy in copies:
-        copy.start()
+        joined[0:rank, lanes] = basis[:, chunk // levels, 0, chunk % levels, :]
+        joined[rank:total, lanes] = held[:, chunk // levels, 0, chunk % levels, :]
     sums = jnp.zeros((3 * total, total), jnp.float32)
     squares = jnp.zeros((total, total), jnp.float32)
     for chunk in range(3 * levels):
-        copies[2 * chunk].wait()
-        copies[2 * chunk + 1].wait()
         high, middle, low = split(joined[:, chunk * points : (chunk + 1) * points])
         sums += matmul(jnp.concatenate([high, middle, low], axis=0), high, 1)
         squares += matmul(middle, middle, 1)
@@ -260,79 +248,114 @@
 
 def first_kernel(
     diffusivity, folded, current, x_pair_in, x_next_in, y_halo, z_pair_in, z_next_in,
-    first, x_pair, x_next, y_row, z_pair, z_next, z_before, z_after, z_low, z_high,
+    first, x_pair, x_next, y_row, z_pair, z_next, *edges,
 ):
     count, cells = current.shape[:2]
     upper = lax.axis_index("zl") > 0
-    lane = iota((8, LANES), 1)
-    y_row[...] = jnp.zeros_like(y_row)
-    z_low[...] = jnp.zeros_like(z_low)
-    z_high[...] = jnp.zeros_like(z_high)
+    y_row[:, cells:, :] = jnp.zeros((count, y_row.shape[1] - cells, y_row.shape[2]), jnp.float32)
     for group in range(3):
         lanes = slice(group % 2 * LANES, (group % 2 + 1) * LANES)
         y_row[group // 2, cells:, lanes] = jnp.where(
             upper, folded[group * 8 : group * 8 + 8], folded[group * 8 + 24 : group * 8 + 32]
         )
 
-    def finish(x, half, centre, rates):
-        lanes = slice(half * LANES, (half + 1) * LANES)
-        for f in range(count):
-            new = []
-            for tile in range(2):
-                value = centre[f, tile] + time_step * rates[f, tile]
-                new.append(value)
-                first[f, x, tile * 8 : tile * 8 + 8, lanes] = value
-                put_columns(x, lane, value, (z_low, z_high)[half], f, tile, half == 1)
-            put_row(x, upper, new[1], new[0], y_row, f, half)
-
-    halos = (x_pair_in, x_next_in, y_halo, z_pair_in, z_next_in, z_before, z_after)
-    planes(current, halos, diffusivity, finish)
-    arrange(
-        first[:, 0], first[:, cells - 1], z_low[...], z_high[...],
-        x_pair, x_next, z_pair, z_next,
-    )
-
-
-def second_kernel(
+    def finish(x, centre, steps):
+        for (f, tile, half), value in centre.items():
+            first[f, x, tile * 8 : tile * 8 + 8, half * LANES : (half + 1) * LANES] = (
+                value + steps[f, tile, half]
+            )
+
+    halos = (x_pair_in, x_next_in, y_halo, z_pair_in, z_next_in, *edges)
+    planes = Planes(current, halos, diffusivity, finish)
+    planes.ends()
+    planes.interior()
+    pack(first, row_shifts(upper), x_pair, x_next, y_row, z_pair, z_next)
+
+
+def pick(picked, plane, column, keep, shift):
+    for f in range(3):
+        for tile in range(2):
+            rows = pltpu.roll(plane(f, slice(tile * 8, tile * 8 + 8)), shift, 0)
+            for part in range(2):
+                row = column * 16 + f * 4 + tile * 2 + part
+                value = rows[part * STRIDE : part * STRIDE + 1, :]
+                if keep is not None:
+                    value = jnp.where(keep, picked[row : row + 1, :], value)
+                picked[row : row + 1, :] = value
+
+
+def average(start, value, step):
+    return 0.5 * (start + value + step)
+
+
+def inner_kernel(
+    diffusivity, offsets, start, current, y_halo, z_pair, z_next,
+    target, picked, y_low, y_high, z_before, z_after, result, semaphores,
+):
+    cells = current.shape[1]
+    blocks = (cells - 2) // BLOCK
+
+    def finish(x, centre, steps):
+        for (f, tile, half), value in centre.items():
+            at = (f, x, slice(tile * 8, tile * 8 + 8), slice(half * LANES, (half + 1) * LANES))
+            result[at] = average(start[at], value, steps[f, tile, half])
+
+    def copied(step):
+        part = pl.ds(step * BLOCK + 1, BLOCK)
+        return pltpu.make_async_copy(result.at[:, part], target.at[:, part], semaphores.at[step])
+
+    halos = (None, None, y_halo, z_pair, z_next, y_low, y_high, z_before, z_after)
+    Planes(current, halos, diffusivity, finish).interior(lambda step: copied(step).start())
+    picked[...] = jnp.zeros_like(picked)
+    shift = (8 - offsets[1]) % 8
+    for column in range(cells // STRIDE):
+        x = jnp.clip(column * STRIDE + offsets[2], 1, cells - 2)
+        pick(picked, lambda f, rows: result[f, x, rows, :], column, None, shift)
+
+    def settle(step, carry):
+        copied(step).wait()
+        return carry
+
+    lax.fori_loop(0, blocks, settle, 0)
+
+
+def outer_kernel(
     diffusivity, offsets, folded, start, current, x_pair, x_next, y_halo, z_pair, z_next,
-    target, snapshot, z_before, z_after, picked, result, semaphores,
+    picked_in, target_in, target, snapshot, y_low, y_high, z_before, z_after, picked, result,
+    semaphores,
 ):
-    count, cells, height, width = current.shape
-    blocks = (cells - 2) // BLOCK
-
-    def finish(x, half, centre, rates):
-        lanes = slice(half * LANES, (half + 1) * LANES)
-        for f in range(count):
-            for tile in range(2):
-                rows = slice(tile * 8, tile * 8 + 8)
-                result[f, x, rows, lanes] = 0.5 * (
-                    start[f, x, rows, lanes] + centre[f, tile] + time_step * rates[f, tile]
-                )
-
-    def copied(first, planes_count, index):
-        part = pl.ds(first, planes_count)
-        return pltpu.make_async_copy(result.at[:, part], target.at[:, part], semaphores.at[index])
-
-    def send(step):
-        copied(step * BLOCK + 1, BLOCK, step).start()
-
-    halos = (x_pair, x_next, y_halo, z_pair, z_next, z_before, z_after)
-    planes(current, halos, diffusivity, finish, send)
-    copied(0, 1, blocks).start()
-    copied(cells - 1, 1, blocks + 1).start()
-    levels = height // STRIDE
-    picked[...] = jnp.zeros_like(picked)
-    for column in range(cells // STRIDE):
-        for f in range(3):
-            for tile in range(2):
-                plane = result[f, column * STRIDE + offsets[2], tile * 8 : tile * 8 + 8, :]
-                plane = pltpu.roll(plane, (8 - offsets[1]) % 8, 0)
-                for part in range(2):
-                    row = column * 16 + f * levels + tile * 2 + part
-                    picked[row : row + 1, :] = plane[part * STRIDE : part * STRIDE + 1, :]
+    _, cells, _, width = current.shape
+
+    def finish(x, centre, steps):
+        slot = 0 if x == 0 else 1
+        for (f, tile, half), value in centre.items():
+            rows, lanes = slice(tile * 8, tile * 8 + 8), slice(half * LANES, (half + 1) * LANES)
+            result[f, slot, rows, lanes] = average(
+                start[f, x, rows, lanes], value, steps[f, tile, half]
+            )
+
+    halos = (x_pair, x_next, y_halo, z_pair, z_next, y_low, y_high, z_before, z_after)
+    Planes(current, halos, diffusivity, finish).ends()
+    copies = [
+        pltpu.make_async_copy(
+            result.at[:, pl.ds(slot, 1)], target.at[:, pl.ds(x, 1)], semaphores.at[slot]
+        )
+        for slot, x in ((0, 0), (1, cells - 1))
+    ]
+    for copy in copies:
+        copy.start()
+    picked[...] = picked_in[...]
+    shift = (8 - offsets[1]) % 8
+    pick(picked, lambda f, rows: result[f, 0, rows, :], 0, offsets[2] > 0, shift)
+    pick(
+        picked, lambda f, rows: result[f, 1, rows, :], cells // STRIDE - 1,
+        offsets[2] < STRIDE - 1, shift,
+    )
     points = width // STRIDE
     choose = iota((width, LANES), 0) == STRIDE * (iota((width, LANES), 1) % points) + offsets[0]
-    snapshot[...] = dot(picked[...], choose.astype(jnp.float32), 1, 0)
+    choose = choose.astype(jnp.float32).astype(jnp.bfloat16)
+    high, middle, low = split(picked[...])
+    snapshot[...] = matmul(high, choose, 0) + matmul(middle, choose, 0) + matmul(low, choose, 0)
     upper = lax.axis_index("zl") > 0
     for group in range(3):
         lanes = slice(group % 2 * LANES, (group % 2 + 1) * LANES)
@@ -343,14 +366,8 @@
         for column in range(cells // STRIDE):
             row = column * 16 + 12 + group
             snapshot[row : row + 1, :] = kept[column : column + 1]
-
-    def settle(step, carry):
-        copied(step * BLOCK + 1, BLOCK, step).wait()
-        return carry
-
-    lax.fori_loop(0, blocks, settle, 0)
-    copied(0, 1, blocks).wait()
-    copied(cells - 1, 1, blocks + 1).wait()
+    for copy in copies:
+        copy.wait()
 
 
 def product_kernel(relayed, joined, message, column, partial):
@@ -533,18 +550,19 @@
         struct(count, height, LANES),
         struct(count, height, LANES),
     )
+    wall = pltpu.VMEM((count, cells, width), jnp.float32)
     edge = pltpu.VMEM((count, height, LANES), jnp.float32)
+    busy = pl.CostEstimate(flops=2 * 10**7, bytes_accessed=2 * 10**7, transcendentals=0)
 
     packed = pl.pallas_call(
         pack_kernel, in_specs=[VMEM], out_specs=[VMEM] * 5, out_shape=faces,
-        scratch_shapes=[edge] * 2, compiler_params=params(16),
+        compiler_params=params(16),
     )(fields)
     halos = exchange(packed)
 
     joined, folded = pl.pallas_call(
-        gram_kernel, in_specs=[ANY] * 2, out_specs=[VMEM] * 2,
+        gram_kernel, in_specs=[VMEM] * 2, out_specs=[VMEM] * 2,
         out_shape=(struct(total, length), struct(48, LANES)),
-        scratch_shapes=[pltpu.SemaphoreType.DMA((2 * chunks,))],
         compiler_params=params(16),
     )(pod_basis, held_block)
 
@@ -552,19 +570,33 @@
         first_kernel, in_specs=[SMEM] + [VMEM] * 7, out_specs=[VMEM] * 6,
         out_shape=(struct(*fields.shape),) + faces[:2] + (struct(count, cells + 8, width),)
         + faces[3:],
-        scratch_shapes=[edge] * 4, compiler_params=params(24),
+        scratch_shapes=[wall, wall, edge, edge], compiler_params=params(24),
     )(diffusivity, folded, fields, *halos)
     halos = exchange(packed)
 
+    x_pair, x_next, *halos = halos
+    sides = [wall, wall, edge, edge]
+    fields_out, picked = pl.pallas_call(
+        inner_kernel, in_specs=[SMEM] * 2 + [VMEM] * 5, out_specs=[ANY, VMEM],
+        out_shape=(struct(*fields.shape), struct(LANES, width)),
+        scratch_shapes=sides + [
+            pltpu.VMEM(fields.shape, jnp.float32), pltpu.SemaphoreType.DMA((10,)),
+        ],
+        cost_estimate=busy, compiler_params=params(24),
+    )(diffusivity, subsample_offsets, fields, first, *halos)
     fields_out, snapshot = pl.pallas_call(
-        second_kernel, in_specs=[SMEM] * 2 + [VMEM] * 8, out_specs=[ANY, VMEM],
+        outer_kernel, in_specs=[SMEM] * 2 + [VMEM] * 9 + [ANY], out_specs=[ANY, VMEM],
         out_shape=(struct(*fields.shape), struct(LANES, LANES)),
-        scratch_shapes=[
-            edge, edge, pltpu.VMEM((LANES, width), jnp.float32),
-            pltpu.VMEM(fields.shape, jnp.float32), pltpu.SemaphoreType.DMA((12,)),
+        scratch_shapes=sides + [
+            pltpu.VMEM((LANES, width), jnp.float32),
+            pltpu.VMEM((count, 2, height, width), jnp.float32),
+            pltpu.SemaphoreType.DMA((2,)),
         ],
-        compiler_params=params(24),
-    )(diffusivity, subsample_offsets, folded, fields, first, *halos)
+        input_output_aliases={11: 0}, compiler_params=params(24),
+    )(
+        diffusivity, subsample_offsets, folded, fields, first, x_pair, x_next, *halos,
+        picked, fields_out,
+    )
     relayed = lax.all_to_all(snapshot.reshape(8, 16, LANES), ("y", "core"), 0, 0, tiled=True)
 
     message, column = pl.pallas_call(

time: 87 us -> 78.7 us (0.905)
  Pallas kernels: 23.9 us -> 18.7 us
  blocking collectives: 22.6 us -> 19.6 us
    all_to_all x1, blocking collectives: 11.8 us -> 8.75 us  [on_device(): lax.all_to_all(snapshot.reshape(8, 16, LANES), ('y', 'core'), 0, 0, tiled...]
    pallas_call x1, Pallas kernels: 7.71 us -> 5.04 us  [on_device(): pl.pallas_call(first_kernel, in_specs=[SMEM] + [VMEM] * 7, out_specs=[VME...]
    pallas_call x2 -> x3, Pallas kernels: 9.99 us -> 7.82 us  [the longest x1 4.79 us: on_device(): pl.pallas_call(inner_kernel, in_specs=[SMEM] * 2 + [VMEM] * 5, out_specs=...]
  transfers between devices with their start and end apart: 13 -> 13, of which waited for: 4 -> 4; matrix products, arithmetic and copies ran while one was open for 0% -> 0% of each run, Pallas kernels for 5% -> 8%
where the time goes in v5:
time: 78.7 us; the launch traced here: 78.4 us
  starting transfers between devices  26.2 us (33%)
  blocking collectives  19.6 us (25%)
  Pallas kernels  18.7 us (24%)
  waiting for transfers between devices  8.32 us (11%)
  local copies, waits for them, and re-layouts  4.15 us (5%)
  between operations  1.43 us (2%)
    ppermute x12, starting transfers between devices, moved(): return lax.ppermute(value, axes, pairs)  21.6 us
    all_to_all x1, blocking collectives, everyone(): lax.all_to_all(message.reshape(rows, 1, LANES), axes, 0, 0, tiled=True)  10.8 us
    all_to_all x1, blocking collectives, on_device(): lax.all_to_all(snapshot.reshape(8, 16, LANES), ('y', 'core'), 0, 0, tiled...  8.75 us
    all_to_all x1, waiting for transfers between devices, everyone(): lax.all_to_all(message.reshape(rows, 1, LANES), axes, 0, 0, tiled=True)  6.81 us
    pallas_call x1, Pallas kernels, on_device(): pl.pallas_call(first_kernel, in_specs=[SMEM] + [VMEM] * 7, out_specs=[VME...  5.04 us
    pallas_call x1, Pallas kernels, on_device(): pl.pallas_call(inner_kernel, in_specs=[SMEM] * 2 + [VMEM] * 5, out_specs=...  4.79 us
    all_to_all x1, starting transfers between devices, everyone(): lax.all_to_all(message.reshape(rows, 1, LANES), axes, 0, 0, tiled=True)  4.59 us
    unnamed x12, local copies, waits for them, and re-layouts  4.15 us
  transfers between devices with their start and end apart: 13, of which 4 were waited for; matrix products, arithmetic and copies ran while one was open for 0% of the time, Pallas kernels for 8%

profile of v5, /device:TPU:1, one launch (start us, length us, event | category | flops | bytes accessed | tf_op | source)
XLA Modules:
  0.0 78.4 jit_solution(10911131899626800013)
XLA Ops:
  0.6 1.7 %copy-done = f32[5,32,16,256]{3,2,1,0:T(8,128)S(1)} copy-done((f32[5,32,16,256]{3,2,1,0:T(8,128)S(1)}, f32[5,32,16,256]{3,2,1,0:T(8,128)}, u32[]{:S(2)}) %copy-start) | copy-done | bytes 2621464
  2.4 1.0 %shard_map.94 = (f32[5,16,256]{2,1,0:T(8,128)S(1)}, f32[5,16,256]{2,1,0:T(8,128)S(1)}, f32[5,32,256]{2,1,0:T(8,128)S(1)}, f32[5,16,128]{2,1,0:T(8,128)S(1)}, f32[5,16,128]{2,1,0:T(8,128)S(1)}) custom-call(f32[5,32,16,256]{3,2,1,0:T(8,128)S(1)} %copy-done), custom_call_target="tpu_custom_call" | custom-call | tf_op jit(solution)/shard_map/pallas_call | solution.py:557
  3.4 0.0 copy-start.5
  3.4 2.6 %collective-permute-start.2 = (f32[5,32,256]{2,1,0:T(8,128)S(1)}, f32[5,32,256]{2,1,0:T(8,128)S(1)}, u32[]{:S(2)}, u32[]{:S(2)}) collective-permute-start(f32[5,32,256]{2,1,0:T(8,128)S(1)} %get-tuple-element.29), channel_id=1, source_target_pairs={{0,1},{1,0},{2,3},{3,2},{4,5},{5,4},{6,7},{7,6},{8,9},{9,8},{10,11... | collective-permute-start | bytes 491528 | tf_op jit(solution)/shard_map/ppermute | solution.py:507
  5.9 1.3 %collective-permute-start.4 = (f32[5,16,128]{2,1,0:T(8,128)S(1)}, f32[5,16,128]{2,1,0:T(8,128)S(1)}, u32[]{:S(2)}, u32[]{:S(2)}) collective-permute-start(f32[5,16,128]{2,1,0:T(8,128)S(1)} %get-tuple-element.31), channel_id=1, source_target_pairs={{0,12},{2,6},{4,0},{6,10},{8,4},{10,14},{12,8},{14,2},{1,13},{3,7}... | collective-permute-start | bytes 122888 | tf_op jit(solution)/shard_map/ppermute | solution.py:507
  7.2 1.2 %collective-permute-start = (f32[5,16,256]{2,1,0:T(8,128)S(1)}, f32[5,16,256]{2,1,0:T(8,128)S(1)}, u32[]{:S(2)}, u32[]{:S(2)}) collective-permute-start(f32[5,16,256]{2,1,0:T(8,128)S(1)} %get-tuple-element.27), channel_id=1, source_target_pairs={{0,16},{16,0},{32,48},{48,32},{1,17},{17,1},{33,49},{49,33},{2,18}... | collective-permute-start | bytes 245768 | tf_op jit(solution)/shard_map/ppermute | solution.py:507
  8.5 6.7 %collective-permute-start.1 = (f32[5,16,256]{2,1,0:T(8,128)S(1)}, f32[5,16,256]{2,1,0:T(8,128)S(1)}, u32[]{:S(2)}, u32[]{:S(2)}) collective-permute-start(f32[5,16,256]{2,1,0:T(8,128)S(1)} %get-tuple-element.28), channel_id=1, source_target_pairs={{0,240},{16,32},{32,16},{48,64},{64,48},{80,96},{96,80},{112,128},... | collective-permute-start | bytes 245768 | tf_op jit(solution)/shard_map/ppermute | solution.py:507
  15.1 3.2 %collective-permute-start.3 = (f32[5,16,128]{2,1,0:T(8,128)S(1)}, f32[5,16,128]{2,1,0:T(8,128)S(1)}, u32[]{:S(2)}, u32[]{:S(2)}) collective-permute-start(f32[5,16,128]{2,1,0:T(8,128)S(1)} %get-tuple-element.30), channel_id=1, source_target_pairs={{0,2},{2,0},{1,3},{3,1},{4,6},{6,4},{5,7},{7,5},{8,10},{10,8},{9,1... | collective-permute-start | bytes 122888 | tf_op jit(solution)/shard_map/ppermute | solution.py:507
  18.3 0.0 collective-permute-done.4
  18.3 0.0 collective-permute-start.5
  18.4 1.4 %copy-done.2 = f32[64,3,1,4,512]{4,3,2,1,0:T(4,128)S(1)} copy-done((f32[64,3,1,4,512]{4,3,2,1,0:T(4,128)S(1)}, f32[64,3,1,4,512]{4,3,2,1,0:T(4,128)}, u32[]{:S(2)}) %copy-start.2) | copy-done | bytes 1572888
  19.8 1.0 %copy-done.3 = f32[16,3,1,4,512]{4,3,2,1,0:T(4,128)S(1)} copy-done((f32[16,3,1,4,512]{4,3,2,1,0:T(4,128)S(1)}, f32[16,3,1,4,512]{4,3,2,1,0:T(4,128)}, u32[]{:S(2)}) %copy-start.3) | copy-done | bytes 393240
  20.8 1.5 %shard_map.93 = (f32[80,6144]{1,0:T(8,128)S(1)}, f32[48,128]{1,0:T(8,128)S(1)}) custom-call(f32[64,3,1,4,512]{4,3,2,1,0:T(4,128)S(1)} %copy-done.2, f32[16,3,1,4,512]{4,3,2,1,0:T(4,128)S(1)} %copy-done.3), custom_call_target="tpu_custom_call" | custom-call | tf_op jit(solution)/shard_map/pallas_call | solution.py:563
  22.3 0.0 collective-permute-done.x_pair_in
  22.3 5.0 %shard_map.95 = (f32[5,32,16,256]{3,2,1,0:T(8,128)S(1)}, f32[5,16,256]{2,1,0:T(8,128)S(1)}, f32[5,16,256]{2,1,0:T(8,128)S(1)}, f32[5,40,256]{2,1,0:T(8,128)S(1)}...) custom-call(f32[5]{0:T(128)S(1)} %copy-done.4, f32[48,128]{1,0:T(8,128)S(1)} %get-tuple-element.26.folded, ...), custom_call_target="tpu_custom_call" | custom-call | tf_op jit(solution)/shard_map/pallas_call | solution.py:569
  27.4 0.8 %collective-permute-start.8 = (f32[5,40,256]{2,1,0:T(8,128)S(1)}, f32[5,40,256]{2,1,0:T(8,128)S(1)}, u32[]{:S(2)}, u32[]{:S(2)}) collective-permute-start(f32[5,40,256]{2,1,0:T(8,128)S(1)} %get-tuple-element.35), channel_id=1, source_target_pairs={{0,1},{1,0},{2,3},{3,2},{4,5},{5,4},{6,7},{7,6},{8,9},{9,8},{10,11... | collective-permute-start | bytes 614408 | tf_op jit(solution)/shard_map/ppermute | solution.py:507
  28.2 0.0 collective-permute-start.10
  28.2 3.4 %collective-permute-start.7 = (f32[5,16,256]{2,1,0:T(8,128)S(1)}, f32[5,16,256]{2,1,0:T(8,128)S(1)}, u32[]{:S(2)}, u32[]{:S(2)}) collective-permute-start(f32[5,16,256]{2,1,0:T(8,128)S(1)} %get-tuple-element.34), channel_id=1, source_target_pairs={{0,240},{16,32},{32,16},{48,64},{64,48},{80,96},{96,80},{112,128},... | collective-permute-start | bytes 245768 | tf_op jit(solution)/shard_map/ppermute | solution.py:507
  31.6 2.4 %collective-permute-start.9 = (f32[5,16,128]{2,1,0:T(8,128)S(1)}, f32[5,16,128]{2,1,0:T(8,128)S(1)}, u32[]{:S(2)}, u32[]{:S(2)}) collective-permute-start(f32[5,16,128]{2,1,0:T(8,128)S(1)} %get-tuple-element.36), channel_id=1, source_target_pairs={{0,2},{2,0},{1,3},{3,1},{4,6},{6,4},{5,7},{7,5},{8,10},{10,8},{9,1... | collective-permute-start | bytes 122888 | tf_op jit(solution)/shard_map/ppermute | solution.py:507
  34.0 0.0 collective-permute-start.11
  34.0 0.9 %collective-permute-done.9.z_pair = f32[5,16,128]{2,1,0:T(8,128)S(1)} collective-permute-done((f32[5,16,128]{2,1,0:T(8,128)S(1)}, f32[5,16,128]{2,1,0:T(8,128)S(1)}, u32[]{:S(2)}, u32[]{:S(2)}) %collective-permute-start.9) | collective-permute-done | bytes 40992 | tf_op jit(solution)/shard_map/ppermute | solution.py:507
  34.9 0.4 collective-permute-done.11.z_next
  35.2 0.3 collective-permute-done.8.y_halo
  35.5 4.8 %shard_map.96 = (f32[5,32,16,256]{3,2,1,0:T(8,128)}, f32[128,256]{1,0:T(8,128)S(1)}) custom-call(f32[5]{0:T(128)S(1)} %copy-done.4, s32[3]{0:T(128)S(1)} %copy-done.5, f32[5,32,16,256]{3,2,1,0:T(8,128)S(1)} %copy-done.1, f32[5,32,16,256]{3,2,1,0:T(8,128)S(1)} %get-tuple-element.32.current, f32[5,40,256]{2,1,0:T(8,128)S(1)} %collective-permute-done.8.y_halo, ...), custom_call_target="tpu_custom_call" | custom-call | flops 20000000 | bytes 20000000 | tf_op jit(solution)/shard_map/pallas_call | solution.py:579
  40.3 1.5 %shard_map.97 = (f32[5,32,16,256]{3,2,1,0:T(8,128)}, f32[128,128]{1,0:T(8,128)S(1)}) custom-call(f32[5]{0:T(128)S(1)} %copy-done.4, s32[3]{0:T(128)S(1)} %copy-done.5, f32[48,128]{1,0:T(8,128)S(1)} %get-tuple-element.26.folded, f32[5,32,16,256]{3,2,1,0:T(8,128)S(1)} %copy-done.1, ...), custom_call_target="tpu_custom_call", output_to_operand_aliasing={{0}: (11, {})} | custom-call | tf_op jit(solution)/shard_map/pallas_call | solution.py:587
  41.9 8.7 %all_to_all.15.relayed = f32[8,16,128]{2,1,0:T(8,128)S(1)} all-to-all(f32[8,16,128]{2,1,0:T(8,128)S(1)} %bitcast.12), channel_id=1, replica_groups=mesh['zh'=4,'x'=4,'y'=4,'core'=2,'zl'=2] {'y','core'}, dimensions={0} | all-to-all | bytes 131072 | tf_op jit(solution)/shard_map/all_to_all | solution.py:600
  50.6 0.4 shard_map.98
  51.0 10.8 %all_to_all.16 = f32[96,1,128]{2,1,0:T(1,128)S(1)} all-to-all(f32[96,1,128]{2,1,0:T(1,128)S(1)} %bitcast.13), channel_id=1, replica_groups=mesh['zh'=4,'x'=4,'y'=4,'core'=2,'zl'=2] {'x','y','core'}, dimensions={0} | all-to-all | bytes 98304 | tf_op jit(solution)/shard_map/all_to_all | solution.py:532
  61.9 0.7 shard_map.99
  62.5 4.6 %all-to-all-start.2 = ((f32[192,1,128]{2,1,0:T(1,128)}), f32[192,1,128]{2,1,0:T(1,128)S(1)}, u32[]{:S(2)}, u32[]{:S(2)}) async-start(f32[192,1,128]{2,1,0:T(1,128)} %bitcast.5), calls=%async_computation.2 | async-start | bytes 196608 | tf_op jit(solution)/shard_map/all_to_all | solution.py:532
  67.8 6.8 %all-to-all-done.2 = f32[192,1,128]{2,1,0:T(1,128)S(1)} async-done(((f32[192,1,128]{2,1,0:T(1,128)}), f32[192,1,128]{2,1,0:T(1,128)S(1)}, u32[]{:S(2)}, u32[]{:S(2)}) %all-to-all-start.2) | async-done | bytes 98336 | tf_op jit(solution)/shard_map/all_to_all | solution.py:532
  74.6 3.8 %shard_map.100 = (f32[16,64]{1,0:T(8,128)}, f32[16,16]{1,0:T(8,128)}, f32[16,3,1,4,512]{4,3,2,1,0:T(4,128)}) custom-call(s32[1]{0:T(128)S(6)} %copy.14.column_id, f32[192,128]{1,0:T(8,128)S(1)} %bitcast.10, f32[80,6144]{1,0:T(8,128)S(1)} %get-tuple-element.42.joined, f32[8,6144]{1,0:T(8,128)S(1)} %get-tuple-element.44.column), custom_call_target="tpu_custom_call" | custom-call | tf_op jit(solution)/shard_map/pallas_call | solution.py:614
  (16 shorter events, 0.0 us)
Async XLA Ops:
  0.6 1.7 %copy-start = (f32[5,32,16,256]{3,2,1,0:T(8,128)S(1)}, f32[5,32,16,256]{3,2,1,0:T(8,128)}, u32[]{:S(2)}) copy-start(f32[5,32,16,256]{3,2,1,0:T(8,128)} %start.3) | copy-start | bytes 7864324
  2.4 19.9 %copy-start.1 = (f32[5,32,16,256]{3,2,1,0:T(8,128)S(1)}, f32[5,32,16,256]{3,2,1,0:T(8,128)}, u32[]{:S(2)}) copy-start(f32[5,32,16,256]{3,2,1,0:T(8,128)} %start.3) | copy-start | bytes 7864324
  2.4 19.9 %copy-start.4 = (f32[5]{0:T(128)S(1)}, f32[5]{0:T(128)}, u32[]{:S(2)}) copy-start(f32[5]{0:T(128)} %diffusivity.5) | copy-start | bytes 64
  3.4 32.1 %copy-start.5 = (s32[3]{0:T(128)S(1)}, s32[3]{0:T(128)}, u32[]{:S(2)}) copy-start(s32[3]{0:T(128)} %offsets.3) | copy-start | bytes 40
  3.4 18.9 %collective-permute-start.2 = (f32[5,32,256]{2,1,0:T(8,128)S(1)}, f32[5,32,256]{2,1,0:T(8,128)S(1)}, u32[]{:S(2)}, u32[]{:S(2)}) collective-permute-start(f32[5,32,256]{2,1,0:T(8,128)S(1)} %get-tuple-element.29), channel_id=1, source_target_pairs={{0,1},{1,0},{2,3},{3,2},{4,5},{5,4},{6,7},{7,6},{8,9},{9,8},{10,11... | collective-permute-start | bytes 491528 | tf_op jit(solution)/shard_map/ppermute | solution.py:507
  5.9 12.4 %collective-permute-start.4 = (f32[5,16,128]{2,1,0:T(8,128)S(1)}, f32[5,16,128]{2,1,0:T(8,128)S(1)}, u32[]{:S(2)}, u32[]{:S(2)}) collective-permute-start(f32[5,16,128]{2,1,0:T(8,128)S(1)} %get-tuple-element.31), channel_id=1, source_target_pairs={{0,12},{2,6},{4,0},{6,10},{8,4},{10,14},{12,8},{14,2},{1,13},{3,7}... | collective-permute-start | bytes 122888 | tf_op jit(solution)/shard_map/ppermute | solution.py:507
  7.2 15.0 %collective-permute-start = (f32[5,16,256]{2,1,0:T(8,128)S(1)}, f32[5,16,256]{2,1,0:T(8,128)S(1)}, u32[]{:S(2)}, u32[]{:S(2)}) collective-permute-start(f32[5,16,256]{2,1,0:T(8,128)S(1)} %get-tuple-element.27), channel_id=1, source_target_pairs={{0,16},{16,0},{32,48},{48,32},{1,17},{17,1},{33,49},{49,33},{2,18}... | collective-permute-start | bytes 245768 | tf_op jit(solution)/shard_map/ppermute | solution.py:507
  8.5 13.8 %collective-permute-start.1 = (f32[5,16,256]{2,1,0:T(8,128)S(1)}, f32[5,16,256]{2,1,0:T(8,128)S(1)}, u32[]{:S(2)}, u32[]{:S(2)}) collective-permute-start(f32[5,16,256]{2,1,0:T(8,128)S(1)} %get-tuple-element.28), channel_id=1, source_target_pairs={{0,240},{16,32},{32,16},{48,64},{64,48},{80,96},{96,80},{112,128},... | collective-permute-start | bytes 245768 | tf_op jit(solution)/shard_map/ppermute | solution.py:507
  15.1 7.2 %collective-permute-start.3 = (f32[5,16,128]{2,1,0:T(8,128)S(1)}, f32[5,16,128]{2,1,0:T(8,128)S(1)}, u32[]{:S(2)}, u32[]{:S(2)}) collective-permute-start(f32[5,16,128]{2,1,0:T(8,128)S(1)} %get-tuple-element.30), channel_id=1, source_target_pairs={{0,2},{2,0},{1,3},{3,1},{4,6},{6,4},{5,7},{7,5},{8,10},{10,8},{9,1... | collective-permute-start | bytes 122888 | tf_op jit(solution)/shard_map/ppermute | solution.py:507
  18.3 3.9 %collective-permute-start.5 = (f32[5,16,128]{2,1,0:T(8,128)S(1)}, f32[5,16,128]{2,1,0:T(8,128)S(1)}, u32[]{:S(2)}, u32[]{:S(2)}) collective-permute-start(f32[5,16,128]{2,1,0:T(8,128)S(1)} %collective-permute-done.4), channel_id=1, source_target_pairs={{0,2},{2,0},{1,3},{3,1},{4,6},{6,4},{5,7},{7,5},{8,10},{10,8},{9,1... | collective-permute-start | bytes 122888 | tf_op jit(solution)/shard_map/ppermute | solution.py:507
  18.4 1.4 %copy-start.2 = (f32[64,3,1,4,512]{4,3,2,1,0:T(4,128)S(1)}, f32[64,3,1,4,512]{4,3,2,1,0:T(4,128)}, u32[]{:S(2)}) copy-start(f32[64,3,1,4,512]{4,3,2,1,0:T(4,128)} %basis.1) | copy-start | bytes 4718596
  19.8 1.0 %copy-start.3 = (f32[16,3,1,4,512]{4,3,2,1,0:T(4,128)S(1)}, f32[16,3,1,4,512]{4,3,2,1,0:T(4,128)}, u32[]{:S(2)}) copy-start(f32[16,3,1,4,512]{4,3,2,1,0:T(4,128)} %held.1) | copy-start | bytes 1179652
  27.4 8.1 %collective-permute-start.8 = (f32[5,40,256]{2,1,0:T(8,128)S(1)}, f32[5,40,256]{2,1,0:T(8,128)S(1)}, u32[]{:S(2)}, u32[]{:S(2)}) collective-permute-start(f32[5,40,256]{2,1,0:T(8,128)S(1)} %get-tuple-element.35), channel_id=1, source_target_pairs={{0,1},{1,0},{2,3},{3,2},{4,5},{5,4},{6,7},{7,6},{8,9},{9,8},{10,11... | collective-permute-start | bytes 614408 | tf_op jit(solution)/shard_map/ppermute | solution.py:507
  28.2 5.8 %collective-permute-start.10 = (f32[5,16,128]{2,1,0:T(8,128)S(1)}, f32[5,16,128]{2,1,0:T(8,128)S(1)}, u32[]{:S(2)}, u32[]{:S(2)}) collective-permute-start(f32[5,16,128]{2,1,0:T(8,128)S(1)} %get-tuple-element.37), channel_id=1, source_target_pairs={{0,12},{2,6},{4,0},{6,10},{8,4},{10,14},{12,8},{14,2},{1,13},{3,7}... | collective-permute-start | bytes 122888 | tf_op jit(solution)/shard_map/ppermute | solution.py:507
  28.2 12.1 %collective-permute-start.6 = (f32[5,16,256]{2,1,0:T(8,128)S(1)}, f32[5,16,256]{2,1,0:T(8,128)S(1)}, u32[]{:S(2)}, u32[]{:S(2)}) collective-permute-start(f32[5,16,256]{2,1,0:T(8,128)S(1)} %get-tuple-element.33), channel_id=1, source_target_pairs={{0,16},{16,0},{32,48},{48,32},{1,17},{17,1},{33,49},{49,33},{2,18}... | collective-permute-start | bytes 245768 | tf_op jit(solution)/shard_map/ppermute | solution.py:507
  28.2 12.1 %collective-permute-start.7 = (f32[5,16,256]{2,1,0:T(8,128)S(1)}, f32[5,16,256]{2,1,0:T(8,128)S(1)}, u32[]{:S(2)}, u32[]{:S(2)}) collective-permute-start(f32[5,16,256]{2,1,0:T(8,128)S(1)} %get-tuple-element.34), channel_id=1, source_target_pairs={{0,240},{16,32},{32,16},{48,64},{64,48},{80,96},{96,80},{112,128},... | collective-permute-start | bytes 245768 | tf_op jit(solution)/shard_map/ppermute | solution.py:507
  31.6 3.3 %collective-permute-start.9 = (f32[5,16,128]{2,1,0:T(8,128)S(1)}, f32[5,16,128]{2,1,0:T(8,128)S(1)}, u32[]{:S(2)}, u32[]{:S(2)}) collective-permute-start(f32[5,16,128]{2,1,0:T(8,128)S(1)} %get-tuple-element.36), channel_id=1, source_target_pairs={{0,2},{2,0},{1,3},{3,1},{4,6},{6,4},{5,7},{7,5},{8,10},{10,8},{9,1... | collective-permute-start | bytes 122888 | tf_op jit(solution)/shard_map/ppermute | solution.py:507
  34.0 1.2 %collective-permute-start.11 = (f32[5,16,128]{2,1,0:T(8,128)S(1)}, f32[5,16,128]{2,1,0:T(8,128)S(1)}, u32[]{:S(2)}, u32[]{:S(2)}) collective-permute-start(f32[5,16,128]{2,1,0:T(8,128)S(1)} %collective-permute-done.10), channel_id=1, source_target_pairs={{0,2},{2,0},{1,3},{3,1},{4,6},{6,4},{5,7},{7,5},{8,10},{10,8},{9,1... | collective-permute-start | bytes 122888 | tf_op jit(solution)/shard_map/ppermute | solution.py:507
  62.5 12.1 %all-to-all-start.2 = ((f32[192,1,128]{2,1,0:T(1,128)}), f32[192,1,128]{2,1,0:T(1,128)S(1)}, u32[]{:S(2)}, u32[]{:S(2)}) async-start(f32[192,1,128]{2,1,0:T(1,128)} %bitcast.5), calls=%async_computation.2 | async-start | bytes 196608 | tf_op jit(solution)/shard_map/all_to_all | solution.py:532

commit v6 on v5

--- a/solution.py
+++ b/solution.py
@@ -10,7 +10,7 @@
 
 STRIDE = 4
 LANES = 128
-BLOCK = 3
+BLOCK = 5
 
 time_step = 0.1
 smagorinsky = 0.02
@@ -320,8 +320,8 @@
 
 
 def outer_kernel(
-    diffusivity, offsets, folded, start, current, x_pair, x_next, y_halo, z_pair, z_next,
-    picked_in, target_in, target, snapshot, y_low, y_high, z_before, z_after, picked, result,
+    diffusivity, offsets, column_id, folded, start, current, x_pair, x_next, y_halo, z_pair,
+    z_next, picked_in, target_in, target, snapshot, chosen, y_low, y_high, z_before, z_after, picked, result,
     semaphores,
 ):
     _, cells, _, width = current.shape
@@ -344,6 +344,7 @@
     ]
     for copy in copies:
         copy.start()
+    chosen[...] = jnp.full(chosen.shape, column_id[0], jnp.int32)
     picked[...] = picked_in[...]
     shift = (8 - offsets[1]) % 8
     pick(picked, lambda f, rows: result[f, 0, rows, :], 0, offsets[2] > 0, shift)
@@ -394,40 +395,48 @@
         partial[group * 8 : group * 8 + 8, :] = sums[group]
     products = dot(jnp.ones((8, LANES), jnp.float32), partial[...], 1, 1)
     own = jnp.sum(relayed[:, 8:16, :], axis=0)
-    lane, which = iota((24, LANES), 1), iota((24, LANES), 0) % 3
-    values = jnp.zeros((24, LANES), jnp.float32)
-    for piece in range(3):
-        moved = pltpu.roll(products, 88 - 40 * piece if piece < 2 else 8, 1)[0:1]
-        row = jnp.where(lane[0:1] < 88, own[4 + piece : 5 + piece], moved)
-        values = jnp.where(which == piece, row, values)
+    lane = iota((1, LANES), 1)
+    rows = [own[4 + piece : 5 + piece] for piece in range(3)]
+    rows = [
+        jnp.where(lane < 81, rows[0], pltpu.roll(rows[2], 81, 1)),
+        jnp.where(lane < 81, rows[1], pltpu.roll(rows[2], 34, 1)),
+        products[0:1],
+    ]
+    which = iota((24, LANES), 0) % 3
+    values = jnp.where(which == 0, rows[0], jnp.where(which == 1, rows[1], rows[2]))
     count = message.shape[0]
     message[...] = jnp.broadcast_to(values[None], (count // 24, 24, LANES)).reshape(count, LANES)
 
 
-def middle_kernel(received, message):
-    rows = jnp.sum(received[...].reshape(-1, 24, LANES), axis=0)
-    count = message.shape[0]
-    message[...] = jnp.broadcast_to(rows[None], (count // 24, 24, LANES)).reshape(count, LANES)
+def middle_kernel(received, message, stacked):
+    stacked[...] = jnp.sum(received[...].reshape(-1, 24, LANES), axis=0)
+    first, second, third = (stacked[pl.ds(piece, 8, stride=3), :] for piece in range(3))
+    third = jnp.sum(third, axis=0, keepdims=True)
+    for target in range(message.shape[0] // 17):
+        message[target * 17 : target * 17 + 8, :] = first
+        message[target * 17 + 8 : target * 17 + 16, :] = second
+        message[target * 17 + 16 : target * 17 + 17, :] = third
 
 
 def final_kernel(
-    rows_total, column_id, gathered, joined, column,
-    coefficients, r_factor, columns_out, stacked,
+    rows_total, chosen_column, gathered, joined, column,
+    coefficients, r_factor, columns_out,
 ):
     total = joined.shape[0]
     count, rank = coefficients.shape
     _, _, _, levels, points = columns_out.shape
-    chosen = column_id[0]
+    chosen = chosen_column[0:1, :]
     half = total // 2
-    stacked[...] = jnp.sum(gathered[...].reshape(-1, 48, LANES), axis=0)
-    pieces = [
-        [stacked[pl.ds(part * 24 + piece, 8, stride=3), :] for piece in range(3)]
-        for part in range(2)
-    ]
-    sums = [jnp.sum(pieces[0][i] + pieces[1][i], axis=0, keepdims=True) for i in range(3)]
-    sums = [pltpu.roll(row, shift, 1) for row, shift in zip(sums, (40, 80, 120))]
-    lane = iota((1, LANES), 1)
-    sums = jnp.where(lane < 40, sums[0], jnp.where(lane < 80, sums[1], sums[2])) / rows_total
+    lane = iota((8, LANES), 1)
+    pieces = []
+    for part in range(2):
+        first, second = (
+            sum(gathered[17 * (2 * i + part) + at : 17 * (2 * i + part) + at + 8, :] for i in range(4))
+            for at in (0, 8)
+        )
+        third = jnp.where(lane < 47, pltpu.roll(first, 47, 1), pltpu.roll(second, 94, 1))
+        pieces.append([first, second, third])
+    sums = sum(gathered[17 * i + 16 : 17 * i + 17, :] for i in range(8)) / rows_total
     folded = jnp.concatenate(pieces[0] + pieces[1][:2], axis=0) / rows_total
     turned = jnp.concatenate([folded, jnp.zeros((LANES - half, LANES), jnp.float32)], axis=0).T
     lane, sub = iota((half, LANES), 1), iota((half, LANES), 0)
@@ -584,18 +593,21 @@
         ],
         cost_estimate=busy, compiler_params=params(24),
     )(diffusivity, subsample_offsets, fields, first, *halos)
-    fields_out, snapshot = pl.pallas_call(
-        outer_kernel, in_specs=[SMEM] * 2 + [VMEM] * 9 + [ANY], out_specs=[ANY, VMEM],
-        out_shape=(struct(*fields.shape), struct(LANES, LANES)),
+    fields_out, snapshot, chosen = pl.pallas_call(
+        outer_kernel, in_specs=[SMEM] * 3 + [VMEM] * 9 + [ANY], out_specs=[ANY, VMEM, VMEM],
+        out_shape=(
+            struct(*fields.shape), struct(LANES, LANES),
+            jax.ShapeDtypeStruct((8, LANES), jnp.int32),
+        ),
         scratch_shapes=sides + [
             pltpu.VMEM((LANES, width), jnp.float32),
             pltpu.VMEM((count, 2, height, width), jnp.float32),
             pltpu.SemaphoreType.DMA((2,)),
         ],
-        input_output_aliases={11: 0}, compiler_params=params(24),
+        input_output_aliases={12: 0}, compiler_params=params(24),
     )(
-        diffusivity, subsample_offsets, folded, fields, first, x_pair, x_next, *halos,
-        picked, fields_out,
+        diffusivity, subsample_offsets, column_id, folded, fields, first, x_pair, x_next,
+        *halos, picked, fields_out,
     )
     relayed = lax.all_to_all(snapshot.reshape(8, 16, LANES), ("y", "core"), 0, 0, tiled=True)
 
@@ -606,22 +618,20 @@
         compiler_params=params(16),
     )(relayed, joined)
     message = pl.pallas_call(
-        middle_kernel, in_specs=[VMEM], out_specs=VMEM, out_shape=struct(192, LANES),
+        middle_kernel, in_specs=[VMEM], out_specs=VMEM, out_shape=struct(136, LANES),
+        scratch_shapes=[pltpu.VMEM((24, LANES), jnp.float32)],
         compiler_params=params(4),
     )(everyone(message, ("x", "y", "core")))
     gathered = everyone(message, ("zh", "zl"))
 
     coefficients, r_factor, new_columns = pl.pallas_call(
         functools.partial(final_kernel, float(devices * length)),
-        in_specs=[SMEM] + [VMEM] * 3, out_specs=[VMEM] * 3,
+        in_specs=[VMEM] * 4, out_specs=[VMEM] * 3,
         out_shape=(
             struct(columns, rank), struct(columns, columns), struct(*held_block.shape)
         ),
-        scratch_shapes=[
-            pltpu.VMEM((48, LANES), jnp.float32),
-        ],
         compiler_params=params(24),
-    )(column_id, gathered, joined, column)
+    )(chosen, gathered, joined, column)
     return fields_out, coefficients.T, r_factor, new_columns
 
 

time: 78.7 us -> 77.5 us (0.985)
  blocking collectives: 19.6 us -> 31.2 us
  waiting for transfers between devices: 8.32 us -> 0.87 us
  starting transfers between devices: 26.2 us -> 21.6 us
    all_to_all x1 -> x2, blocking collectives: 10.8 us -> 22.4 us  [everyone(): lax.all_to_all(message.reshape(rows, 1, LANES), axes, 0, 0, tiled=True)]
    all_to_all x1 -> x0, waiting for transfers between devices: 6.81 us -> none  [everyone(): lax.all_to_all(message.reshape(rows, 1, LANES), axes, 0, 0, tiled=True)]
    all_to_all x1 -> x0, starting transfers between devices: 4.59 us -> none  [everyone(): lax.all_to_all(message.reshape(rows, 1, LANES), axes, 0, 0, tiled=True)]
  transfers between devices with their start and end apart: 13 -> 12, of which waited for: 4 -> 3; matrix products, arithmetic and copies ran while one was open for 0% -> 0% of each run, Pallas kernels for 8% -> 8%
where the time goes in v6:
time: 77.5 us; the launch traced here: 77.2 us
  blocking collectives  31.2 us (40%)
  starting transfers between devices  21.6 us (28%)
  Pallas kernels  18 us (23%)
  local copies, waits for them, and re-layouts  4.15 us (5%)
  between operations  1.43 us (2%)
  waiting for transfers between devices  0.87 us (1%)
    all_to_all x2, blocking collectives, everyone(): lax.all_to_all(message.reshape(rows, 1, LANES), axes, 0, 0, tiled=True)  22.4 us
    ppermute x12, starting transfers between devices, moved(): return lax.ppermute(value, axes, pairs)  21.6 us
    all_to_all x1, blocking collectives, on_device(): lax.all_to_all(snapshot.reshape(8, 16, LANES), ('y', 'core'), 0, 0, tiled...  8.75 us
    pallas_call x1, Pallas kernels, on_device(): pl.pallas_call(first_kernel, in_specs=[SMEM] + [VMEM] * 7, out_specs=[VME...  4.91 us
    pallas_call x1, Pallas kernels, on_device(): pl.pallas_call(inner_kernel, in_specs=[SMEM] * 2 + [VMEM] * 5, out_specs=...  4.73 us
    unnamed x12, local copies, waits for them, and re-layouts  4.15 us
    pallas_call x1, Pallas kernels, on_device(): pl.pallas_call(functools.partial(final_kernel, float(devices * length)),...  3.88 us
  transfers between devices with their start and end apart: 12, of which 3 were waited for; matrix products, arithmetic and copies ran while one was open for 0% of the time, Pallas kernels for 8%

profile of v6, /device:TPU:1, one launch (start us, length us, event | category | flops | bytes accessed | tf_op | source)
XLA Modules:
  0.0 77.2 jit_solution(6117043306288444595)
XLA Ops:
  0.6 1.7 %copy-done = f32[5,32,16,256]{3,2,1,0:T(8,128)S(1)} copy-done((f32[5,32,16,256]{3,2,1,0:T(8,128)S(1)}, f32[5,32,16,256]{3,2,1,0:T(8,128)}, u32[]{:S(2)}) %copy-start) | copy-done | bytes 2621464
  2.4 1.0 %shard_map.94 = (f32[5,16,256]{2,1,0:T(8,128)S(1)}, f32[5,16,256]{2,1,0:T(8,128)S(1)}, f32[5,32,256]{2,1,0:T(8,128)S(1)}, f32[5,16,128]{2,1,0:T(8,128)S(1)}, f32[5,16,128]{2,1,0:T(8,128)S(1)}) custom-call(f32[5,32,16,256]{3,2,1,0:T(8,128)S(1)} %copy-done), custom_call_target="tpu_custom_call" | custom-call | tf_op jit(solution)/shard_map/pallas_call | solution.py:566
  3.4 0.0 copy-start.5
  3.4 2.6 %collective-permute-start.2 = (f32[5,32,256]{2,1,0:T(8,128)S(1)}, f32[5,32,256]{2,1,0:T(8,128)S(1)}, u32[]{:S(2)}, u32[]{:S(2)}) collective-permute-start(f32[5,32,256]{2,1,0:T(8,128)S(1)} %get-tuple-element.30), channel_id=1, source_target_pairs={{0,1},{1,0},{2,3},{3,2},{4,5},{5,4},{6,7},{7,6},{8,9},{9,8},{10,11... | collective-permute-start | bytes 491528 | tf_op jit(solution)/shard_map/ppermute | solution.py:516
  5.9 1.3 %collective-permute-start.4 = (f32[5,16,128]{2,1,0:T(8,128)S(1)}, f32[5,16,128]{2,1,0:T(8,128)S(1)}, u32[]{:S(2)}, u32[]{:S(2)}) collective-permute-start(f32[5,16,128]{2,1,0:T(8,128)S(1)} %get-tuple-element.32), channel_id=1, source_target_pairs={{0,12},{2,6},{4,0},{6,10},{8,4},{10,14},{12,8},{14,2},{1,13},{3,7}... | collective-permute-start | bytes 122888 | tf_op jit(solution)/shard_map/ppermute | solution.py:516
  7.2 1.2 %collective-permute-start = (f32[5,16,256]{2,1,0:T(8,128)S(1)}, f32[5,16,256]{2,1,0:T(8,128)S(1)}, u32[]{:S(2)}, u32[]{:S(2)}) collective-permute-start(f32[5,16,256]{2,1,0:T(8,128)S(1)} %get-tuple-element.28), channel_id=1, source_target_pairs={{0,16},{16,0},{32,48},{48,32},{1,17},{17,1},{33,49},{49,33},{2,18}... | collective-permute-start | bytes 245768 | tf_op jit(solution)/shard_map/ppermute | solution.py:516
  8.5 6.7 %collective-permute-start.1 = (f32[5,16,256]{2,1,0:T(8,128)S(1)}, f32[5,16,256]{2,1,0:T(8,128)S(1)}, u32[]{:S(2)}, u32[]{:S(2)}) collective-permute-start(f32[5,16,256]{2,1,0:T(8,128)S(1)} %get-tuple-element.29), channel_id=1, source_target_pairs={{0,240},{16,32},{32,16},{48,64},{64,48},{80,96},{96,80},{112,128},... | collective-permute-start | bytes 245768 | tf_op jit(solution)/shard_map/ppermute | solution.py:516
  15.1 3.2 %collective-permute-start.3 = (f32[5,16,128]{2,1,0:T(8,128)S(1)}, f32[5,16,128]{2,1,0:T(8,128)S(1)}, u32[]{:S(2)}, u32[]{:S(2)}) collective-permute-start(f32[5,16,128]{2,1,0:T(8,128)S(1)} %get-tuple-element.31), channel_id=1, source_target_pairs={{0,2},{2,0},{1,3},{3,1},{4,6},{6,4},{5,7},{7,5},{8,10},{10,8},{9,1... | collective-permute-start | bytes 122888 | tf_op jit(solution)/shard_map/ppermute | solution.py:516
  18.3 0.0 collective-permute-start.5
  18.4 1.4 %copy-done.2 = f32[64,3,1,4,512]{4,3,2,1,0:T(4,128)S(1)} copy-done((f32[64,3,1,4,512]{4,3,2,1,0:T(4,128)S(1)}, f32[64,3,1,4,512]{4,3,2,1,0:T(4,128)}, u32[]{:S(2)}) %copy-start.2) | copy-done | bytes 1572888
  19.8 1.0 %copy-done.3 = f32[16,3,1,4,512]{4,3,2,1,0:T(4,128)S(1)} copy-done((f32[16,3,1,4,512]{4,3,2,1,0:T(4,128)S(1)}, f32[16,3,1,4,512]{4,3,2,1,0:T(4,128)}, u32[]{:S(2)}) %copy-start.3) | copy-done | bytes 393240
  20.8 1.5 %shard_map.93 = (f32[80,6144]{1,0:T(8,128)S(1)}, f32[48,128]{1,0:T(8,128)S(1)}) custom-call(f32[64,3,1,4,512]{4,3,2,1,0:T(4,128)S(1)} %copy-done.2, f32[16,3,1,4,512]{4,3,2,1,0:T(4,128)S(1)} %copy-done.3), custom_call_target="tpu_custom_call" | custom-call | tf_op jit(solution)/shard_map/pallas_call | solution.py:572
  22.3 0.0 collective-permute-done.3.z_pair_in
  22.3 0.0 collective-permute-done.x_pair_in
  22.3 0.0 collective-permute-done.1.x_next_in
  22.3 4.9 %shard_map.95 = (f32[5,32,16,256]{3,2,1,0:T(8,128)S(1)}, f32[5,16,256]{2,1,0:T(8,128)S(1)}, f32[5,16,256]{2,1,0:T(8,128)S(1)}, f32[5,40,256]{2,1,0:T(8,128)S(1)}...) custom-call(f32[5]{0:T(128)S(1)} %copy-done.4, f32[48,128]{1,0:T(8,128)S(1)} %get-tuple-element.27.folded, ...), custom_call_target="tpu_custom_call" | custom-call | tf_op jit(solution)/shard_map/pallas_call | solution.py:578
  27.3 0.8 %collective-permute-start.8 = (f32[5,40,256]{2,1,0:T(8,128)S(1)}, f32[5,40,256]{2,1,0:T(8,128)S(1)}, u32[]{:S(2)}, u32[]{:S(2)}) collective-permute-start(f32[5,40,256]{2,1,0:T(8,128)S(1)} %get-tuple-element.36), channel_id=1, source_target_pairs={{0,1},{1,0},{2,3},{3,2},{4,5},{5,4},{6,7},{7,6},{8,9},{9,8},{10,11... | collective-permute-start | bytes 614408 | tf_op jit(solution)/shard_map/ppermute | solution.py:516
  28.1 0.0 collective-permute-start.10
  28.1 3.4 %collective-permute-start.7 = (f32[5,16,256]{2,1,0:T(8,128)S(1)}, f32[5,16,256]{2,1,0:T(8,128)S(1)}, u32[]{:S(2)}, u32[]{:S(2)}) collective-permute-start(f32[5,16,256]{2,1,0:T(8,128)S(1)} %get-tuple-element.35), channel_id=1, source_target_pairs={{0,240},{16,32},{32,16},{48,64},{64,48},{80,96},{96,80},{112,128},... | collective-permute-start | bytes 245768 | tf_op jit(solution)/shard_map/ppermute | solution.py:516
  31.5 2.4 %collective-permute-start.9 = (f32[5,16,128]{2,1,0:T(8,128)S(1)}, f32[5,16,128]{2,1,0:T(8,128)S(1)}, u32[]{:S(2)}, u32[]{:S(2)}) collective-permute-start(f32[5,16,128]{2,1,0:T(8,128)S(1)} %get-tuple-element.37), channel_id=1, source_target_pairs={{0,2},{2,0},{1,3},{3,1},{4,6},{6,4},{5,7},{7,5},{8,10},{10,8},{9,1... | collective-permute-start | bytes 122888 | tf_op jit(solution)/shard_map/ppermute | solution.py:516
  33.9 0.0 collective-permute-start.11
  34.5 0.2 collective-permute-done.9.z_pair
  34.7 0.4 collective-permute-done.11.z_next
  35.1 0.3 collective-permute-done.8.y_halo
  35.4 4.7 %shard_map.96 = (f32[5,32,16,256]{3,2,1,0:T(8,128)}, f32[128,256]{1,0:T(8,128)S(1)}) custom-call(f32[5]{0:T(128)S(1)} %copy-done.4, s32[3]{0:T(128)S(1)} %copy-done.5, f32[5,32,16,256]{3,2,1,0:T(8,128)S(1)} %copy-done.1, f32[5,32,16,256]{3,2,1,0:T(8,128)S(1)} %get-tuple-element.33.current, f32[5,40,256]{2,1,0:T(8,128)S(1)} %collective-permute-done.8.y_halo, ...), custom_call_target="tpu_custom_call" | custom-call | flops 20000000 | bytes 20000000 | tf_op jit(solution)/shard_map/pallas_call | solution.py:588
  40.1 0.0 collective-permute-done.7.x_next
  40.1 1.5 %shard_map.97 = (f32[5,32,16,256]{3,2,1,0:T(8,128)}, f32[128,128]{1,0:T(8,128)S(1)}, s32[8,128]{1,0:T(8,128)S(1)}) custom-call(f32[5]{0:T(128)S(1)} %copy-done.4, s32[3]{0:T(128)S(1)} %copy-done.5, s32[1]{0:T(128)S(6)} %copy.14.column_id, f32[48,128]{1,0:T(8,128)S(1)} %get-tuple-element.27.folded, ...), custom_call_target="tpu_custom_call", output_to_operand_aliasing={{0}: (12, {})} | custom-call | tf_op jit(solution)/shard_map/pallas_call | solution.py:596
  41.7 8.7 %all_to_all.15.relayed = f32[8,16,128]{2,1,0:T(8,128)S(1)} all-to-all(f32[8,16,128]{2,1,0:T(8,128)S(1)} %bitcast.13), channel_id=1, replica_groups=mesh['zh'=4,'x'=4,'y'=4,'core'=2,'zl'=2] {'y','core'}, dimensions={0} | all-to-all | bytes 131072 | tf_op jit(solution)/shard_map/all_to_all | solution.py:612
  50.5 0.4 shard_map.98
  50.8 10.8 %all_to_all.16 = f32[96,1,128]{2,1,0:T(1,128)S(1)} all-to-all(f32[96,1,128]{2,1,0:T(1,128)S(1)} %bitcast.14), channel_id=1, replica_groups=mesh['zh'=4,'x'=4,'y'=4,'core'=2,'zl'=2] {'x','y','core'}, dimensions={0} | all-to-all | bytes 98304 | tf_op jit(solution)/shard_map/all_to_all | solution.py:541
  61.7 11.6 %all_to_all.17 = f32[136,1,128]{2,1,0:T(1,128)S(1)} all-to-all(f32[136,1,128]{2,1,0:T(1,128)S(1)} %bitcast.11), channel_id=1, replica_groups=mesh['zh'=4,'x'=4,'y'=4,'core'=2,'zl'=2] {'zh','zl'}, dimensions={0} | all-to-all | bytes 139264 | tf_op jit(solution)/shard_map/all_to_all | solution.py:541
  73.3 3.9 %shard_map.100 = (f32[16,64]{1,0:T(8,128)}, f32[16,16]{1,0:T(8,128)}, f32[16,3,1,4,512]{4,3,2,1,0:T(4,128)}) custom-call(s32[8,128]{1,0:T(8,128)S(1)} %get-tuple-element.42.chosen_column, f32[136,128]{1,0:T(8,128)S(1)} %bitcast.10, f32[80,6144]{1,0:T(8,128)S(1)} %get-tuple-element.44.joined, f32[8,6144]{1,0:T(8,128)S(1)} %get-tuple-element.46.column), custom_call_target="tpu_custom_call" | custom-call | tf_op jit(solution)/shard_map/pallas_call | solution.py:627
  (15 shorter events, 0.0 us)
Async XLA Ops:
  0.6 1.7 %copy-start = (f32[5,32,16,256]{3,2,1,0:T(8,128)S(1)}, f32[5,32,16,256]{3,2,1,0:T(8,128)}, u32[]{:S(2)}) copy-start(f32[5,32,16,256]{3,2,1,0:T(8,128)} %start.3) | copy-start | bytes 7864324
  2.4 19.9 %copy-start.1 = (f32[5,32,16,256]{3,2,1,0:T(8,128)S(1)}, f32[5,32,16,256]{3,2,1,0:T(8,128)}, u32[]{:S(2)}) copy-start(f32[5,32,16,256]{3,2,1,0:T(8,128)} %start.3) | copy-start | bytes 7864324
  2.4 20.0 %copy-start.4 = (f32[5]{0:T(128)S(1)}, f32[5]{0:T(128)}, u32[]{:S(2)}) copy-start(f32[5]{0:T(128)} %diffusivity.5) | copy-start | bytes 64
  3.4 32.0 %copy-start.5 = (s32[3]{0:T(128)S(1)}, s32[3]{0:T(128)}, u32[]{:S(2)}) copy-start(s32[3]{0:T(128)} %offsets.3) | copy-start | bytes 40
  3.4 18.9 %collective-permute-start.2 = (f32[5,32,256]{2,1,0:T(8,128)S(1)}, f32[5,32,256]{2,1,0:T(8,128)S(1)}, u32[]{:S(2)}, u32[]{:S(2)}) collective-permute-start(f32[5,32,256]{2,1,0:T(8,128)S(1)} %get-tuple-element.30), channel_id=1, source_target_pairs={{0,1},{1,0},{2,3},{3,2},{4,5},{5,4},{6,7},{7,6},{8,9},{9,8},{10,11... | collective-permute-start | bytes 491528 | tf_op jit(solution)/shard_map/ppermute | solution.py:516
  5.9 12.4 %collective-permute-start.4 = (f32[5,16,128]{2,1,0:T(8,128)S(1)}, f32[5,16,128]{2,1,0:T(8,128)S(1)}, u32[]{:S(2)}, u32[]{:S(2)}) collective-permute-start(f32[5,16,128]{2,1,0:T(8,128)S(1)} %get-tuple-element.32), channel_id=1, source_target_pairs={{0,12},{2,6},{4,0},{6,10},{8,4},{10,14},{12,8},{14,2},{1,13},{3,7}... | collective-permute-start | bytes 122888 | tf_op jit(solution)/shard_map/ppermute | solution.py:516
  7.2 15.0 %collective-permute-start = (f32[5,16,256]{2,1,0:T(8,128)S(1)}, f32[5,16,256]{2,1,0:T(8,128)S(1)}, u32[]{:S(2)}, u32[]{:S(2)}) collective-permute-start(f32[5,16,256]{2,1,0:T(8,128)S(1)} %get-tuple-element.28), channel_id=1, source_target_pairs={{0,16},{16,0},{32,48},{48,32},{1,17},{17,1},{33,49},{49,33},{2,18}... | collective-permute-start | bytes 245768 | tf_op jit(solution)/shard_map/ppermute | solution.py:516
  8.5 13.8 %collective-permute-start.1 = (f32[5,16,256]{2,1,0:T(8,128)S(1)}, f32[5,16,256]{2,1,0:T(8,128)S(1)}, u32[]{:S(2)}, u32[]{:S(2)}) collective-permute-start(f32[5,16,256]{2,1,0:T(8,128)S(1)} %get-tuple-element.29), channel_id=1, source_target_pairs={{0,240},{16,32},{32,16},{48,64},{64,48},{80,96},{96,80},{112,128},... | collective-permute-start | bytes 245768 | tf_op jit(solution)/shard_map/ppermute | solution.py:516
  15.1 7.2 %collective-permute-start.3 = (f32[5,16,128]{2,1,0:T(8,128)S(1)}, f32[5,16,128]{2,1,0:T(8,128)S(1)}, u32[]{:S(2)}, u32[]{:S(2)}) collective-permute-start(f32[5,16,128]{2,1,0:T(8,128)S(1)} %get-tuple-element.31), channel_id=1, source_target_pairs={{0,2},{2,0},{1,3},{3,1},{4,6},{6,4},{5,7},{7,5},{8,10},{10,8},{9,1... | collective-permute-start | bytes 122888 | tf_op jit(solution)/shard_map/ppermute | solution.py:516
  18.3 3.9 %collective-permute-start.5 = (f32[5,16,128]{2,1,0:T(8,128)S(1)}, f32[5,16,128]{2,1,0:T(8,128)S(1)}, u32[]{:S(2)}, u32[]{:S(2)}) collective-permute-start(f32[5,16,128]{2,1,0:T(8,128)S(1)} %collective-permute-done.4), channel_id=1, source_target_pairs={{0,2},{2,0},{1,3},{3,1},{4,6},{6,4},{5,7},{7,5},{8,10},{10,8},{9,1... | collective-permute-start | bytes 122888 | tf_op jit(solution)/shard_map/ppermute | solution.py:516
  18.4 1.4 %copy-start.2 = (f32[64,3,1,4,512]{4,3,2,1,0:T(4,128)S(1)}, f32[64,3,1,4,512]{4,3,2,1,0:T(4,128)}, u32[]{:S(2)}) copy-start(f32[64,3,1,4,512]{4,3,2,1,0:T(4,128)} %basis.1) | copy-start | bytes 4718596
  19.8 1.0 %copy-start.3 = (f32[16,3,1,4,512]{4,3,2,1,0:T(4,128)S(1)}, f32[16,3,1,4,512]{4,3,2,1,0:T(4,128)}, u32[]{:S(2)}) copy-start(f32[16,3,1,4,512]{4,3,2,1,0:T(4,128)} %held.1) | copy-start | bytes 1179652
  27.3 8.1 %collective-permute-start.8 = (f32[5,40,256]{2,1,0:T(8,128)S(1)}, f32[5,40,256]{2,1,0:T(8,128)S(1)}, u32[]{:S(2)}, u32[]{:S(2)}) collective-permute-start(f32[5,40,256]{2,1,0:T(8,128)S(1)} %get-tuple-element.36), channel_id=1, source_target_pairs={{0,1},{1,0},{2,3},{3,2},{4,5},{5,4},{6,7},{7,6},{8,9},{9,8},{10,11... | collective-permute-start | bytes 614408 | tf_op jit(solution)/shard_map/ppermute | solution.py:516
  28.1 5.8 %collective-permute-start.10 = (f32[5,16,128]{2,1,0:T(8,128)S(1)}, f32[5,16,128]{2,1,0:T(8,128)S(1)}, u32[]{:S(2)}, u32[]{:S(2)}) collective-permute-start(f32[5,16,128]{2,1,0:T(8,128)S(1)} %get-tuple-element.38), channel_id=1, source_target_pairs={{0,12},{2,6},{4,0},{6,10},{8,4},{10,14},{12,8},{14,2},{1,13},{3,7}... | collective-permute-start | bytes 122888 | tf_op jit(solution)/shard_map/ppermute | solution.py:516
  28.1 12.1 %collective-permute-start.6 = (f32[5,16,256]{2,1,0:T(8,128)S(1)}, f32[5,16,256]{2,1,0:T(8,128)S(1)}, u32[]{:S(2)}, u32[]{:S(2)}) collective-permute-start(f32[5,16,256]{2,1,0:T(8,128)S(1)} %get-tuple-element.34), channel_id=1, source_target_pairs={{0,16},{16,0},{32,48},{48,32},{1,17},{17,1},{33,49},{49,33},{2,18}... | collective-permute-start | bytes 245768 | tf_op jit(solution)/shard_map/ppermute | solution.py:516
  28.1 12.1 %collective-permute-start.7 = (f32[5,16,256]{2,1,0:T(8,128)S(1)}, f32[5,16,256]{2,1,0:T(8,128)S(1)}, u32[]{:S(2)}, u32[]{:S(2)}) collective-permute-start(f32[5,16,256]{2,1,0:T(8,128)S(1)} %get-tuple-element.35), channel_id=1, source_target_pairs={{0,240},{16,32},{32,16},{48,64},{64,48},{80,96},{96,80},{112,128},... | collective-permute-start | bytes 245768 | tf_op jit(solution)/shard_map/ppermute | solution.py:516
  31.5 3.3 %collective-permute-start.9 = (f32[5,16,128]{2,1,0:T(8,128)S(1)}, f32[5,16,128]{2,1,0:T(8,128)S(1)}, u32[]{:S(2)}, u32[]{:S(2)}) collective-permute-start(f32[5,16,128]{2,1,0:T(8,128)S(1)} %get-tuple-element.37), channel_id=1, source_target_pairs={{0,2},{2,0},{1,3},{3,1},{4,6},{6,4},{5,7},{7,5},{8,10},{10,8},{9,1... | collective-permute-start | bytes 122888 | tf_op jit(solution)/shard_map/ppermute | solution.py:516
  33.9 1.2 %collective-permute-start.11 = (f32[5,16,128]{2,1,0:T(8,128)S(1)}, f32[5,16,128]{2,1,0:T(8,128)S(1)}, u32[]{:S(2)}, u32[]{:S(2)}) collective-permute-start(f32[5,16,128]{2,1,0:T(8,128)S(1)} %collective-permute-done.10), channel_id=1, source_target_pairs={{0,2},{2,0},{1,3},{3,1},{4,6},{6,4},{5,7},{7,5},{8,10},{10,8},{9,1... | collective-permute-start | bytes 122888 | tf_op jit(solution)/shard_map/ppermute | solution.py:516

commit v7 on v6

--- a/solution.py
+++ b/solution.py
@@ -277,7 +277,7 @@
         for tile in range(2):
             rows = pltpu.roll(plane(f, slice(tile * 8, tile * 8 + 8)), shift, 0)
             for part in range(2):
-                row = column * 16 + f * 4 + tile * 2 + part
+                row = part * 64 + column * 8 + f * 2 + tile
                 value = rows[part * STRIDE : part * STRIDE + 1, :]
                 if keep is not None:
                     value = jnp.where(keep, picked[row : row + 1, :], value)
@@ -356,17 +356,28 @@
     choose = iota((width, LANES), 0) == STRIDE * (iota((width, LANES), 1) % points) + offsets[0]
     choose = choose.astype(jnp.float32).astype(jnp.bfloat16)
     high, middle, low = split(picked[...])
-    snapshot[...] = matmul(high, choose, 0) + matmul(middle, choose, 0) + matmul(low, choose, 0)
+    sampled = matmul(high, choose, 0) + matmul(middle, choose, 0) + matmul(low, choose, 0)
+    half = snapshot.shape[0]
+    snapshot[...] = jnp.where(iota((half, LANES), 1) < points, sampled[:half], sampled[half:])
     upper = lax.axis_index("zl") > 0
+    kept = []
     for group in range(3):
         lanes = slice(group % 2 * LANES, (group % 2 + 1) * LANES)
-        kept = jnp.where(
-            upper, folded[group * 8 + 24 : group * 8 + 32], folded[group * 8 : group * 8 + 8]
+        kept.append(
+            jnp.where(
+                upper, folded[group * 8 + 24 : group * 8 + 32], folded[group * 8 : group * 8 + 8]
+            )
+            + y_halo[group // 2, cells:, lanes]
         )
-        kept = kept + y_halo[group // 2, cells:, lanes]
-        for column in range(cells // STRIDE):
-            row = column * 16 + 12 + group
-            snapshot[row : row + 1, :] = kept[column : column + 1]
+    lane = iota((8, LANES), 1)
+    kept = [
+        jnp.where(lane < 81, kept[0], pltpu.roll(kept[2], 81, 1)),
+        jnp.where(lane < 81, kept[1], pltpu.roll(kept[2], 34, 1)),
+    ]
+    for column in range(cells // STRIDE):
+        for i in range(2):
+            row = column * 8 + 6 + i
+            snapshot[row : row + 1, :] = kept[i][column : column + 1]
     for copy in copies:
         copy.wait()
 
@@ -376,15 +387,15 @@
     groups = total // 8
     low = iota((1, LANES), 1) < LANES // 2
     sums = [jnp.zeros((8, LANES), jnp.float32) for _ in range(groups + 1)]
+    here = [relayed[source] for source in range(8)]
+    turned = [pltpu.roll(rows, LANES // 2, 1) for rows in here]
     for row in range(12):
+        left, right = (here, turned) if row % 2 == 0 else (turned, here)
+        place = slice(row // 2, row // 2 + 1)
         for pair in range(4):
             tile = row * 4 + pair
             lanes = slice(tile * LANES, (tile + 1) * LANES)
-            values = jnp.where(
-                low,
-                relayed[2 * pair, row : row + 1, :],
-                relayed[2 * pair + 1, row : row + 1, :],
-            )
+            values = jnp.where(low, left[2 * pair][place], right[2 * pair + 1][place])
             values = jnp.broadcast_to(values, (8, LANES))
             column[:, lanes] = values
             for group in range(groups):
@@ -394,14 +405,8 @@
     for group in range(groups + 1):
         partial[group * 8 : group * 8 + 8, :] = sums[group]
     products = dot(jnp.ones((8, LANES), jnp.float32), partial[...], 1, 1)
-    own = jnp.sum(relayed[:, 8:16, :], axis=0)
-    lane = iota((1, LANES), 1)
-    rows = [own[4 + piece : 5 + piece] for piece in range(3)]
-    rows = [
-        jnp.where(lane < 81, rows[0], pltpu.roll(rows[2], 81, 1)),
-        jnp.where(lane < 81, rows[1], pltpu.roll(rows[2], 34, 1)),
-        products[0:1],
-    ]
+    own = sum(here)
+    rows = (own[6:7], own[7:8], products[0:1])
     which = iota((24, LANES), 0) % 3
     values = jnp.where(which == 0, rows[0], jnp.where(which == 1, rows[1], rows[2]))
     count = message.shape[0]
@@ -596,7 +601,7 @@
     fields_out, snapshot, chosen = pl.pallas_call(
         outer_kernel, in_specs=[SMEM] * 3 + [VMEM] * 9 + [ANY], out_specs=[ANY, VMEM, VMEM],
         out_shape=(
-            struct(*fields.shape), struct(LANES, LANES),
+            struct(*fields.shape), struct(LANES // 2, LANES),
             jax.ShapeDtypeStruct((8, LANES), jnp.int32),
         ),
         scratch_shapes=sides + [
@@ -609,7 +614,7 @@
         diffusivity, subsample_offsets, column_id, folded, fields, first, x_pair, x_next,
         *halos, picked, fields_out,
     )
-    relayed = lax.all_to_all(snapshot.reshape(8, 16, LANES), ("y", "core"), 0, 0, tiled=True)
+    relayed = lax.all_to_all(snapshot.reshape(8, 8, LANES), ("y", "core"), 0, 0, tiled=True)
 
     message, column = pl.pallas_call(
         product_kernel, in_specs=[VMEM] * 2, out_specs=[VMEM] * 2,

time: 77.5 us -> 77.3 us (level)
  no operation moved by 1% of the time
where the time goes in v7:
time: 77.3 us; the launch traced here: 77 us
  blocking collectives  31 us (40%)
  starting transfers between devices  21.6 us (28%)
  Pallas kernels  18 us (23%)
  local copies, waits for them, and re-layouts  4.15 us (5%)
  between operations  1.43 us (2%)
  waiting for transfers between devices  0.87 us (1%)
    all_to_all x2, blocking collectives, everyone(): lax.all_to_all(message.reshape(rows, 1, LANES), axes, 0, 0, tiled=True)  22.4 us
    ppermute x12, starting transfers between devices, moved(): return lax.ppermute(value, axes, pairs)  21.6 us
    all_to_all x1, blocking collectives, on_device(): lax.all_to_all(snapshot.reshape(8, 8, LANES), ('y', 'core'), 0, 0, tiled=...  8.62 us
    pallas_call x1, Pallas kernels, on_device(): pl.pallas_call(first_kernel, in_specs=[SMEM] + [VMEM] * 7, out_specs=[VME...  4.91 us
    pallas_call x1, Pallas kernels, on_device(): pl.pallas_call(inner_kernel, in_specs=[SMEM] * 2 + [VMEM] * 5, out_specs=...  4.73 us
    unnamed x12, local copies, waits for them, and re-layouts  4.15 us
    pallas_call x1, Pallas kernels, on_device(): pl.pallas_call(functools.partial(final_kernel, float(devices * length)),...  3.88 us
    pallas_call x1, Pallas kernels, on_device(): pl.pallas_call(outer_kernel, in_specs=[SMEM] * 3 + [VMEM] * 9 + [ANY], ou...  1.55 us
  transfers between devices with their start and end apart: 12, of which 3 were waited for; matrix products, arithmetic and copies ran while one was open for 0% of the time, Pallas kernels for 8%

profile of v7, /device:TPU:1, one launch (start us, length us, event | category | flops | bytes accessed | tf_op | source)
XLA Modules:
  0.0 77.0 jit_solution(10606882935289089496)
XLA Ops:
  0.6 1.7 %copy-done = f32[5,32,16,256]{3,2,1,0:T(8,128)S(1)} copy-done((f32[5,32,16,256]{3,2,1,0:T(8,128)S(1)}, f32[5,32,16,256]{3,2,1,0:T(8,128)}, u32[]{:S(2)}) %copy-start) | copy-done | bytes 2621464
  2.4 1.0 %shard_map.94 = (f32[5,16,256]{2,1,0:T(8,128)S(1)}, f32[5,16,256]{2,1,0:T(8,128)S(1)}, f32[5,32,256]{2,1,0:T(8,128)S(1)}, f32[5,16,128]{2,1,0:T(8,128)S(1)}, f32[5,16,128]{2,1,0:T(8,128)S(1)}) custom-call(f32[5,32,16,256]{3,2,1,0:T(8,128)S(1)} %copy-done), custom_call_target="tpu_custom_call" | custom-call | tf_op jit(solution)/shard_map/pallas_call | solution.py:571
  3.4 0.0 copy-start.5
  3.4 2.6 %collective-permute-start.2 = (f32[5,32,256]{2,1,0:T(8,128)S(1)}, f32[5,32,256]{2,1,0:T(8,128)S(1)}, u32[]{:S(2)}, u32[]{:S(2)}) collective-permute-start(f32[5,32,256]{2,1,0:T(8,128)S(1)} %get-tuple-element.30), channel_id=1, source_target_pairs={{0,1},{1,0},{2,3},{3,2},{4,5},{5,4},{6,7},{7,6},{8,9},{9,8},{10,11... | collective-permute-start | bytes 491528 | tf_op jit(solution)/shard_map/ppermute | solution.py:521
  5.9 1.3 %collective-permute-start.4 = (f32[5,16,128]{2,1,0:T(8,128)S(1)}, f32[5,16,128]{2,1,0:T(8,128)S(1)}, u32[]{:S(2)}, u32[]{:S(2)}) collective-permute-start(f32[5,16,128]{2,1,0:T(8,128)S(1)} %get-tuple-element.32), channel_id=1, source_target_pairs={{0,12},{2,6},{4,0},{6,10},{8,4},{10,14},{12,8},{14,2},{1,13},{3,7}... | collective-permute-start | bytes 122888 | tf_op jit(solution)/shard_map/ppermute | solution.py:521
  7.2 1.2 %collective-permute-start = (f32[5,16,256]{2,1,0:T(8,128)S(1)}, f32[5,16,256]{2,1,0:T(8,128)S(1)}, u32[]{:S(2)}, u32[]{:S(2)}) collective-permute-start(f32[5,16,256]{2,1,0:T(8,128)S(1)} %get-tuple-element.28), channel_id=1, source_target_pairs={{0,16},{16,0},{32,48},{48,32},{1,17},{17,1},{33,49},{49,33},{2,18}... | collective-permute-start | bytes 245768 | tf_op jit(solution)/shard_map/ppermute | solution.py:521
  8.5 6.7 %collective-permute-start.1 = (f32[5,16,256]{2,1,0:T(8,128)S(1)}, f32[5,16,256]{2,1,0:T(8,128)S(1)}, u32[]{:S(2)}, u32[]{:S(2)}) collective-permute-start(f32[5,16,256]{2,1,0:T(8,128)S(1)} %get-tuple-element.29), channel_id=1, source_target_pairs={{0,240},{16,32},{32,16},{48,64},{64,48},{80,96},{96,80},{112,128},... | collective-permute-start | bytes 245768 | tf_op jit(solution)/shard_map/ppermute | solution.py:521
  15.1 3.2 %collective-permute-start.3 = (f32[5,16,128]{2,1,0:T(8,128)S(1)}, f32[5,16,128]{2,1,0:T(8,128)S(1)}, u32[]{:S(2)}, u32[]{:S(2)}) collective-permute-start(f32[5,16,128]{2,1,0:T(8,128)S(1)} %get-tuple-element.31), channel_id=1, source_target_pairs={{0,2},{2,0},{1,3},{3,1},{4,6},{6,4},{5,7},{7,5},{8,10},{10,8},{9,1... | collective-permute-start | bytes 122888 | tf_op jit(solution)/shard_map/ppermute | solution.py:521
  18.3 0.0 collective-permute-done.4
  18.3 0.0 collective-permute-start.5
  18.4 1.4 %copy-done.2 = f32[64,3,1,4,512]{4,3,2,1,0:T(4,128)S(1)} copy-done((f32[64,3,1,4,512]{4,3,2,1,0:T(4,128)S(1)}, f32[64,3,1,4,512]{4,3,2,1,0:T(4,128)}, u32[]{:S(2)}) %copy-start.2) | copy-done | bytes 1572888
  19.8 1.0 %copy-done.3 = f32[16,3,1,4,512]{4,3,2,1,0:T(4,128)S(1)} copy-done((f32[16,3,1,4,512]{4,3,2,1,0:T(4,128)S(1)}, f32[16,3,1,4,512]{4,3,2,1,0:T(4,128)}, u32[]{:S(2)}) %copy-start.3) | copy-done | bytes 393240
  20.8 1.5 %shard_map.93 = (f32[80,6144]{1,0:T(8,128)S(1)}, f32[48,128]{1,0:T(8,128)S(1)}) custom-call(f32[64,3,1,4,512]{4,3,2,1,0:T(4,128)S(1)} %copy-done.2, f32[16,3,1,4,512]{4,3,2,1,0:T(4,128)S(1)} %copy-done.3), custom_call_target="tpu_custom_call" | custom-call | tf_op jit(solution)/shard_map/pallas_call | solution.py:577
  22.3 0.0 collective-permute-done.5.z_next_in
  22.3 0.0 collective-permute-done.2.y_halo
  22.3 4.9 %shard_map.95 = (f32[5,32,16,256]{3,2,1,0:T(8,128)S(1)}, f32[5,16,256]{2,1,0:T(8,128)S(1)}, f32[5,16,256]{2,1,0:T(8,128)S(1)}, f32[5,40,256]{2,1,0:T(8,128)S(1)}...) custom-call(f32[5]{0:T(128)S(1)} %copy-done.4, f32[48,128]{1,0:T(8,128)S(1)} %get-tuple-element.27.folded, ...), custom_call_target="tpu_custom_call" | custom-call | tf_op jit(solution)/shard_map/pallas_call | solution.py:583
  27.3 0.8 %collective-permute-start.8 = (f32[5,40,256]{2,1,0:T(8,128)S(1)}, f32[5,40,256]{2,1,0:T(8,128)S(1)}, u32[]{:S(2)}, u32[]{:S(2)}) collective-permute-start(f32[5,40,256]{2,1,0:T(8,128)S(1)} %get-tuple-element.36), channel_id=1, source_target_pairs={{0,1},{1,0},{2,3},{3,2},{4,5},{5,4},{6,7},{7,6},{8,9},{9,8},{10,11... | collective-permute-start | bytes 614408 | tf_op jit(solution)/shard_map/ppermute | solution.py:521
  28.1 0.0 collective-permute-start.10
  28.1 0.0 collective-permute-start.6
  28.1 3.4 %collective-permute-start.7 = (f32[5,16,256]{2,1,0:T(8,128)S(1)}, f32[5,16,256]{2,1,0:T(8,128)S(1)}, u32[]{:S(2)}, u32[]{:S(2)}) collective-permute-start(f32[5,16,256]{2,1,0:T(8,128)S(1)} %get-tuple-element.35), channel_id=1, source_target_pairs={{0,240},{16,32},{32,16},{48,64},{64,48},{80,96},{96,80},{112,128},... | collective-permute-start | bytes 245768 | tf_op jit(solution)/shard_map/ppermute | solution.py:521
  31.5 2.4 %collective-permute-start.9 = (f32[5,16,128]{2,1,0:T(8,128)S(1)}, f32[5,16,128]{2,1,0:T(8,128)S(1)}, u32[]{:S(2)}, u32[]{:S(2)}) collective-permute-start(f32[5,16,128]{2,1,0:T(8,128)S(1)} %get-tuple-element.37), channel_id=1, source_target_pairs={{0,2},{2,0},{1,3},{3,1},{4,6},{6,4},{5,7},{7,5},{8,10},{10,8},{9,1... | collective-permute-start | bytes 122888 | tf_op jit(solution)/shard_map/ppermute | solution.py:521
  33.9 0.0 collective-permute-start.11
  34.5 0.2 collective-permute-done.9.z_pair
  34.7 0.4 collective-permute-done.11.z_next
  35.1 0.3 collective-permute-done.8.y_halo
  35.4 4.7 %shard_map.96 = (f32[5,32,16,256]{3,2,1,0:T(8,128)}, f32[128,256]{1,0:T(8,128)S(1)}) custom-call(f32[5]{0:T(128)S(1)} %copy-done.4, s32[3]{0:T(128)S(1)} %copy-done.5, f32[5,32,16,256]{3,2,1,0:T(8,128)S(1)} %copy-done.1, f32[5,32,16,256]{3,2,1,0:T(8,128)S(1)} %get-tuple-element.33.current, f32[5,40,256]{2,1,0:T(8,128)S(1)} %collective-permute-done.8.y_halo, ...), custom_call_target="tpu_custom_call" | custom-call | flops 20000000 | bytes 20000000 | tf_op jit(solution)/shard_map/pallas_call | solution.py:593
  40.1 1.6 %shard_map.97 = (f32[5,32,16,256]{3,2,1,0:T(8,128)}, f32[64,128]{1,0:T(8,128)S(1)}, s32[8,128]{1,0:T(8,128)S(1)}) custom-call(f32[5]{0:T(128)S(1)} %copy-done.4, s32[3]{0:T(128)S(1)} %copy-done.5, s32[1]{0:T(128)S(6)} %copy.14.column_id, f32[48,128]{1,0:T(8,128)S(1)} %get-tuple-element.27.folded, ...), custom_call_target="tpu_custom_call", output_to_operand_aliasing={{0}: (12, {})} | custom-call | tf_op jit(solution)/shard_map/pallas_call | solution.py:601
  41.7 8.6 %all_to_all.15.relayed = f32[8,8,128]{2,1,0:T(8,128)S(1)} all-to-all(f32[8,8,128]{2,1,0:T(8,128)S(1)} %bitcast.14), channel_id=1, replica_groups=mesh['zh'=4,'x'=4,'y'=4,'core'=2,'zl'=2] {'y','core'}, dimensions={0} | all-to-all | bytes 65536 | tf_op jit(solution)/shard_map/all_to_all | solution.py:617
  50.3 0.4 shard_map.98
  50.8 10.8 %all_to_all.16 = f32[96,1,128]{2,1,0:T(1,128)S(1)} all-to-all(f32[96,1,128]{2,1,0:T(1,128)S(1)} %bitcast.13), channel_id=1, replica_groups=mesh['zh'=4,'x'=4,'y'=4,'core'=2,'zl'=2] {'x','y','core'}, dimensions={0} | all-to-all | bytes 98304 | tf_op jit(solution)/shard_map/all_to_all | solution.py:546
  61.6 11.6 %all_to_all.17 = f32[136,1,128]{2,1,0:T(1,128)S(1)} all-to-all(f32[136,1,128]{2,1,0:T(1,128)S(1)} %bitcast.11), channel_id=1, replica_groups=mesh['zh'=4,'x'=4,'y'=4,'core'=2,'zl'=2] {'zh','zl'}, dimensions={0} | all-to-all | bytes 139264 | tf_op jit(solution)/shard_map/all_to_all | solution.py:546
  73.1 3.9 %shard_map.100 = (f32[16,64]{1,0:T(8,128)}, f32[16,16]{1,0:T(8,128)}, f32[16,3,1,4,512]{4,3,2,1,0:T(4,128)}) custom-call(s32[8,128]{1,0:T(8,128)S(1)} %get-tuple-element.42.chosen_column, f32[136,128]{1,0:T(8,128)S(1)} %bitcast.10, f32[80,6144]{1,0:T(8,128)S(1)} %get-tuple-element.44.joined, f32[8,6144]{1,0:T(8,128)S(1)} %get-tuple-element.46.column), custom_call_target="tpu_custom_call" | custom-call | tf_op jit(solution)/shard_map/pallas_call | solution.py:632
  (15 shorter events, 0.1 us)
Async XLA Ops:
  0.6 1.7 %copy-start = (f32[5,32,16,256]{3,2,1,0:T(8,128)S(1)}, f32[5,32,16,256]{3,2,1,0:T(8,128)}, u32[]{:S(2)}) copy-start(f32[5,32,16,256]{3,2,1,0:T(8,128)} %start.3) | copy-start | bytes 7864324
  2.4 19.9 %copy-start.1 = (f32[5,32,16,256]{3,2,1,0:T(8,128)S(1)}, f32[5,32,16,256]{3,2,1,0:T(8,128)}, u32[]{:S(2)}) copy-start(f32[5,32,16,256]{3,2,1,0:T(8,128)} %start.3) | copy-start | bytes 7864324
  2.4 20.0 %copy-start.4 = (f32[5]{0:T(128)S(1)}, f32[5]{0:T(128)}, u32[]{:S(2)}) copy-start(f32[5]{0:T(128)} %diffusivity.5) | copy-start | bytes 64
  3.4 32.0 %copy-start.5 = (s32[3]{0:T(128)S(1)}, s32[3]{0:T(128)}, u32[]{:S(2)}) copy-start(s32[3]{0:T(128)} %offsets.3) | copy-start | bytes 40
  3.4 18.9 %collective-permute-start.2 = (f32[5,32,256]{2,1,0:T(8,128)S(1)}, f32[5,32,256]{2,1,0:T(8,128)S(1)}, u32[]{:S(2)}, u32[]{:S(2)}) collective-permute-start(f32[5,32,256]{2,1,0:T(8,128)S(1)} %get-tuple-element.30), channel_id=1, source_target_pairs={{0,1},{1,0},{2,3},{3,2},{4,5},{5,4},{6,7},{7,6},{8,9},{9,8},{10,11... | collective-permute-start | bytes 491528 | tf_op jit(solution)/shard_map/ppermute | solution.py:521
  5.9 12.4 %collective-permute-start.4 = (f32[5,16,128]{2,1,0:T(8,128)S(1)}, f32[5,16,128]{2,1,0:T(8,128)S(1)}, u32[]{:S(2)}, u32[]{:S(2)}) collective-permute-start(f32[5,16,128]{2,1,0:T(8,128)S(1)} %get-tuple-element.32), channel_id=1, source_target_pairs={{0,12},{2,6},{4,0},{6,10},{8,4},{10,14},{12,8},{14,2},{1,13},{3,7}... | collective-permute-start | bytes 122888 | tf_op jit(solution)/shard_map/ppermute | solution.py:521
  7.2 15.0 %collective-permute-start = (f32[5,16,256]{2,1,0:T(8,128)S(1)}, f32[5,16,256]{2,1,0:T(8,128)S(1)}, u32[]{:S(2)}, u32[]{:S(2)}) collective-permute-start(f32[5,16,256]{2,1,0:T(8,128)S(1)} %get-tuple-element.28), channel_id=1, source_target_pairs={{0,16},{16,0},{32,48},{48,32},{1,17},{17,1},{33,49},{49,33},{2,18}... | collective-permute-start | bytes 245768 | tf_op jit(solution)/shard_map/ppermute | solution.py:521
  8.5 13.8 %collective-permute-start.1 = (f32[5,16,256]{2,1,0:T(8,128)S(1)}, f32[5,16,256]{2,1,0:T(8,128)S(1)}, u32[]{:S(2)}, u32[]{:S(2)}) collective-permute-start(f32[5,16,256]{2,1,0:T(8,128)S(1)} %get-tuple-element.29), channel_id=1, source_target_pairs={{0,240},{16,32},{32,16},{48,64},{64,48},{80,96},{96,80},{112,128},... | collective-permute-start | bytes 245768 | tf_op jit(solution)/shard_map/ppermute | solution.py:521
  15.1 7.2 %collective-permute-start.3 = (f32[5,16,128]{2,1,0:T(8,128)S(1)}, f32[5,16,128]{2,1,0:T(8,128)S(1)}, u32[]{:S(2)}, u32[]{:S(2)}) collective-permute-start(f32[5,16,128]{2,1,0:T(8,128)S(1)} %get-tuple-element.31), channel_id=1, source_target_pairs={{0,2},{2,0},{1,3},{3,1},{4,6},{6,4},{5,7},{7,5},{8,10},{10,8},{9,1... | collective-permute-start | bytes 122888 | tf_op jit(solution)/shard_map/ppermute | solution.py:521
  18.3 3.9 %collective-permute-start.5 = (f32[5,16,128]{2,1,0:T(8,128)S(1)}, f32[5,16,128]{2,1,0:T(8,128)S(1)}, u32[]{:S(2)}, u32[]{:S(2)}) collective-permute-start(f32[5,16,128]{2,1,0:T(8,128)S(1)} %collective-permute-done.4), channel_id=1, source_target_pairs={{0,2},{2,0},{1,3},{3,1},{4,6},{6,4},{5,7},{7,5},{8,10},{10,8},{9,1... | collective-permute-start | bytes 122888 | tf_op jit(solution)/shard_map/ppermute | solution.py:521
  18.4 1.4 %copy-start.2 = (f32[64,3,1,4,512]{4,3,2,1,0:T(4,128)S(1)}, f32[64,3,1,4,512]{4,3,2,1,0:T(4,128)}, u32[]{:S(2)}) copy-start(f32[64,3,1,4,512]{4,3,2,1,0:T(4,128)} %basis.1) | copy-start | bytes 4718596
  19.8 1.0 %copy-start.3 = (f32[16,3,1,4,512]{4,3,2,1,0:T(4,128)S(1)}, f32[16,3,1,4,512]{4,3,2,1,0:T(4,128)}, u32[]{:S(2)}) copy-start(f32[16,3,1,4,512]{4,3,2,1,0:T(4,128)} %held.1) | copy-start | bytes 1179652
  27.3 8.1 %collective-permute-start.8 = (f32[5,40,256]{2,1,0:T(8,128)S(1)}, f32[5,40,256]{2,1,0:T(8,128)S(1)}, u32[]{:S(2)}, u32[]{:S(2)}) collective-permute-start(f32[5,40,256]{2,1,0:T(8,128)S(1)} %get-tuple-element.36), channel_id=1, source_target_pairs={{0,1},{1,0},{2,3},{3,2},{4,5},{5,4},{6,7},{7,6},{8,9},{9,8},{10,11... | collective-permute-start | bytes 614408 | tf_op jit(solution)/shard_map/ppermute | solution.py:521
  28.1 5.8 %collective-permute-start.10 = (f32[5,16,128]{2,1,0:T(8,128)S(1)}, f32[5,16,128]{2,1,0:T(8,128)S(1)}, u32[]{:S(2)}, u32[]{:S(2)}) collective-permute-start(f32[5,16,128]{2,1,0:T(8,128)S(1)} %get-tuple-element.38), channel_id=1, source_target_pairs={{0,12},{2,6},{4,0},{6,10},{8,4},{10,14},{12,8},{14,2},{1,13},{3,7}... | collective-permute-start | bytes 122888 | tf_op jit(solution)/shard_map/ppermute | solution.py:521
  28.1 12.1 %collective-permute-start.6 = (f32[5,16,256]{2,1,0:T(8,128)S(1)}, f32[5,16,256]{2,1,0:T(8,128)S(1)}, u32[]{:S(2)}, u32[]{:S(2)}) collective-permute-start(f32[5,16,256]{2,1,0:T(8,128)S(1)} %get-tuple-element.34), channel_id=1, source_target_pairs={{0,16},{16,0},{32,48},{48,32},{1,17},{17,1},{33,49},{49,33},{2,18}... | collective-permute-start | bytes 245768 | tf_op jit(solution)/shard_map/ppermute | solution.py:521
  28.1 12.1 %collective-permute-start.7 = (f32[5,16,256]{2,1,0:T(8,128)S(1)}, f32[5,16,256]{2,1,0:T(8,128)S(1)}, u32[]{:S(2)}, u32[]{:S(2)}) collective-permute-start(f32[5,16,256]{2,1,0:T(8,128)S(1)} %get-tuple-element.35), channel_id=1, source_target_pairs={{0,240},{16,32},{32,16},{48,64},{64,48},{80,96},{96,80},{112,128},... | collective-permute-start | bytes 245768 | tf_op jit(solution)/shard_map/ppermute | solution.py:521
  31.5 3.3 %collective-permute-start.9 = (f32[5,16,128]{2,1,0:T(8,128)S(1)}, f32[5,16,128]{2,1,0:T(8,128)S(1)}, u32[]{:S(2)}, u32[]{:S(2)}) collective-permute-start(f32[5,16,128]{2,1,0:T(8,128)S(1)} %get-tuple-element.37), channel_id=1, source_target_pairs={{0,2},{2,0},{1,3},{3,1},{4,6},{6,4},{5,7},{7,5},{8,10},{10,8},{9,1... | collective-permute-start | bytes 122888 | tf_op jit(solution)/shard_map/ppermute | solution.py:521
  33.9 1.2 %collective-permute-start.11 = (f32[5,16,128]{2,1,0:T(8,128)S(1)}, f32[5,16,128]{2,1,0:T(8,128)S(1)}, u32[]{:S(2)}, u32[]{:S(2)}) collective-permute-start(f32[5,16,128]{2,1,0:T(8,128)S(1)} %collective-permute-done.10), channel_id=1, source_target_pairs={{0,2},{2,0},{1,3},{3,1},{4,6},{6,4},{5,7},{7,5},{8,10},{10,8},{9,1... | collective-permute-start | bytes 122888 | tf_op jit(solution)/shard_map/ppermute | solution.py:521

commit v8 on v7

--- a/solution.py
+++ b/solution.py
@@ -106,7 +106,7 @@
     return [(i + jnp.where(upper, 0, 1)) % 8 for i in range(8)]
 
 
-def pack_kernel(fields, x_pair, x_next, y_row, z_pair, z_next):
+def pack_kernel(fields, x_next, x_pair, y_row, z_pair, z_next):
     rows = row_shifts(lax.axis_index("zl") > 0)
     pack(fields, rows, x_pair, x_next, y_row, z_pair, z_next)
 
@@ -247,8 +247,8 @@
 
 
 def first_kernel(
-    diffusivity, folded, current, x_pair_in, x_next_in, y_halo, z_pair_in, z_next_in,
-    first, x_pair, x_next, y_row, z_pair, z_next, *edges,
+    diffusivity, folded, current, x_next_in, x_pair_in, y_halo, z_pair_in, z_next_in,
+    first, x_next, x_pair, y_row, z_pair, z_next, *edges,
 ):
     count, cells = current.shape[:2]
     upper = lax.axis_index("zl") > 0
@@ -320,7 +320,7 @@
 
 
 def outer_kernel(
-    diffusivity, offsets, column_id, folded, start, current, x_pair, x_next, y_halo, z_pair,
+    diffusivity, offsets, column_id, folded, start, current, x_next, x_pair, y_halo, z_pair,
     z_next, picked_in, target_in, target, snapshot, chosen, y_low, y_high, z_before, z_after, picked, result,
     semaphores,
 ):
@@ -522,7 +522,7 @@
 
 
 def exchange(faces):
-    x_pair, x_next, y_row, z_pair, z_next = faces
+    x_next, x_pair, y_row, z_pair, z_next = faces
 
     def along(zh, x):
         step = x + 1 if x % 2 else x - 1
@@ -533,8 +533,8 @@
 
     z_next = moved(z_next, ("y", "core"), lambda y, core: (y + 2 * core - 1, core))
     return (
+        moved(x_next, ("zh", "x"), along),
         moved(x_pair, ("x",), lambda x: (x ^ 1,)),
-        moved(x_next, ("zh", "x"), along),
         moved(y_row, ("zl",), lambda zl: (zl + 1,)),
         moved(z_pair, ("core",), swap),
         moved(z_next, ("core",), swap),
@@ -588,7 +588,7 @@
     )(diffusivity, folded, fields, *halos)
     halos = exchange(packed)
 
-    x_pair, x_next, *halos = halos
+    x_next, x_pair, *halos = halos
     sides = [wall, wall, edge, edge]
     fields_out, picked = pl.pallas_call(
         inner_kernel, in_specs=[SMEM] * 2 + [VMEM] * 5, out_specs=[ANY, VMEM],
@@ -611,7 +611,7 @@
         ],
         input_output_aliases={12: 0}, compiler_params=params(24),
     )(
-        diffusivity, subsample_offsets, column_id, folded, fields, first, x_pair, x_next,
+        diffusivity, subsample_offsets, column_id, folded, fields, first, x_next, x_pair,
         *halos, picked, fields_out,
     )
     relayed = lax.all_to_all(snapshot.reshape(8, 8, LANES), ("y", "core"), 0, 0, tiled=True)

time: 77.3 us -> 77 us (level)
  starting transfers between devices: 21.6 us -> 20.7 us
  blocking collectives: 31 us -> 31.8 us
    all_to_all x1, blocking collectives: 8.62 us -> 9.92 us  [on_device(): lax.all_to_all(snapshot.reshape(8, 8, LANES), ('y', 'core'), 0, 0, tiled=...]
    ppermute x12, starting transfers between devices: 21.6 us -> 20.7 us  [moved(): return lax.ppermute(value, axes, pairs)]
  transfers between devices with their start and end apart: 12 -> 12, of which waited for: 3 -> 2; matrix products, arithmetic and copies ran while one was open for 0% -> 0% of each run, Pallas kernels for 8% -> 8%
where the time goes in v8:
time: 77 us; the launch traced here: 76.7 us
  blocking collectives  31.8 us (41%)
  starting transfers between devices  20.7 us (27%)
  Pallas kernels  18 us (23%)
  local copies, waits for them, and re-layouts  4.15 us (5%)
  between operations  1.42 us (2%)
    all_to_all x2, blocking collectives, everyone(): lax.all_to_all(message.reshape(rows, 1, LANES), axes, 0, 0, tiled=True)  21.9 us
    ppermute x12, starting transfers between devices, moved(): return lax.ppermute(value, axes, pairs)  20.7 us
    all_to_all x1, blocking collectives, on_device(): lax.all_to_all(snapshot.reshape(8, 8, LANES), ('y', 'core'), 0, 0, tiled=...  9.92 us
    pallas_call x1, Pallas kernels, on_device(): pl.pallas_call(first_kernel, in_specs=[SMEM] + [VMEM] * 7, out_specs=[VME...  4.91 us
    pallas_call x1, Pallas kernels, on_device(): pl.pallas_call(inner_kernel, in_specs=[SMEM] * 2 + [VMEM] * 5, out_specs=...  4.73 us
    unnamed x12, local copies, waits for them, and re-layouts  4.15 us
    pallas_call x1, Pallas kernels, on_device(): pl.pallas_call(functools.partial(final_kernel, float(devices * length)),...  3.88 us
    pallas_call x1, Pallas kernels, on_device(): pl.pallas_call(outer_kernel, in_specs=[SMEM] * 3 + [VMEM] * 9 + [ANY], ou...  1.55 us
  transfers between devices with their start and end apart: 12, of which 2 were waited for; matrix products, arithmetic and copies ran while one was open for 0% of the time, Pallas kernels for 8%

profile of v8, /device:TPU:1, one launch (start us, length us, event | category | flops | bytes accessed | tf_op | source)
XLA Modules:
  0.0 76.7 jit_solution(12605107568635367941)
XLA Ops:
  0.6 1.7 %copy-done = f32[5,32,16,256]{3,2,1,0:T(8,128)S(1)} copy-done((f32[5,32,16,256]{3,2,1,0:T(8,128)S(1)}, f32[5,32,16,256]{3,2,1,0:T(8,128)}, u32[]{:S(2)}) %copy-start) | copy-done | bytes 2621464
  2.4 1.0 %shard_map.94 = (f32[5,16,256]{2,1,0:T(8,128)S(1)}, f32[5,16,256]{2,1,0:T(8,128)S(1)}, f32[5,32,256]{2,1,0:T(8,128)S(1)}, f32[5,16,128]{2,1,0:T(8,128)S(1)}, f32[5,16,128]{2,1,0:T(8,128)S(1)}) custom-call(f32[5,32,16,256]{3,2,1,0:T(8,128)S(1)} %copy-done), custom_call_target="tpu_custom_call" | custom-call | tf_op jit(solution)/shard_map/pallas_call | solution.py:571
  3.4 0.0 copy-start.5
  3.4 2.6 %collective-permute-start.2 = (f32[5,32,256]{2,1,0:T(8,128)S(1)}, f32[5,32,256]{2,1,0:T(8,128)S(1)}, u32[]{:S(2)}, u32[]{:S(2)}) collective-permute-start(f32[5,32,256]{2,1,0:T(8,128)S(1)} %get-tuple-element.30), channel_id=1, source_target_pairs={{0,1},{1,0},{2,3},{3,2},{4,5},{5,4},{6,7},{7,6},{8,9},{9,8},{10,11... | collective-permute-start | bytes 491528 | tf_op jit(solution)/shard_map/ppermute | solution.py:521
  5.9 1.3 %collective-permute-start.4 = (f32[5,16,128]{2,1,0:T(8,128)S(1)}, f32[5,16,128]{2,1,0:T(8,128)S(1)}, u32[]{:S(2)}, u32[]{:S(2)}) collective-permute-start(f32[5,16,128]{2,1,0:T(8,128)S(1)} %get-tuple-element.32), channel_id=1, source_target_pairs={{0,12},{2,6},{4,0},{6,10},{8,4},{10,14},{12,8},{14,2},{1,13},{3,7}... | collective-permute-start | bytes 122888 | tf_op jit(solution)/shard_map/ppermute | solution.py:521
  7.2 7.3 %collective-permute-start = (f32[5,16,256]{2,1,0:T(8,128)S(1)}, f32[5,16,256]{2,1,0:T(8,128)S(1)}, u32[]{:S(2)}, u32[]{:S(2)}) collective-permute-start(f32[5,16,256]{2,1,0:T(8,128)S(1)} %get-tuple-element.28), channel_id=1, source_target_pairs={{0,240},{16,32},{32,16},{48,64},{64,48},{80,96},{96,80},{112,128},... | collective-permute-start | bytes 245768 | tf_op jit(solution)/shard_map/ppermute | solution.py:521
  14.6 0.0 collective-permute-start.1
  14.6 3.0 %collective-permute-start.3 = (f32[5,16,128]{2,1,0:T(8,128)S(1)}, f32[5,16,128]{2,1,0:T(8,128)S(1)}, u32[]{:S(2)}, u32[]{:S(2)}) collective-permute-start(f32[5,16,128]{2,1,0:T(8,128)S(1)} %get-tuple-element.31), channel_id=1, source_target_pairs={{0,2},{2,0},{1,3},{3,1},{4,6},{6,4},{5,7},{7,5},{8,10},{10,8},{9,1... | collective-permute-start | bytes 122888 | tf_op jit(solution)/shard_map/ppermute | solution.py:521
  17.5 0.0 collective-permute-done.4
  17.5 0.1 collective-permute-start.5
  17.6 1.4 %copy-done.2 = f32[64,3,1,4,512]{4,3,2,1,0:T(4,128)S(1)} copy-done((f32[64,3,1,4,512]{4,3,2,1,0:T(4,128)S(1)}, f32[64,3,1,4,512]{4,3,2,1,0:T(4,128)}, u32[]{:S(2)}) %copy-start.2) | copy-done | bytes 1572888
  19.0 1.0 %copy-done.3 = f32[16,3,1,4,512]{4,3,2,1,0:T(4,128)S(1)} copy-done((f32[16,3,1,4,512]{4,3,2,1,0:T(4,128)S(1)}, f32[16,3,1,4,512]{4,3,2,1,0:T(4,128)}, u32[]{:S(2)}) %copy-start.3) | copy-done | bytes 393240
  20.0 1.5 %shard_map.93 = (f32[80,6144]{1,0:T(8,128)S(1)}, f32[48,128]{1,0:T(8,128)S(1)}) custom-call(f32[64,3,1,4,512]{4,3,2,1,0:T(4,128)S(1)} %copy-done.2, f32[16,3,1,4,512]{4,3,2,1,0:T(4,128)S(1)} %copy-done.3), custom_call_target="tpu_custom_call" | custom-call | tf_op jit(solution)/shard_map/pallas_call | solution.py:577
  21.5 0.0 collective-permute-done.5.z_next_in
  21.5 0.0 collective-permute-done.x_next_in
  21.6 0.0 collective-permute-done.2.y_halo
  21.6 4.9 %shard_map.95 = (f32[5,32,16,256]{3,2,1,0:T(8,128)S(1)}, f32[5,16,256]{2,1,0:T(8,128)S(1)}, f32[5,16,256]{2,1,0:T(8,128)S(1)}, f32[5,40,256]{2,1,0:T(8,128)S(1)}...) custom-call(f32[5]{0:T(128)S(1)} %copy-done.4, f32[48,128]{1,0:T(8,128)S(1)} %get-tuple-element.27.folded, ...), custom_call_target="tpu_custom_call" | custom-call | tf_op jit(solution)/shard_map/pallas_call | solution.py:583
  26.5 0.8 %collective-permute-start.8 = (f32[5,40,256]{2,1,0:T(8,128)S(1)}, f32[5,40,256]{2,1,0:T(8,128)S(1)}, u32[]{:S(2)}, u32[]{:S(2)}) collective-permute-start(f32[5,40,256]{2,1,0:T(8,128)S(1)} %get-tuple-element.36), channel_id=1, source_target_pairs={{0,1},{1,0},{2,3},{3,2},{4,5},{5,4},{6,7},{7,6},{8,9},{9,8},{10,11... | collective-permute-start | bytes 614408 | tf_op jit(solution)/shard_map/ppermute | solution.py:521
  27.3 0.0 collective-permute-start.10
  27.3 3.6 %collective-permute-start.6 = (f32[5,16,256]{2,1,0:T(8,128)S(1)}, f32[5,16,256]{2,1,0:T(8,128)S(1)}, u32[]{:S(2)}, u32[]{:S(2)}) collective-permute-start(f32[5,16,256]{2,1,0:T(8,128)S(1)} %get-tuple-element.34), channel_id=1, source_target_pairs={{0,240},{16,32},{32,16},{48,64},{64,48},{80,96},{96,80},{112,128},... | collective-permute-start | bytes 245768 | tf_op jit(solution)/shard_map/ppermute | solution.py:521
  31.0 0.0 collective-permute-start.7
  31.0 2.0 %collective-permute-start.9 = (f32[5,16,128]{2,1,0:T(8,128)S(1)}, f32[5,16,128]{2,1,0:T(8,128)S(1)}, u32[]{:S(2)}, u32[]{:S(2)}) collective-permute-start(f32[5,16,128]{2,1,0:T(8,128)S(1)} %get-tuple-element.37), channel_id=1, source_target_pairs={{0,2},{2,0},{1,3},{3,1},{4,6},{6,4},{5,7},{7,5},{8,10},{10,8},{9,1... | collective-permute-start | bytes 122888 | tf_op jit(solution)/shard_map/ppermute | solution.py:521
  33.0 0.1 collective-permute-start.11
  33.7 0.1 collective-permute-done.9.z_pair
  33.8 0.4 collective-permute-done.11.z_next
  34.2 4.7 %shard_map.96 = (f32[5,32,16,256]{3,2,1,0:T(8,128)}, f32[128,256]{1,0:T(8,128)S(1)}) custom-call(f32[5]{0:T(128)S(1)} %copy-done.4, s32[3]{0:T(128)S(1)} %copy-done.5, f32[5,32,16,256]{3,2,1,0:T(8,128)S(1)} %copy-done.1, f32[5,32,16,256]{3,2,1,0:T(8,128)S(1)} %get-tuple-element.33.current, f32[5,40,256]{2,1,0:T(8,128)S(1)} %collective-permute-done.8.y_halo, ...), custom_call_target="tpu_custom_call" | custom-call | flops 20000000 | bytes 20000000 | tf_op jit(solution)/shard_map/pallas_call | solution.py:593
  38.9 1.6 %shard_map.97 = (f32[5,32,16,256]{3,2,1,0:T(8,128)}, f32[64,128]{1,0:T(8,128)S(1)}, s32[8,128]{1,0:T(8,128)S(1)}) custom-call(f32[5]{0:T(128)S(1)} %copy-done.4, s32[3]{0:T(128)S(1)} %copy-done.5, s32[1]{0:T(128)S(6)} %copy.14.column_id, f32[48,128]{1,0:T(8,128)S(1)} %get-tuple-element.27.folded, ...), custom_call_target="tpu_custom_call", output_to_operand_aliasing={{0}: (12, {})} | custom-call | tf_op jit(solution)/shard_map/pallas_call | solution.py:601
  40.5 9.9 %all_to_all.15.relayed = f32[8,8,128]{2,1,0:T(8,128)S(1)} all-to-all(f32[8,8,128]{2,1,0:T(8,128)S(1)} %bitcast.14), channel_id=1, replica_groups=mesh['zh'=4,'x'=4,'y'=4,'core'=2,'zl'=2] {'y','core'}, dimensions={0} | all-to-all | bytes 65536 | tf_op jit(solution)/shard_map/all_to_all | solution.py:617
  50.4 0.4 shard_map.98
  50.9 10.8 %all_to_all.16 = f32[96,1,128]{2,1,0:T(1,128)S(1)} all-to-all(f32[96,1,128]{2,1,0:T(1,128)S(1)} %bitcast.13), channel_id=1, replica_groups=mesh['zh'=4,'x'=4,'y'=4,'core'=2,'zl'=2] {'x','y','core'}, dimensions={0} | all-to-all | bytes 98304 | tf_op jit(solution)/shard_map/all_to_all | solution.py:546
  61.7 11.1 %all_to_all.17 = f32[136,1,128]{2,1,0:T(1,128)S(1)} all-to-all(f32[136,1,128]{2,1,0:T(1,128)S(1)} %bitcast.11), channel_id=1, replica_groups=mesh['zh'=4,'x'=4,'y'=4,'core'=2,'zl'=2] {'zh','zl'}, dimensions={0} | all-to-all | bytes 139264 | tf_op jit(solution)/shard_map/all_to_all | solution.py:546
  72.8 3.9 %shard_map.100 = (f32[16,64]{1,0:T(8,128)}, f32[16,16]{1,0:T(8,128)}, f32[16,3,1,4,512]{4,3,2,1,0:T(4,128)}) custom-call(s32[8,128]{1,0:T(8,128)S(1)} %get-tuple-element.42.chosen_column, f32[136,128]{1,0:T(8,128)S(1)} %bitcast.10, f32[80,6144]{1,0:T(8,128)S(1)} %get-tuple-element.44.joined, f32[8,6144]{1,0:T(8,128)S(1)} %get-tuple-element.46.column), custom_call_target="tpu_custom_call" | custom-call | tf_op jit(solution)/shard_map/pallas_call | solution.py:632
  (15 shorter events, 0.1 us)
Async XLA Ops:
  0.6 1.7 %copy-start = (f32[5,32,16,256]{3,2,1,0:T(8,128)S(1)}, f32[5,32,16,256]{3,2,1,0:T(8,128)}, u32[]{:S(2)}) copy-start(f32[5,32,16,256]{3,2,1,0:T(8,128)} %start.3) | copy-start | bytes 7864324
  2.4 19.2 %copy-start.1 = (f32[5,32,16,256]{3,2,1,0:T(8,128)S(1)}, f32[5,32,16,256]{3,2,1,0:T(8,128)}, u32[]{:S(2)}) copy-start(f32[5,32,16,256]{3,2,1,0:T(8,128)} %start.3) | copy-start | bytes 7864324
  2.4 19.2 %copy-start.4 = (f32[5]{0:T(128)S(1)}, f32[5]{0:T(128)}, u32[]{:S(2)}) copy-start(f32[5]{0:T(128)} %diffusivity.5) | copy-start | bytes 64
  3.4 30.8 %copy-start.5 = (s32[3]{0:T(128)S(1)}, s32[3]{0:T(128)}, u32[]{:S(2)}) copy-start(s32[3]{0:T(128)} %offsets.3) | copy-start | bytes 40
  3.4 18.2 %collective-permute-start.2 = (f32[5,32,256]{2,1,0:T(8,128)S(1)}, f32[5,32,256]{2,1,0:T(8,128)S(1)}, u32[]{:S(2)}, u32[]{:S(2)}) collective-permute-start(f32[5,32,256]{2,1,0:T(8,128)S(1)} %get-tuple-element.30), channel_id=1, source_target_pairs={{0,1},{1,0},{2,3},{3,2},{4,5},{5,4},{6,7},{7,6},{8,9},{9,8},{10,11... | collective-permute-start | bytes 491528 | tf_op jit(solution)/shard_map/ppermute | solution.py:521
  5.9 11.6 %collective-permute-start.4 = (f32[5,16,128]{2,1,0:T(8,128)S(1)}, f32[5,16,128]{2,1,0:T(8,128)S(1)}, u32[]{:S(2)}, u32[]{:S(2)}) collective-permute-start(f32[5,16,128]{2,1,0:T(8,128)S(1)} %get-tuple-element.32), channel_id=1, source_target_pairs={{0,12},{2,6},{4,0},{6,10},{8,4},{10,14},{12,8},{14,2},{1,13},{3,7}... | collective-permute-start | bytes 122888 | tf_op jit(solution)/shard_map/ppermute | solution.py:521
  7.2 14.3 %collective-permute-start = (f32[5,16,256]{2,1,0:T(8,128)S(1)}, f32[5,16,256]{2,1,0:T(8,128)S(1)}, u32[]{:S(2)}, u32[]{:S(2)}) collective-permute-start(f32[5,16,256]{2,1,0:T(8,128)S(1)} %get-tuple-element.28), channel_id=1, source_target_pairs={{0,240},{16,32},{32,16},{48,64},{64,48},{80,96},{96,80},{112,128},... | collective-permute-start | bytes 245768 | tf_op jit(solution)/shard_map/ppermute | solution.py:521
  14.6 7.0 %collective-permute-start.1 = (f32[5,16,256]{2,1,0:T(8,128)S(1)}, f32[5,16,256]{2,1,0:T(8,128)S(1)}, u32[]{:S(2)}, u32[]{:S(2)}) collective-permute-start(f32[5,16,256]{2,1,0:T(8,128)S(1)} %get-tuple-element.29), channel_id=1, source_target_pairs={{0,16},{16,0},{32,48},{48,32},{1,17},{17,1},{33,49},{49,33},{2,18}... | collective-permute-start | bytes 245768 | tf_op jit(solution)/shard_map/ppermute | solution.py:521
  14.6 7.0 %collective-permute-start.3 = (f32[5,16,128]{2,1,0:T(8,128)S(1)}, f32[5,16,128]{2,1,0:T(8,128)S(1)}, u32[]{:S(2)}, u32[]{:S(2)}) collective-permute-start(f32[5,16,128]{2,1,0:T(8,128)S(1)} %get-tuple-element.31), channel_id=1, source_target_pairs={{0,2},{2,0},{1,3},{3,1},{4,6},{6,4},{5,7},{7,5},{8,10},{10,8},{9,1... | collective-permute-start | bytes 122888 | tf_op jit(solution)/shard_map/ppermute | solution.py:521
  17.5 4.0 %collective-permute-start.5 = (f32[5,16,128]{2,1,0:T(8,128)S(1)}, f32[5,16,128]{2,1,0:T(8,128)S(1)}, u32[]{:S(2)}, u32[]{:S(2)}) collective-permute-start(f32[5,16,128]{2,1,0:T(8,128)S(1)} %collective-permute-done.4), channel_id=1, source_target_pairs={{0,2},{2,0},{1,3},{3,1},{4,6},{6,4},{5,7},{7,5},{8,10},{10,8},{9,1... | collective-permute-start | bytes 122888 | tf_op jit(solution)/shard_map/ppermute | solution.py:521
  17.6 1.4 %copy-start.2 = (f32[64,3,1,4,512]{4,3,2,1,0:T(4,128)S(1)}, f32[64,3,1,4,512]{4,3,2,1,0:T(4,128)}, u32[]{:S(2)}) copy-start(f32[64,3,1,4,512]{4,3,2,1,0:T(4,128)} %basis.1) | copy-start | bytes 4718596
  19.0 1.0 %copy-start.3 = (f32[16,3,1,4,512]{4,3,2,1,0:T(4,128)S(1)}, f32[16,3,1,4,512]{4,3,2,1,0:T(4,128)}, u32[]{:S(2)}) copy-start(f32[16,3,1,4,512]{4,3,2,1,0:T(4,128)} %held.1) | copy-start | bytes 1179652
  26.5 7.7 %collective-permute-start.8 = (f32[5,40,256]{2,1,0:T(8,128)S(1)}, f32[5,40,256]{2,1,0:T(8,128)S(1)}, u32[]{:S(2)}, u32[]{:S(2)}) collective-permute-start(f32[5,40,256]{2,1,0:T(8,128)S(1)} %get-tuple-element.36), channel_id=1, source_target_pairs={{0,1},{1,0},{2,3},{3,2},{4,5},{5,4},{6,7},{7,6},{8,9},{9,8},{10,11... | collective-permute-start | bytes 614408 | tf_op jit(solution)/shard_map/ppermute | solution.py:521
  27.3 5.6 %collective-permute-start.10 = (f32[5,16,128]{2,1,0:T(8,128)S(1)}, f32[5,16,128]{2,1,0:T(8,128)S(1)}, u32[]{:S(2)}, u32[]{:S(2)}) collective-permute-start(f32[5,16,128]{2,1,0:T(8,128)S(1)} %get-tuple-element.38), channel_id=1, source_target_pairs={{0,12},{2,6},{4,0},{6,10},{8,4},{10,14},{12,8},{14,2},{1,13},{3,7}... | collective-permute-start | bytes 122888 | tf_op jit(solution)/shard_map/ppermute | solution.py:521
  27.3 11.6 %collective-permute-start.6 = (f32[5,16,256]{2,1,0:T(8,128)S(1)}, f32[5,16,256]{2,1,0:T(8,128)S(1)}, u32[]{:S(2)}, u32[]{:S(2)}) collective-permute-start(f32[5,16,256]{2,1,0:T(8,128)S(1)} %get-tuple-element.34), channel_id=1, source_target_pairs={{0,240},{16,32},{32,16},{48,64},{64,48},{80,96},{96,80},{112,128},... | collective-permute-start | bytes 245768 | tf_op jit(solution)/shard_map/ppermute | solution.py:521
  31.0 8.0 %collective-permute-start.7 = (f32[5,16,256]{2,1,0:T(8,128)S(1)}, f32[5,16,256]{2,1,0:T(8,128)S(1)}, u32[]{:S(2)}, u32[]{:S(2)}) collective-permute-start(f32[5,16,256]{2,1,0:T(8,128)S(1)} %get-tuple-element.35), channel_id=1, source_target_pairs={{0,16},{16,0},{32,48},{48,32},{1,17},{17,1},{33,49},{49,33},{2,18}... | collective-permute-start | bytes 245768 | tf_op jit(solution)/shard_map/ppermute | solution.py:521
  31.0 2.8 %collective-permute-start.9 = (f32[5,16,128]{2,1,0:T(8,128)S(1)}, f32[5,16,128]{2,1,0:T(8,128)S(1)}, u32[]{:S(2)}, u32[]{:S(2)}) collective-permute-start(f32[5,16,128]{2,1,0:T(8,128)S(1)} %get-tuple-element.37), channel_id=1, source_target_pairs={{0,2},{2,0},{1,3},{3,1},{4,6},{6,4},{5,7},{7,5},{8,10},{10,8},{9,1... | collective-permute-start | bytes 122888 | tf_op jit(solution)/shard_map/ppermute | solution.py:521
  33.0 1.2 %collective-permute-start.11 = (f32[5,16,128]{2,1,0:T(8,128)S(1)}, f32[5,16,128]{2,1,0:T(8,128)S(1)}, u32[]{:S(2)}, u32[]{:S(2)}) collective-permute-start(f32[5,16,128]{2,1,0:T(8,128)S(1)} %collective-permute-done.10), channel_id=1, source_target_pairs={{0,2},{2,0},{1,3},{3,1},{4,6},{6,4},{5,7},{7,5},{8,10},{10,8},{9,1... | collective-permute-start | bytes 122888 | tf_op jit(solution)/shard_map/ppermute | solution.py:521

commit v9 on v8

--- a/solution.py
+++ b/solution.py
@@ -248,7 +248,7 @@
 
 def first_kernel(
     diffusivity, folded, current, x_next_in, x_pair_in, y_halo, z_pair_in, z_next_in,
-    first, x_next, x_pair, y_row, z_pair, z_next, *edges,
+    first, x_pair, x_next, y_row, z_pair, z_next, *edges,
 ):
     count, cells = current.shape[:2]
     upper = lax.axis_index("zl") > 0
@@ -320,7 +320,7 @@
 
 
 def outer_kernel(
-    diffusivity, offsets, column_id, folded, start, current, x_next, x_pair, y_halo, z_pair,
+    diffusivity, offsets, column_id, folded, start, current, x_pair, x_next, y_halo, z_pair,
     z_next, picked_in, target_in, target, snapshot, chosen, y_low, y_high, z_before, z_after, picked, result,
     semaphores,
 ):
@@ -586,7 +586,8 @@
         + faces[3:],
         scratch_shapes=[wall, wall, edge, edge], compiler_params=params(24),
     )(diffusivity, folded, fields, *halos)
-    halos = exchange(packed)
+    x_pair, x_next, *packed = packed
+    halos = exchange((x_next, x_pair, *packed))
 
     x_next, x_pair, *halos = halos
     sides = [wall, wall, edge, edge]
@@ -611,7 +612,7 @@
         ],
         input_output_aliases={12: 0}, compiler_params=params(24),
     )(
-        diffusivity, subsample_offsets, column_id, folded, fields, first, x_next, x_pair,
+        diffusivity, subsample_offsets, column_id, folded, fields, first, x_pair, x_next,
         *halos, picked, fields_out,
     )
     relayed = lax.all_to_all(snapshot.reshape(8, 8, LANES), ("y", "core"), 0, 0, tiled=True)

time: 77 us -> 75.6 us (0.982)
  blocking collectives: 31.8 us -> 29.7 us
    all_to_all x2, blocking collectives: 21.9 us -> 20.4 us  [everyone(): lax.all_to_all(message.reshape(rows, 1, LANES), axes, 0, 0, tiled=True)]
  transfers between devices with their start and end apart: 12 -> 12, of which waited for: 2 -> 3; matrix products, arithmetic and copies ran while one was open for 0% -> 0% of each run, Pallas kernels for 8% -> 8%
where the time goes in v9:
time: 75.6 us; the launch traced here: 75.3 us
  blocking collectives  29.7 us (39%)
  starting transfers between devices  21.3 us (28%)
  Pallas kernels  18 us (24%)
  local copies, waits for them, and re-layouts  4.15 us (5%)
  between operations  1.42 us (2%)
    ppermute x12, starting transfers between devices, moved(): return lax.ppermute(value, axes, pairs)  21.3 us
    all_to_all x2, blocking collectives, everyone(): lax.all_to_all(message.reshape(rows, 1, LANES), axes, 0, 0, tiled=True)  20.4 us
    all_to_all x1, blocking collectives, on_device(): lax.all_to_all(snapshot.reshape(8, 8, LANES), ('y', 'core'), 0, 0, tiled=...  9.37 us
    pallas_call x1, Pallas kernels, on_device(): pl.pallas_call(first_kernel, in_specs=[SMEM] + [VMEM] * 7, out_specs=[VME...  4.91 us
    pallas_call x1, Pallas kernels, on_device(): pl.pallas_call(inner_kernel, in_specs=[SMEM] * 2 + [VMEM] * 5, out_specs=...  4.73 us
    unnamed x12, local copies, waits for them, and re-layouts  4.15 us
    pallas_call x1, Pallas kernels, on_device(): pl.pallas_call(functools.partial(final_kernel, float(devices * length)),...  3.88 us
    pallas_call x1, Pallas kernels, on_device(): pl.pallas_call(outer_kernel, in_specs=[SMEM] * 3 + [VMEM] * 9 + [ANY], ou...  1.55 us
  transfers between devices with their start and end apart: 12, of which 3 were waited for; matrix products, arithmetic and copies ran while one was open for 0% of the time, Pallas kernels for 8%

profile of v9, /device:TPU:1, one launch (start us, length us, event | category | flops | bytes accessed | tf_op | source)
XLA Modules:
  0.0 75.3 jit_solution(8761811916488117770)
XLA Ops:
  0.6 1.7 %copy-done = f32[5,32,16,256]{3,2,1,0:T(8,128)S(1)} copy-done((f32[5,32,16,256]{3,2,1,0:T(8,128)S(1)}, f32[5,32,16,256]{3,2,1,0:T(8,128)}, u32[]{:S(2)}) %copy-start) | copy-done | bytes 2621464
  2.4 1.0 %shard_map.94 = (f32[5,16,256]{2,1,0:T(8,128)S(1)}, f32[5,16,256]{2,1,0:T(8,128)S(1)}, f32[5,32,256]{2,1,0:T(8,128)S(1)}, f32[5,16,128]{2,1,0:T(8,128)S(1)}, f32[5,16,128]{2,1,0:T(8,128)S(1)}) custom-call(f32[5,32,16,256]{3,2,1,0:T(8,128)S(1)} %copy-done), custom_call_target="tpu_custom_call" | custom-call | tf_op jit(solution)/shard_map/pallas_call | solution.py:571
  3.4 0.0 copy-start.5
  3.4 2.6 %collective-permute-start.2 = (f32[5,32,256]{2,1,0:T(8,128)S(1)}, f32[5,32,256]{2,1,0:T(8,128)S(1)}, u32[]{:S(2)}, u32[]{:S(2)}) collective-permute-start(f32[5,32,256]{2,1,0:T(8,128)S(1)} %get-tuple-element.30), channel_id=1, source_target_pairs={{0,1},{1,0},{2,3},{3,2},{4,5},{5,4},{6,7},{7,6},{8,9},{9,8},{10,11... | collective-permute-start | bytes 491528 | tf_op jit(solution)/shard_map/ppermute | solution.py:521
  5.9 1.3 %collective-permute-start.4 = (f32[5,16,128]{2,1,0:T(8,128)S(1)}, f32[5,16,128]{2,1,0:T(8,128)S(1)}, u32[]{:S(2)}, u32[]{:S(2)}) collective-permute-start(f32[5,16,128]{2,1,0:T(8,128)S(1)} %get-tuple-element.32), channel_id=1, source_target_pairs={{0,12},{2,6},{4,0},{6,10},{8,4},{10,14},{12,8},{14,2},{1,13},{3,7}... | collective-permute-start | bytes 122888 | tf_op jit(solution)/shard_map/ppermute | solution.py:521
  7.2 7.3 %collective-permute-start = (f32[5,16,256]{2,1,0:T(8,128)S(1)}, f32[5,16,256]{2,1,0:T(8,128)S(1)}, u32[]{:S(2)}, u32[]{:S(2)}) collective-permute-start(f32[5,16,256]{2,1,0:T(8,128)S(1)} %get-tuple-element.28), channel_id=1, source_target_pairs={{0,240},{16,32},{32,16},{48,64},{64,48},{80,96},{96,80},{112,128},... | collective-permute-start | bytes 245768 | tf_op jit(solution)/shard_map/ppermute | solution.py:521
  14.6 0.0 collective-permute-start.1
  14.6 3.0 %collective-permute-start.3 = (f32[5,16,128]{2,1,0:T(8,128)S(1)}, f32[5,16,128]{2,1,0:T(8,128)S(1)}, u32[]{:S(2)}, u32[]{:S(2)}) collective-permute-start(f32[5,16,128]{2,1,0:T(8,128)S(1)} %get-tuple-element.31), channel_id=1, source_target_pairs={{0,2},{2,0},{1,3},{3,1},{4,6},{6,4},{5,7},{7,5},{8,10},{10,8},{9,1... | collective-permute-start | bytes 122888 | tf_op jit(solution)/shard_map/ppermute | solution.py:521
  17.5 0.0 collective-permute-done.4
  17.5 0.1 collective-permute-start.5
  17.6 1.4 %copy-done.2 = f32[64,3,1,4,512]{4,3,2,1,0:T(4,128)S(1)} copy-done((f32[64,3,1,4,512]{4,3,2,1,0:T(4,128)S(1)}, f32[64,3,1,4,512]{4,3,2,1,0:T(4,128)}, u32[]{:S(2)}) %copy-start.2) | copy-done | bytes 1572888
  19.0 1.0 %copy-done.3 = f32[16,3,1,4,512]{4,3,2,1,0:T(4,128)S(1)} copy-done((f32[16,3,1,4,512]{4,3,2,1,0:T(4,128)S(1)}, f32[16,3,1,4,512]{4,3,2,1,0:T(4,128)}, u32[]{:S(2)}) %copy-start.3) | copy-done | bytes 393240
  20.0 1.5 %shard_map.93 = (f32[80,6144]{1,0:T(8,128)S(1)}, f32[48,128]{1,0:T(8,128)S(1)}) custom-call(f32[64,3,1,4,512]{4,3,2,1,0:T(4,128)S(1)} %copy-done.2, f32[16,3,1,4,512]{4,3,2,1,0:T(4,128)S(1)} %copy-done.3), custom_call_target="tpu_custom_call" | custom-call | tf_op jit(solution)/shard_map/pallas_call | solution.py:577
  21.5 0.0 collective-permute-done.5.z_next_in
  21.5 0.0 collective-permute-done.x_next_in
  21.6 0.0 collective-permute-done.2.y_halo
  21.6 4.9 %shard_map.95 = (f32[5,32,16,256]{3,2,1,0:T(8,128)S(1)}, f32[5,16,256]{2,1,0:T(8,128)S(1)}, f32[5,16,256]{2,1,0:T(8,128)S(1)}, f32[5,40,256]{2,1,0:T(8,128)S(1)}...) custom-call(f32[5]{0:T(128)S(1)} %copy-done.4, f32[48,128]{1,0:T(8,128)S(1)} %get-tuple-element.27.folded, ...), custom_call_target="tpu_custom_call" | custom-call | tf_op jit(solution)/shard_map/pallas_call | solution.py:583
  26.5 0.8 %collective-permute-start.8 = (f32[5,40,256]{2,1,0:T(8,128)S(1)}, f32[5,40,256]{2,1,0:T(8,128)S(1)}, u32[]{:S(2)}, u32[]{:S(2)}) collective-permute-start(f32[5,40,256]{2,1,0:T(8,128)S(1)} %get-tuple-element.36), channel_id=1, source_target_pairs={{0,1},{1,0},{2,3},{3,2},{4,5},{5,4},{6,7},{7,6},{8,9},{9,8},{10,11... | collective-permute-start | bytes 614408 | tf_op jit(solution)/shard_map/ppermute | solution.py:521
  27.3 1.7 %collective-permute-start.6 = (f32[5,16,256]{2,1,0:T(8,128)S(1)}, f32[5,16,256]{2,1,0:T(8,128)S(1)}, u32[]{:S(2)}, u32[]{:S(2)}) collective-permute-start(f32[5,16,256]{2,1,0:T(8,128)S(1)} %get-tuple-element.34), channel_id=1, source_target_pairs={{0,16},{16,0},{32,48},{48,32},{1,17},{17,1},{33,49},{49,33},{2,18}... | collective-permute-start | bytes 245768 | tf_op jit(solution)/shard_map/ppermute | solution.py:521
  29.0 2.0 %collective-permute-start.7 = (f32[5,16,256]{2,1,0:T(8,128)S(1)}, f32[5,16,256]{2,1,0:T(8,128)S(1)}, u32[]{:S(2)}, u32[]{:S(2)}) collective-permute-start(f32[5,16,256]{2,1,0:T(8,128)S(1)} %get-tuple-element.35), channel_id=1, source_target_pairs={{0,240},{16,32},{32,16},{48,64},{64,48},{80,96},{96,80},{112,128},... | collective-permute-start | bytes 245768 | tf_op jit(solution)/shard_map/ppermute | solution.py:521
  31.0 2.6 %collective-permute-start.9 = (f32[5,16,128]{2,1,0:T(8,128)S(1)}, f32[5,16,128]{2,1,0:T(8,128)S(1)}, u32[]{:S(2)}, u32[]{:S(2)}) collective-permute-start(f32[5,16,128]{2,1,0:T(8,128)S(1)} %get-tuple-element.37), channel_id=1, source_target_pairs={{0,2},{2,0},{1,3},{3,1},{4,6},{6,4},{5,7},{7,5},{8,10},{10,8},{9,1... | collective-permute-start | bytes 122888 | tf_op jit(solution)/shard_map/ppermute | solution.py:521
  33.6 0.0 collective-permute-start.11
  34.2 0.2 collective-permute-done.9.z_pair
  34.4 0.4 collective-permute-done.11.z_next
  34.8 0.1 collective-permute-done.8.y_halo
  34.9 4.7 %shard_map.96 = (f32[5,32,16,256]{3,2,1,0:T(8,128)}, f32[128,256]{1,0:T(8,128)S(1)}) custom-call(f32[5]{0:T(128)S(1)} %copy-done.4, s32[3]{0:T(128)S(1)} %copy-done.5, f32[5,32,16,256]{3,2,1,0:T(8,128)S(1)} %copy-done.1, f32[5,32,16,256]{3,2,1,0:T(8,128)S(1)} %get-tuple-element.33.current, f32[5,40,256]{2,1,0:T(8,128)S(1)} %collective-permute-done.8.y_halo, ...), custom_call_target="tpu_custom_call" | custom-call | flops 20000000 | bytes 20000000 | tf_op jit(solution)/shard_map/pallas_call | solution.py:594
  39.6 1.6 %shard_map.97 = (f32[5,32,16,256]{3,2,1,0:T(8,128)}, f32[64,128]{1,0:T(8,128)S(1)}, s32[8,128]{1,0:T(8,128)S(1)}) custom-call(f32[5]{0:T(128)S(1)} %copy-done.4, s32[3]{0:T(128)S(1)} %copy-done.5, s32[1]{0:T(128)S(6)} %copy.14.column_id, f32[48,128]{1,0:T(8,128)S(1)} %get-tuple-element.27.folded, ...), custom_call_target="tpu_custom_call", output_to_operand_aliasing={{0}: (12, {})} | custom-call | tf_op jit(solution)/shard_map/pallas_call | solution.py:602
  41.2 9.4 %all_to_all.15.relayed = f32[8,8,128]{2,1,0:T(8,128)S(1)} all-to-all(f32[8,8,128]{2,1,0:T(8,128)S(1)} %bitcast.14), channel_id=1, replica_groups=mesh['zh'=4,'x'=4,'y'=4,'core'=2,'zl'=2] {'y','core'}, dimensions={0} | all-to-all | bytes 65536 | tf_op jit(solution)/shard_map/all_to_all | solution.py:618
  50.5 0.4 shard_map.98
  51.0 10.8 %all_to_all.16 = f32[96,1,128]{2,1,0:T(1,128)S(1)} all-to-all(f32[96,1,128]{2,1,0:T(1,128)S(1)} %bitcast.13), channel_id=1, replica_groups=mesh['zh'=4,'x'=4,'y'=4,'core'=2,'zl'=2] {'x','y','core'}, dimensions={0} | all-to-all | bytes 98304 | tf_op jit(solution)/shard_map/all_to_all | solution.py:546
  61.8 9.6 %all_to_all.17 = f32[136,1,128]{2,1,0:T(1,128)S(1)} all-to-all(f32[136,1,128]{2,1,0:T(1,128)S(1)} %bitcast.11), channel_id=1, replica_groups=mesh['zh'=4,'x'=4,'y'=4,'core'=2,'zl'=2] {'zh','zl'}, dimensions={0} | all-to-all | bytes 139264 | tf_op jit(solution)/shard_map/all_to_all | solution.py:546
  71.4 3.9 %shard_map.100 = (f32[16,64]{1,0:T(8,128)}, f32[16,16]{1,0:T(8,128)}, f32[16,3,1,4,512]{4,3,2,1,0:T(4,128)}) custom-call(s32[8,128]{1,0:T(8,128)S(1)} %get-tuple-element.42.chosen_column, f32[136,128]{1,0:T(8,128)S(1)} %bitcast.10, f32[80,6144]{1,0:T(8,128)S(1)} %get-tuple-element.44.joined, f32[8,6144]{1,0:T(8,128)S(1)} %get-tuple-element.46.column), custom_call_target="tpu_custom_call" | custom-call | tf_op jit(solution)/shard_map/pallas_call | solution.py:633
  (15 shorter events, 0.1 us)
Async XLA Ops:
  0.6 1.7 %copy-start = (f32[5,32,16,256]{3,2,1,0:T(8,128)S(1)}, f32[5,32,16,256]{3,2,1,0:T(8,128)}, u32[]{:S(2)}) copy-start(f32[5,32,16,256]{3,2,1,0:T(8,128)} %start.3) | copy-start | bytes 7864324
  2.4 19.2 %copy-start.1 = (f32[5,32,16,256]{3,2,1,0:T(8,128)S(1)}, f32[5,32,16,256]{3,2,1,0:T(8,128)}, u32[]{:S(2)}) copy-start(f32[5,32,16,256]{3,2,1,0:T(8,128)} %start.3) | copy-start | bytes 7864324
  2.4 19.2 %copy-start.4 = (f32[5]{0:T(128)S(1)}, f32[5]{0:T(128)}, u32[]{:S(2)}) copy-start(f32[5]{0:T(128)} %diffusivity.5) | copy-start | bytes 64
  3.4 31.5 %copy-start.5 = (s32[3]{0:T(128)S(1)}, s32[3]{0:T(128)}, u32[]{:S(2)}) copy-start(s32[3]{0:T(128)} %offsets.3) | copy-start | bytes 40
  3.4 18.2 %collective-permute-start.2 = (f32[5,32,256]{2,1,0:T(8,128)S(1)}, f32[5,32,256]{2,1,0:T(8,128)S(1)}, u32[]{:S(2)}, u32[]{:S(2)}) collective-permute-start(f32[5,32,256]{2,1,0:T(8,128)S(1)} %get-tuple-element.30), channel_id=1, source_target_pairs={{0,1},{1,0},{2,3},{3,2},{4,5},{5,4},{6,7},{7,6},{8,9},{9,8},{10,11... | collective-permute-start | bytes 491528 | tf_op jit(solution)/shard_map/ppermute | solution.py:521
  5.9 11.6 %collective-permute-start.4 = (f32[5,16,128]{2,1,0:T(8,128)S(1)}, f32[5,16,128]{2,1,0:T(8,128)S(1)}, u32[]{:S(2)}, u32[]{:S(2)}) collective-permute-start(f32[5,16,128]{2,1,0:T(8,128)S(1)} %get-tuple-element.32), channel_id=1, source_target_pairs={{0,12},{2,6},{4,0},{6,10},{8,4},{10,14},{12,8},{14,2},{1,13},{3,7}... | collective-permute-start | bytes 122888 | tf_op jit(solution)/shard_map/ppermute | solution.py:521
  7.2 14.3 %collective-permute-start = (f32[5,16,256]{2,1,0:T(8,128)S(1)}, f32[5,16,256]{2,1,0:T(8,128)S(1)}, u32[]{:S(2)}, u32[]{:S(2)}) collective-permute-start(f32[5,16,256]{2,1,0:T(8,128)S(1)} %get-tuple-element.28), channel_id=1, source_target_pairs={{0,240},{16,32},{32,16},{48,64},{64,48},{80,96},{96,80},{112,128},... | collective-permute-start | bytes 245768 | tf_op jit(solution)/shard_map/ppermute | solution.py:521
  14.6 7.0 %collective-permute-start.1 = (f32[5,16,256]{2,1,0:T(8,128)S(1)}, f32[5,16,256]{2,1,0:T(8,128)S(1)}, u32[]{:S(2)}, u32[]{:S(2)}) collective-permute-start(f32[5,16,256]{2,1,0:T(8,128)S(1)} %get-tuple-element.29), channel_id=1, source_target_pairs={{0,16},{16,0},{32,48},{48,32},{1,17},{17,1},{33,49},{49,33},{2,18}... | collective-permute-start | bytes 245768 | tf_op jit(solution)/shard_map/ppermute | solution.py:521
  14.6 7.0 %collective-permute-start.3 = (f32[5,16,128]{2,1,0:T(8,128)S(1)}, f32[5,16,128]{2,1,0:T(8,128)S(1)}, u32[]{:S(2)}, u32[]{:S(2)}) collective-permute-start(f32[5,16,128]{2,1,0:T(8,128)S(1)} %get-tuple-element.31), channel_id=1, source_target_pairs={{0,2},{2,0},{1,3},{3,1},{4,6},{6,4},{5,7},{7,5},{8,10},{10,8},{9,1... | collective-permute-start | bytes 122888 | tf_op jit(solution)/shard_map/ppermute | solution.py:521
  17.5 4.0 %collective-permute-start.5 = (f32[5,16,128]{2,1,0:T(8,128)S(1)}, f32[5,16,128]{2,1,0:T(8,128)S(1)}, u32[]{:S(2)}, u32[]{:S(2)}) collective-permute-start(f32[5,16,128]{2,1,0:T(8,128)S(1)} %collective-permute-done.4), channel_id=1, source_target_pairs={{0,2},{2,0},{1,3},{3,1},{4,6},{6,4},{5,7},{7,5},{8,10},{10,8},{9,1... | collective-permute-start | bytes 122888 | tf_op jit(solution)/shard_map/ppermute | solution.py:521
  17.6 1.4 %copy-start.2 = (f32[64,3,1,4,512]{4,3,2,1,0:T(4,128)S(1)}, f32[64,3,1,4,512]{4,3,2,1,0:T(4,128)}, u32[]{:S(2)}) copy-start(f32[64,3,1,4,512]{4,3,2,1,0:T(4,128)} %basis.1) | copy-start | bytes 4718596
  19.0 1.0 %copy-start.3 = (f32[16,3,1,4,512]{4,3,2,1,0:T(4,128)S(1)}, f32[16,3,1,4,512]{4,3,2,1,0:T(4,128)}, u32[]{:S(2)}) copy-start(f32[16,3,1,4,512]{4,3,2,1,0:T(4,128)} %held.1) | copy-start | bytes 1179652
  26.5 8.3 %collective-permute-start.8 = (f32[5,40,256]{2,1,0:T(8,128)S(1)}, f32[5,40,256]{2,1,0:T(8,128)S(1)}, u32[]{:S(2)}, u32[]{:S(2)}) collective-permute-start(f32[5,40,256]{2,1,0:T(8,128)S(1)} %get-tuple-element.36), channel_id=1, source_target_pairs={{0,1},{1,0},{2,3},{3,2},{4,5},{5,4},{6,7},{7,6},{8,9},{9,8},{10,11... | collective-permute-start | bytes 614408 | tf_op jit(solution)/shard_map/ppermute | solution.py:521
  27.3 6.2 %collective-permute-start.10 = (f32[5,16,128]{2,1,0:T(8,128)S(1)}, f32[5,16,128]{2,1,0:T(8,128)S(1)}, u32[]{:S(2)}, u32[]{:S(2)}) collective-permute-start(f32[5,16,128]{2,1,0:T(8,128)S(1)} %get-tuple-element.38), channel_id=1, source_target_pairs={{0,12},{2,6},{4,0},{6,10},{8,4},{10,14},{12,8},{14,2},{1,13},{3,7}... | collective-permute-start | bytes 122888 | tf_op jit(solution)/shard_map/ppermute | solution.py:521
  27.3 12.3 %collective-permute-start.6 = (f32[5,16,256]{2,1,0:T(8,128)S(1)}, f32[5,16,256]{2,1,0:T(8,128)S(1)}, u32[]{:S(2)}, u32[]{:S(2)}) collective-permute-start(f32[5,16,256]{2,1,0:T(8,128)S(1)} %get-tuple-element.34), channel_id=1, source_target_pairs={{0,16},{16,0},{32,48},{48,32},{1,17},{17,1},{33,49},{49,33},{2,18}... | collective-permute-start | bytes 245768 | tf_op jit(solution)/shard_map/ppermute | solution.py:521
  29.0 10.6 %collective-permute-start.7 = (f32[5,16,256]{2,1,0:T(8,128)S(1)}, f32[5,16,256]{2,1,0:T(8,128)S(1)}, u32[]{:S(2)}, u32[]{:S(2)}) collective-permute-start(f32[5,16,256]{2,1,0:T(8,128)S(1)} %get-tuple-element.35), channel_id=1, source_target_pairs={{0,240},{16,32},{32,16},{48,64},{64,48},{80,96},{96,80},{112,128},... | collective-permute-start | bytes 245768 | tf_op jit(solution)/shard_map/ppermute | solution.py:521
  31.0 3.5 %collective-permute-start.9 = (f32[5,16,128]{2,1,0:T(8,128)S(1)}, f32[5,16,128]{2,1,0:T(8,128)S(1)}, u32[]{:S(2)}, u32[]{:S(2)}) collective-permute-start(f32[5,16,128]{2,1,0:T(8,128)S(1)} %get-tuple-element.37), channel_id=1, source_target_pairs={{0,2},{2,0},{1,3},{3,1},{4,6},{6,4},{5,7},{7,5},{8,10},{10,8},{9,1... | collective-permute-start | bytes 122888 | tf_op jit(solution)/shard_map/ppermute | solution.py:521
  33.6 1.2 %collective-permute-start.11 = (f32[5,16,128]{2,1,0:T(8,128)S(1)}, f32[5,16,128]{2,1,0:T(8,128)S(1)}, u32[]{:S(2)}, u32[]{:S(2)}) collective-permute-start(f32[5,16,128]{2,1,0:T(8,128)S(1)} %collective-permute-done.10), channel_id=1, source_target_pairs={{0,2},{2,0},{1,3},{3,1},{4,6},{6,4},{5,7},{7,5},{8,10},{10,8},{9,1... | collective-permute-start | bytes 122888 | tf_op jit(solution)/shard_map/ppermute | solution.py:521
